TPU v7x, 512 devices: a whole 4x8x8 slice. The times are simulated.
512 devices in a mesh: seq: 64 (over x, y, z_hi), head: 8 (over z_lo, core).
Axes of the slice: x: 4, y: 8, z: 8 (z_hi: 2, z_lo: 4; z = z_hi * 4 + z_lo), core: 2. Of those that a mesh axis runs over, the one named last changes fastest.
Arguments:
- query: bfloat16 [8192, 64, 512], P('seq', 'head'), may hold values from -100 to 100
- latent: bfloat16 [8192, 512], P('seq'), may hold values from -6 to 6
- segment_ids: int32 [8192], replicated, may hold values from 0 to 31, never falling along the last dimension, each value on 1 to 3072 neighbouring positions
- block_of_slot: int32 [128], replicated, may hold values from 0 to 127, each once
- value_up: bfloat16 [64, 448, 128], P('head'), may hold values from -0.25 to 0.25
- out_proj: bfloat16 [8192, 3584], P('head', 'seq'), may hold values from -0.0625 to 0.0625
Outputs:
- mixed: bfloat16 [8192, 3584], P(('seq', 'head'))
Inputs may be any that keep to these rules, and one draw needn't show every extreme that they name: segment_ids never falls along positions; every document has 1 to 3072 positions and one has exactly 3072. block_of_slot holds every position block once.
All inputs are finite; a program needn't handle non-finite values.
Results may differ from a plain program's by a relative error of at most 0.022.
Values may be sent and summed in bfloat16 or wider, within the bound.
No kernel may reach another device: no remote copies, remote signals or barrier semaphores. Data moves between devices by JAX's collectives and lax.ppermute only.
A program may use at most 64 MiB of HBM per device.

v0:
```python
import jax
import jax.numpy as jnp
from jax import lax
from jax.sharding import PartitionSpec as P

score_scale = 192 ** (-0.5)
negative = -1e30


def per_device(query, latent, segment_ids, block_of_slot, value_up, out_proj):
    tok_rows = query.shape[0]
    head_count = query.shape[1]
    latent_width = value_up.shape[1]
    block_rows = tok_rows // 2
    seq_index = lax.axis_index("seq")
    my_blocks = lax.dynamic_slice_in_dim(block_of_slot, 2 * seq_index, 2, 0)
    offsets = jnp.arange(block_rows, dtype=jnp.int32)
    query_pos = (my_blocks[:, None] * block_rows + offsets[None, :]).reshape(tok_rows)
    query_seg = segment_ids[query_pos]
    first_seg = segment_ids[my_blocks * block_rows]

    def attend(carry, block_keys, key_block):
        key_start = key_block * block_rows
        key_seg = lax.dynamic_slice_in_dim(segment_ids, key_start, block_rows, 0)
        needed = jnp.any((key_block <= my_blocks) & (key_seg[block_rows - 1] >= first_seg))

        def update(current):
            maximum, total, summed = current
            key_pos = key_start + offsets
            allowed = (key_pos[None, :] <= query_pos[:, None]) & (
                key_seg[None, :] == query_seg[:, None]
            )
            scores = (
                jnp.einsum("qhc,kc->hqk", query, block_keys, preferred_element_type=jnp.float32)
                * score_scale
            )
            masked = jnp.where(allowed[None], scores, negative)
            new_max = jnp.maximum(maximum, jnp.max(masked, axis=-1))
            weights = jnp.where(allowed[None], jnp.exp(masked - new_max[..., None]), 0.0)
            factor = jnp.exp(maximum - new_max)
            total = total * factor + jnp.sum(weights, axis=-1)
            added = jnp.einsum(
                "hqk,kc->hqc",
                weights.astype(jnp.bfloat16),
                block_keys[:, :latent_width],
                preferred_element_type=jnp.float32,
            )
            return (new_max, total, summed * factor[..., None] + added)

        return lax.cond(needed, update, lambda current: current, carry)

    initial = (
        jnp.full((head_count, tok_rows), negative, jnp.float32),
        jnp.zeros((head_count, tok_rows), jnp.float32),
        jnp.zeros((head_count, tok_rows, latent_width), jnp.float32),
    )
    piece = lax.all_gather(latent, "seq", axis=0, tiled=True)
    block_count = piece.shape[0] // block_rows

    def one_block(number, current):
        block_keys = lax.dynamic_slice_in_dim(piece, number * block_rows, block_rows, 0)
        key_block = lax.dynamic_slice_in_dim(block_of_slot, number, 1, 0)[0]
        return attend(current, block_keys, key_block)

    carry = lax.fori_loop(0, block_count, one_block, initial)
    maximum, total, summed = carry
    latent_out = (summed / total[..., None]).astype(jnp.bfloat16)
    head_values = jnp.einsum(
        "hqc,hcv->qhv", latent_out, value_up, preferred_element_type=jnp.float32
    )
    head_values = head_values.astype(jnp.bfloat16).reshape(tok_rows, -1)
    partial_value = jnp.dot(
        head_values,
        lax.all_gather(out_proj, "seq", axis=1, tiled=True),
        preferred_element_type=jnp.float32,
    )
    rounded = lax.optimization_barrier(partial_value.astype(jnp.bfloat16)).astype(jnp.float32)
    return lax.psum_scatter(rounded.astype(jnp.bfloat16), "head", scatter_dimension=0, tiled=True)


def solution(mesh):
    return jax.shard_map(
        per_device,
        mesh=mesh,
        in_specs=(
            P("seq", "head", None),
            P("seq", None),
            P(),
            P(),
            P("head", None, None),
            P("head", "seq"),
        ),
        out_specs=P(("seq", "head"), None),
        check_vma=False,
    )
```

profile of v0, /device:TPU:1, one launch (start us, length us, event | category | flops | bytes accessed | tf_op | source)
XLA Modules:
  0.0 1125.1 jit_solution(13802711830781828655)
XLA Ops:
  13.4 201.9 %all-gather.3.cloned.1.call-done = bf16[8192,512]{1,0:T(8,128)(2,1)} async-done(((bf16[128,512]{1,0:T(8,128)(2,1)}), bf16[8192,512]{1,0:T(8,128)(2,1)}) %all-gather.3.cloned.1.call-update) | async-done | bytes 8388624 | tf_op jit(solution)/shard_map/all_gather | solution.py:57
  215.4 654.8 %while.18 = (s32[]{:T(128)}, f32[8,128]{1,0:T(8,128)S(1)}, f32[8,128]{1,0:T(8,128)S(1)}, f32[8,128,448]{1,2,0:T(8,128)S(1)}, s32[128]{0:T(128)S(1)}, /*index=5*/...) while((s32[]{:T(128)}, f32[8,128]{1,0:T(8,128)S(1)}, ...), condition=%wide.region_6.7_spmd.clone, body=%wide.region_0.6_spmd.clone.sunk | while | flops 127363280 | bytes 5740243 | solution.py:65
  220.4 3.8 conditional.3
  229.2 3.8 conditional.3
  275.5 1.8 and_reduce_fusion.2
  280.5 1.8 and_reduce_fusion.2
  285.5 1.8 and_reduce_fusion.2
  290.5 1.8 and_reduce_fusion.2
  325.5 1.8 and_reduce_fusion.2
  330.5 1.8 and_reduce_fusion.2
  335.5 1.8 and_reduce_fusion.2
  370.4 1.8 and_reduce_fusion.2
  375.4 1.8 and_reduce_fusion.2
  380.4 1.8 and_reduce_fusion.2
  390.4 1.8 and_reduce_fusion.2
  395.4 1.8 and_reduce_fusion.2
  397.9 3.8 conditional.3
  404.2 1.8 and_reduce_fusion.2
  409.2 1.8 and_reduce_fusion.2
  414.2 1.8 and_reduce_fusion.2
  419.2 1.8 and_reduce_fusion.2
  466.6 3.8 conditional.3
  870.8 6.6 convolution_convert_fusion
  877.4 241.1 %reduce-scatter.2.cloned.1.call-done = bf16[16,3584]{1,0:T(8,128)(2,1)} async-done(((bf16[128,3584]{1,0:T(8,128)(2,1)}), bf16[16,3584]{1,0:T(8,128)(2,1)}) %reduce-scatter.2.cloned.1.call-update) | async-done | bytes 114704 | tf_op jit(solution)/shard_map/reduce_scatter | solution.py:78
  (943 shorter events, 477.7 us)
Async XLA Ops:
  6.5 863.7 %copy-start = (bf16[8,448,128]{2,1,0:T(8,128)(2,1)S(1)}, bf16[8,448,128]{2,1,0:T(8,128)(2,1)}, u32[]{:S(2)}) copy-start(bf16[8,448,128]{2,1,0:T(8,128)(2,1)} %param.14) | copy-start | bytes 2752516
  6.5 5.5 copy-start.1
  6.5 208.7 %all-gather.3.cloned.1.call-start = ((), (), s32[]{:S(2)}) async-start(), calls=%async_computation.1 | async-start | bytes 8519680 | tf_op jit(solution)/shard_map/all_gather | solution.py:57
  7.3 863.5 %all-gather.5.cloned.1.call-start = ((), (), s32[]{:S(2)}) async-start(), calls=%async_computation.2 | async-start | bytes 7454720 | tf_op jit(solution)/shard_map/all_gather | solution.py:74
  8.0 1110.6 %reduce-scatter.2.cloned.1.call-start = ((), (), s32[]{:S(2)}) async-start(), calls=%async_computation.3 | async-start | bytes 1032192 | tf_op jit(solution)/shard_map/reduce_scatter | solution.py:78
  12.1 203.3 %copy-start.2 = (s32[128]{0:T(128)S(1)}, s32[128]{0:T(128)}, u32[]{:S(2)}) copy-start(s32[128]{0:T(128)} %param.13) | copy-start | bytes 1540
Sparse Core Ops, SparseCore 0:
  11.9 203.3 all-gather.2
  219.6 184.0 all-gather.4
  877.5 240.9 reduce-scatter.1
where the time goes:
time: 1140 us; the launch traced here: 1130 us
  waiting for transfers between devices  445 us (39%)
  local copies, waits for them, and re-layouts  256 us (22%)
  other arithmetic  233 us (20%)
  loops' own time  157 us (14%)
  matrix products  20.8 us (2%)
  between operations  13.2 us (1%)
    reduce_scatter x1, waiting for transfers between devices, per_device(): lax.psum_scatter(rounded.astype(jnp.bfloat16), 'head', scatter_dimension=...  241 us
    reduce_or x128, other arithmetic, attend(): jnp.any((key_block <= my_blocks) & (key_seg[block_rows - 1] >= first_seg))  232 us
    all_gather x1, waiting for transfers between devices, per_device(): piece = lax.all_gather(latent, 'seq', axis=0, tiled=True)  202 us
    another operation x1, loops' own time, per_device(): carry = lax.fori_loop(0, block_count, one_block, initial)  155 us
    dynamic_slice x128, local copies, waits for them, and re-layouts, attend(): key_seg = lax.dynamic_slice_in_dim(segment_ids, key_start, block_rows, 0)  97.8 us
    slice x128, local copies, waits for them, and re-layouts, attend(): key_seg[block_rows - 1] >= first_seg  81.5 us
    dynamic_slice x128, local copies, waits for them, and re-layouts, one_block(): key_block = lax.dynamic_slice_in_dim(block_of_slot, number, 1, 0)[0]  71.2 us
  transfers between devices with their start and end apart: 3, of which 2 were waited for; matrix products, arithmetic and copies ran while one was open for 45% of the time, Pallas kernels for 0%

commit v1 on v0

v1 whole, which is shorter than its diff:
```python
import functools
import math

import jax
import jax.numpy as jnp
from jax import lax
from jax.experimental import pallas as pl
from jax.experimental.pallas import tpu as pltpu
from jax.sharding import Mesh
from jax.sharding import PartitionSpec as P

BLK = 64
CHUNK = 8
KEYS = BLK * CHUNK
PART = 16
exp2_scale = 192 ** (-0.5) * math.log2(math.e)
floor_max = -1e30
masked_score = -2e30


def attention_kernel(n_pieces, part_stride, scal, lo_ref, q_ref, vup_ref, *rest):
    pieces = rest[:n_pieces]
    out_ref, lat, kbuf, acc, done, sems = rest[n_pieces:]
    heads, toks, width = q_ref.shape
    rows = heads * BLK
    copies = []
    at = 0
    for i, piece in enumerate(pieces):
        n = piece.shape[0]
        copies.append(pltpu.make_async_copy(piece, lat.at[pl.ds(at, n)], sems.at[i]))
        at += n
    for c in copies:
        c.start()
    for c in copies:
        c.wait()
    last_block = scal.shape[0] - 5

    for b in range(toks // BLK):
        block = scal[b]
        first = scal[2 + b]
        q = q_ref[:, b * BLK : (b + 1) * BLK, :].reshape(rows, width)
        lo = lo_ref[:, b * BLK : (b + 1) * BLK, :].reshape(rows, 1)
        pos = block * BLK + lax.broadcasted_iota(jnp.int32, (heads, BLK, 1), 1).reshape(rows, 1)
        acc[...] = jnp.zeros_like(acc)

        def step(i, carry):
            m, total = carry
            base = first + i * CHUNK
            for j in range(CHUNK):
                src = scal[4 + jnp.minimum(base + j, last_block)]
                for part in range(BLK // PART):
                    row = pl.multiple_of(src * PART + part * part_stride, PART)
                    at = j * BLK + part * PART
                    kbuf[at : at + PART, :] = lat[pl.ds(row, PART), :]
            keys = kbuf[...]
            s = lax.dot_general(q, keys, (((1,), (1,)), ((), ())), preferred_element_type=jnp.float32)
            kp = base * BLK + lax.broadcasted_iota(jnp.int32, (1, KEYS), 1)
            allowed = (kp <= pos) & (kp >= lo)
            s = jnp.where(allowed, s * exp2_scale, masked_score)
            new = jnp.maximum(m, jnp.max(s, axis=1, keepdims=True))
            w = jnp.exp2(s - new)
            factor = jnp.exp2(m - new)
            total = total * factor + jnp.sum(w, axis=1, keepdims=True)
            acc[...] = acc[...] * factor + jnp.dot(
                w.astype(jnp.bfloat16), keys, preferred_element_type=jnp.float32
            )
            return new, total

        count = (block - first + CHUNK) // CHUNK
        init = (jnp.full((rows, 1), floor_max, jnp.float32), jnp.zeros((rows, 1), jnp.float32))
        _, total = lax.fori_loop(0, count, step, init)
        latent_out = (acc[...] / total).astype(jnp.bfloat16)
        done[:, b * BLK : (b + 1) * BLK, :] = latent_out.reshape(heads, BLK, width)

    vh = vup_ref.shape[2]
    for h in range(heads):
        out_ref[:, h * vh : (h + 1) * vh] = jnp.dot(
            done[h], vup_ref[h], preferred_element_type=jnp.float32
        ).astype(jnp.bfloat16)


def attention(scal, lo, q, vup, pieces, part_stride):
    heads, toks, width = q.shape
    vh = vup.shape[2]
    total_rows = sum(p.shape[0] for p in pieces)
    vmem = pl.BlockSpec(memory_space=pltpu.VMEM)
    return pl.pallas_call(
        functools.partial(attention_kernel, len(pieces), part_stride),
        out_shape=jax.ShapeDtypeStruct((toks, heads * vh), jnp.bfloat16),
        in_specs=[pl.BlockSpec(memory_space=pltpu.SMEM), vmem, vmem, vmem]
        + [pl.BlockSpec(memory_space=pl.ANY)] * len(pieces),
        out_specs=vmem,
        scratch_shapes=[
            pltpu.VMEM((total_rows, width), jnp.bfloat16),
            pltpu.VMEM((KEYS, width), jnp.bfloat16),
            pltpu.VMEM((heads * BLK, width), jnp.float32),
            pltpu.VMEM((heads, toks, width), jnp.bfloat16),
            pltpu.SemaphoreType.DMA((len(pieces),)),
        ],
        compiler_params=pltpu.CompilerParams(vmem_limit_bytes=40 * 2**20),
        name="latent_attention",
    )(scal, lo, q, vup, *pieces)


def prepare(query, segment_ids, block_of_slot, value_up, seq_index):
    toks, heads, _ = query.shape
    my_blocks = lax.dynamic_slice_in_dim(block_of_slot, 2 * seq_index, 2, 0)
    segs = jnp.concatenate(
        [lax.dynamic_slice_in_dim(segment_ids, my_blocks[i] * BLK, BLK, 0) for i in range(2)]
    )
    lo = jnp.sum((segment_ids[None, :] < segs[:, None]).astype(jnp.int32), axis=1)
    first = lo.reshape(2, BLK)[:, 0] // BLK
    n = block_of_slot.shape[0]
    slots = jnp.arange(n, dtype=jnp.int32)
    slot_of_block = jnp.sum(
        jnp.where(block_of_slot[None, :] == slots[:, None], slots[None, :], 0), axis=1
    )
    lo_rows = jnp.broadcast_to(lo[None, :, None], (heads, toks, 1))
    q = query.transpose(1, 0, 2)
    vup = jnp.pad(value_up, ((0, 0), (0, query.shape[2] - value_up.shape[1]), (0, 0)))
    return my_blocks, first, slot_of_block, lo_rows, q, vup


def per_device(query, latent, segment_ids, block_of_slot, value_up, out_proj):
    nx, ny, nzh = (lax.axis_size(a) for a in ("x", "y", "zh"))
    nzl, nc = lax.axis_size("zl"), lax.axis_size("core")
    plane = nx * ny
    x, y, zh = (lax.axis_index(a) for a in ("x", "y", "zh"))
    zl, core = lax.axis_index("zl"), lax.axis_index("core")
    seq_index = (x * ny + y) * nzh + zh

    part = lax.dynamic_slice_in_dim(latent, (zl * nc + core) * PART, PART, 0)
    spread = jnp.broadcast_to(part[None], (plane,) + part.shape)
    plane_rows = lax.all_to_all(spread, ("x", "y"), 0, 0, tiled=True)
    plane_rows = plane_rows.reshape(plane * PART, latent.shape[1])
    gathered = lax.all_gather(plane_rows, ("zh", "zl", "core"), axis=0, tiled=True)

    cols = out_proj.T
    other = lax.ppermute(cols, "zh", [(i, nzh - 1 - i) for i in range(nzh)])
    pair = jnp.where(zh == 0, jnp.stack([cols, other]), jnp.stack([other, cols]))
    columns = lax.all_gather(pair.reshape(-1, cols.shape[1]), "y", axis=0, tiled=True)

    my_blocks, first, slot_of_block, lo_rows, q, vup = prepare(
        query, segment_ids, block_of_slot, value_up, seq_index
    )
    slot_seq, slot_half = slot_of_block // 2, slot_of_block % 2
    parts = BLK // PART
    start = ((slot_seq % nzh) * 2 * parts + slot_half * parts) * plane + slot_seq // nzh
    scal = jnp.concatenate([my_blocks, first, start]).astype(jnp.int32)
    head_values = attention(scal, lo_rows, q, vup, [gathered], plane * PART)

    toks, wide = head_values.shape
    spread = jnp.broadcast_to(head_values[None], (nx, toks, wide))
    rows = lax.all_to_all(spread, "x", 0, 0, tiled=True).reshape(nx * toks, wide)
    partial_value = lax.dot_general(
        rows, columns, (((1,), (1,)), ((), ())), preferred_element_type=jnp.float32
    ).astype(jnp.bfloat16)
    n_cols = columns.shape[0]
    own = toks // (nzl * nc)
    partial_value = partial_value.reshape(nx * nzl, nc, own, n_cols)
    keep = lax.dynamic_index_in_dim(partial_value, core, 1, keepdims=False)
    give = lax.dynamic_index_in_dim(partial_value, nc - 1 - core, 1, keepdims=False)
    got = lax.ppermute(give, "core", [(i, nc - 1 - i) for i in range(nc)])
    chip = (keep.astype(jnp.float32) + got.astype(jnp.float32)).astype(jnp.bfloat16)
    terms = lax.all_to_all(chip, ("x", "zl"), 0, 0, tiled=True)
    terms = terms.reshape(nx, nzl, own, n_cols).astype(jnp.float32)
    mixed = jnp.sum(terms, axis=1).astype(jnp.bfloat16)
    return mixed.transpose(1, 0, 2).reshape(own, nx * n_cols)


AXES = {"x": 4, "y": 8, "zh": 2, "zl": 4, "core": 2}


def solution(mesh):
    names = tuple(AXES)
    fine = Mesh(mesh.devices.reshape(tuple(AXES.values())), names)
    seq, head = names[:3], names[3:]
    return jax.shard_map(
        per_device,
        mesh=fine,
        in_specs=(
            P(seq, head, None),
            P(seq, None),
            P(),
            P(),
            P(head, None, None),
            P(head, seq),
        ),
        out_specs=P(names, None),
        check_vma=False,
    )
```

time: 1140 us -> 175 us (0.15); the launches traced: 1130 us -> 174 us
  waiting for transfers between devices: 445 us -> 71.3 us
  local copies, waits for them, and re-layouts: 256 us -> 7.52 us
  other arithmetic: 233 us -> 1.81 us
  loops' own time: 157 us -> 0 us
  blocking collectives: 0 us -> 46.2 us
  starting transfers between devices: 0.08 us -> 21.1 us
  matrix products: 20.8 us -> 2.79 us
    reduce_scatter x1 -> x0, waiting for transfers between devices: 241 us -> none  [per_device(): lax.psum_scatter(rounded.astype(jnp.bfloat16), 'head', scatter_dimension=...]
    reduce_or x128 -> x0, other arithmetic: 232 us -> none  [attend(): jnp.any((key_block <= my_blocks) & (key_seg[block_rows - 1] >= first_seg))]
    dynamic_slice x256 -> x3, local copies, waits for them, and re-layouts: 169 us -> 0.16 us  [the longest x1 0.08 us: prepare(): lax.dynamic_slice_in_dim(segment_ids, my_blocks[i] * BLK, BLK, 0)]
    another operation x129 -> x0, loops' own time: 157 us -> none  [the longest x1 155 us: per_device(): carry = lax.fori_loop(0, block_count, one_block, initial)]
    all_gather x2, waiting for transfers between devices: 202 us -> 67.6 us  [the longest x1 45.7 us: per_device(): lax.all_gather(plane_rows, ('zh', 'zl', 'core'), axis=0, tiled=True)]
    slice x128 -> x2, local copies, waits for them, and re-layouts: 81.5 us -> 0.7 us  [the longest x1 0.59 us: prepare(): my_blocks[i] * BLK]
    all_to_all x0 -> x2, blocking collectives: none -> 46.2 us  [the longest x1 24.7 us: per_device(): plane_rows = lax.all_to_all(spread, ('x', 'y'), 0, 0, tiled=True)]
    dot_general x10 -> x1, matrix products: 20.8 us -> 2.79 us  [per_device(): lax.dot_general(rows, columns, (((1,), (1,)), ((), ())), preferred_elemen...]
  transfers between devices with their start and end apart: 3 -> 5, of which waited for: 2 -> 4; matrix products, arithmetic and copies ran while one was open for 45% -> 2% of each run, Pallas kernels for 0% -> 5%
where the time goes in v1:
time: 175 us; the launch traced here: 174 us
  waiting for transfers between devices  71.3 us (41%)
  blocking collectives  46.2 us (26%)
  starting transfers between devices  21.1 us (12%)
  between operations  14.8 us (8%)
  Pallas kernels  8.59 us (5%)
  local copies, waits for them, and re-layouts  7.52 us (4%)
  matrix products  2.79 us (2%)
  other arithmetic  1.81 us (1%)
    all_gather x1, waiting for transfers between devices, per_device(): lax.all_gather(plane_rows, ('zh', 'zl', 'core'), axis=0, tiled=True)  45.7 us
    all_to_all x1, blocking collectives, per_device(): plane_rows = lax.all_to_all(spread, ('x', 'y'), 0, 0, tiled=True)  24.7 us
    all_gather x1, waiting for transfers between devices, per_device(): lax.all_gather(pair.reshape(-1, cols.shape[1]), 'y', axis=0, tiled=True)  21.9 us
    all_to_all x1, blocking collectives, per_device(): terms = lax.all_to_all(chip, ('x', 'zl'), 0, 0, tiled=True)  21.5 us
    ppermute x1, starting transfers between devices, per_device(): other = lax.ppermute(cols, 'zh', [(i, nzh - 1 - i) for i in range(nzh)])  10.8 us
    pallas_call x1, Pallas kernels, attention(): pl.pallas_call(functools.partial(attention_kernel, len(pieces), part_stri...  8.59 us
    ppermute x1, starting transfers between devices, per_device(): got = lax.ppermute(give, 'core', [(i, nc - 1 - i) for i in range(nc)])  6.73 us
    unnamed x15, local copies, waits for them, and re-layouts  4.54 us
  transfers between devices with their start and end apart: 5, of which 4 were waited for; matrix products, arithmetic and copies ran while one was open for 2% of the time, Pallas kernels for 5%

profile of v1, /device:TPU:1, one launch (start us, length us, event | category | flops | bytes accessed | tf_op | source)
XLA Modules:
  0.0 174.1 jit_solution(6355021250961486820)
XLA Ops:
  6.6 0.8 copy-done
  7.5 24.7 %all_to_all.15 = bf16[32,16,512]{2,1,0:T(8,128)(2,1)} all-to-all(bf16[32,16,512]{2,1,0:T(8,128)(2,1)S(1)} %broadcast_in_dim.21), channel_id=1, replica_groups=mesh['x'=4,'y'=8,'zh'=2,'zl'=4,'core'=2] {'x','y'}, dimensions={0} | all-to-all | bytes 1048576 | tf_op jit(solution)/shard_map/all_to_all | solution.py:134
  32.3 10.8 %collective-permute-start = (bf16[56,1024]{1,0:T(8,128)(2,1)S(1)}, bf16[56,1024]{1,0:T(8,128)(2,1)S(1)}, u32[]{:S(2)}, u32[]{:S(2)}) collective-permute-start(bf16[56,1024]{1,0:T(8,128)(2,1)S(1)} %bitcast.32), channel_id=1, source_target_pairs={{0,8},{8,0},{1,9},{9,1},{2,10},{10,2},{3,11},{11,3},{4,12},{12,4},... | collective-permute-start | bytes 344072 | tf_op jit(solution)/shard_map/ppermute | solution.py:139
  43.1 2.3 %collective-permute-done = bf16[56,1024]{1,0:T(8,128)(2,1)S(1)} collective-permute-done((bf16[56,1024]{1,0:T(8,128)(2,1)S(1)}, bf16[56,1024]{1,0:T(8,128)(2,1)S(1)}, u32[]{:S(2)}, u32[]{:S(2)}) %collective-permute-start) | collective-permute-done | bytes 114720 | tf_op jit(solution)/shard_map/ppermute | solution.py:139
  45.3 0.7 maximum_select_fusion
  46.2 0.6 fusion.5
  48.1 0.6 convert_reduce_fusion
  48.8 0.1 reshape.37
  48.9 0.3 copy.16
  49.3 0.1 slice_reduce_fusion
  49.4 0.1 select_reduce_fusion
  49.6 45.7 %all-gather.3.cloned.1.call-done.rest_0_ = bf16[8192,512]{1,0:T(8,128)(2,1)} async-done(((bf16[512,512]{1,0:T(8,128)(2,1)}), bf16[8192,512]{1,0:T(8,128)(2,1)}) %all-gather.3.cloned.1.call-update) | async-done | bytes 8388624 | tf_op jit(solution)/shard_map/all_gather | solution.py:136
  95.3 0.1 broadcast_in_dim.20.lo_ref
  95.4 3.4 %copy-done.1 = bf16[8192,512]{1,0:T(8,128)(2,1)S(1)} copy-done((bf16[8192,512]{1,0:T(8,128)(2,1)S(1)}, bf16[8192,512]{1,0:T(8,128)(2,1)}, u32[]{:S(2)}) %copy-start.1) | copy-done | bytes 8388632
  98.8 8.6 %latent_attention.1 = bf16[128,1024]{1,0:T(8,128)(2,1)S(1)} custom-call(s32[132]{0:T(256)S(1)} %pad_add_fusion.scal, s32[8,128,1]{2,1,0:T(8,128)S(1)} %broadcast_in_dim.20.lo_ref, bf16[8,128,512]{2,1,0:T(8,128)(2,1)S(1)} %bitcast.25, bf16[8,512,128]{2,1,0:T(8,128)(2,1)S(1)} %pad.4.vup_ref, bf16[8192,512]{1,0:T(8,128)(2,1)S(1)} %copy-done.1), custom_call_target="tpu_custom_call" | custom-call | tf_op jit(solution)/shard_map/latent_attention/pallas_call | solution.py:87
  107.4 1.1 broadcast_in_dim.22
  108.5 3.5 %all-to-all-start.1 = ((bf16[4,128,1024]{2,1,0:T(8,128)(2,1)}), bf16[4,128,1024]{2,1,0:T(8,128)(2,1)S(1)}, u32[]{:S(2)}, u32[]{:S(2)}) async-start(bf16[4,128,1024]{2,1,0:T(8,128)(2,1)} %broadcast_in_dim.22), calls=%async_computation.1 | async-start | bytes 2097152 | tf_op jit(solution)/shard_map/all_to_all | solution.py:154
  112.0 21.9 %all-gather.5.cloned.1.call-done = bf16[896,1024]{1,0:T(8,128)(2,1)} async-done(((bf16[112,1024]{1,0:T(8,128)(2,1)}), bf16[896,1024]{1,0:T(8,128)(2,1)}) %all-gather.5.cloned.1.call-update) | async-done | bytes 1835024 | tf_op jit(solution)/shard_map/all_gather | solution.py:141
  134.0 2.8 %convolution_convert_fusion = bf16[512,896]{1,0:T(8,128)(2,1)S(1)} fusion(bf16[512,1024]{1,0:T(8,128)(2,1)S(1)} %bitcast.27, bf16[896,1024]{1,0:T(8,128)(2,1)} %all-gather.5.cloned.1.call-done), kind=kOutput, calls=%fused_computation.1 | convolution fusion | flops 939982848 | bytes 3801088 | tf_op jit(solution)/shard_map/dot_general | solution.py:155
  136.8 6.7 %collective-permute-start.1 = (bf16[16,16,896]{2,1,0:T(8,128)(2,1)S(1)}, bf16[16,16,896]{2,1,0:T(8,128)(2,1)S(1)}, u32[]{:S(2)}, u32[]{:S(2)}) collective-permute-start(bf16[16,16,896]{2,1,0:T(8,128)(2,1)S(1)} %dynamic-slice_bitcast_fusion), channel_id=1, source_target_pairs={{0,1},{1,0},{2,3},{3,2},{4,5},{5,4},{6,7},{7,6},{8,9},{9,8},{10,11... | collective-permute-start | bytes 1376264 | tf_op jit(solution)/shard_map/ppermute | solution.py:163
  143.5 1.4 collective-permute-done.1
  145.0 0.1 fusion
  145.1 21.5 %all_to_all.16 = bf16[16,16,896]{2,1,0:T(8,128)(2,1)S(1)} all-to-all(bf16[16,16,896]{2,1,0:T(8,128)(2,1)S(1)} %fusion), channel_id=1, replica_groups=mesh['x'=4,'y'=8,'zh'=2,'zl'=4,'core'=2] {'x','zl'}, dimensions={0} | all-to-all | bytes 917504 | tf_op jit(solution)/shard_map/all_to_all | solution.py:165
  166.6 0.7 copy.14
  (28 shorter events, 0.7 us)
Async XLA Ops:
  6.5 0.9 copy-start
  6.5 25.8 %copy-start.4 = (bf16[1024,56]{0,1:T(8,128)(2,1)S(1)}, bf16[1024,56]{0,1:T(8,128)(2,1)}, u32[]{:S(2)}) copy-start(bf16[1024,56]{0,1:T(8,128)(2,1)} %param.11) | copy-start | bytes 344068
  6.5 39.5 %copy-start.6 = (s32[128]{0:T(128)S(1)}, s32[128]{0:T(128)}, u32[]{:S(2)}) copy-start(s32[128]{0:T(128)} %param.9) | copy-start | bytes 1540
  6.5 41.4 %copy-start.5 = (s32[8192]{0:T(1024)S(1)}, s32[8192]{0:T(1024)}, u32[]{:S(2)}) copy-start(s32[8192]{0:T(1024)} %param.8) | copy-start | bytes 98308
  6.5 42.3 %copy-start.2 = (bf16[128,8,512]{2,1,0:T(8,128)(2,1)S(1)}, bf16[128,8,512]{2,1,0:T(8,128)(2,1)}, u32[]{:S(2)}) copy-start(bf16[128,8,512]{2,1,0:T(8,128)(2,1)} %param.6) | copy-start | bytes 3145732
  6.5 88.8 %all-gather.3.cloned.1.call-start = ((), (), s32[]{:S(2)}) async-start(), calls=%async_computation.3 | async-start | bytes 8912896 | tf_op jit(solution)/shard_map/all_gather | solution.py:136
  32.2 17.0 %copy-start.3 = (bf16[8,448,128]{2,1,0:T(8,128)(2,1)S(1)}, bf16[8,448,128]{2,1,0:T(8,128)(2,1)}, u32[]{:S(2)}) copy-start(bf16[8,448,128]{2,1,0:T(8,128)(2,1)} %param.10) | copy-start | bytes 2752516
  32.2 101.7 %all-gather.5.cloned.1.call-start = ((), (), s32[]{:S(2)}) async-start(), calls=%async_computation.4 | async-start | bytes 2064384 | tf_op jit(solution)/shard_map/all_gather | solution.py:141
  32.3 13.0 %collective-permute-start = (bf16[56,1024]{1,0:T(8,128)(2,1)S(1)}, bf16[56,1024]{1,0:T(8,128)(2,1)S(1)}, u32[]{:S(2)}, u32[]{:S(2)}) collective-permute-start(bf16[56,1024]{1,0:T(8,128)(2,1)S(1)} %bitcast.32), channel_id=1, source_target_pairs={{0,8},{8,0},{1,9},{9,1},{2,10},{10,2},{3,11},{11,3},{4,12},{12,4},... | collective-permute-start | bytes 344072 | tf_op jit(solution)/shard_map/ppermute | solution.py:139
  95.4 3.4 %copy-start.1 = (bf16[8192,512]{1,0:T(8,128)(2,1)S(1)}, bf16[8192,512]{1,0:T(8,128)(2,1)}, u32[]{:S(2)}) copy-start(bf16[8192,512]{1,0:T(8,128)(2,1)} %all-gather.3.cloned.1.call-done.rest_0_) | copy-start | bytes 25165828
  108.5 25.5 %all-to-all-start.1 = ((bf16[4,128,1024]{2,1,0:T(8,128)(2,1)}), bf16[4,128,1024]{2,1,0:T(8,128)(2,1)S(1)}, u32[]{:S(2)}, u32[]{:S(2)}) async-start(bf16[4,128,1024]{2,1,0:T(8,128)(2,1)} %broadcast_in_dim.22), calls=%async_computation.1 | async-start | bytes 2097152 | tf_op jit(solution)/shard_map/all_to_all | solution.py:154
  136.8 8.2 %collective-permute-start.1 = (bf16[16,16,896]{2,1,0:T(8,128)(2,1)S(1)}, bf16[16,16,896]{2,1,0:T(8,128)(2,1)S(1)}, u32[]{:S(2)}, u32[]{:S(2)}) collective-permute-start(bf16[16,16,896]{2,1,0:T(8,128)(2,1)S(1)} %dynamic-slice_bitcast_fusion), channel_id=1, source_target_pairs={{0,1},{1,0},{2,3},{3,2},{4,5},{5,4},{6,7},{7,6},{8,9},{9,8},{10,11... | collective-permute-start | bytes 1376264 | tf_op jit(solution)/shard_map/ppermute | solution.py:163
Sparse Core Ops, SparseCore 0:
  32.4 62.9 all-gather.2
  97.4 36.5 all-gather.4

commit v2 on v1

--- a/solution.py
+++ b/solution.py
@@ -12,27 +12,18 @@
 BLK = 64
 CHUNK = 8
 KEYS = BLK * CHUNK
-PART = 16
+ROWS, LANES = 32, 128
+PARTS = 8
 exp2_scale = 192 ** (-0.5) * math.log2(math.e)
 floor_max = -1e30
 masked_score = -2e30
 
 
-def attention_kernel(n_pieces, part_stride, scal, lo_ref, q_ref, vup_ref, *rest):
-    pieces = rest[:n_pieces]
-    out_ref, lat, kbuf, acc, done, sems = rest[n_pieces:]
+def attention_kernel(scal, lo_ref, q_ref, vup_ref, lat, out_ref, kbuf, acc, done):
     heads, toks, width = q_ref.shape
     rows = heads * BLK
-    copies = []
-    at = 0
-    for i, piece in enumerate(pieces):
-        n = piece.shape[0]
-        copies.append(pltpu.make_async_copy(piece, lat.at[pl.ds(at, n)], sems.at[i]))
-        at += n
-    for c in copies:
-        c.start()
-    for c in copies:
-        c.wait()
+    slices = lat.shape[0] // 16
+    across = width // LANES
     last_block = scal.shape[0] - 5
 
     for b in range(toks // BLK):
@@ -48,10 +39,10 @@
             base = first + i * CHUNK
             for j in range(CHUNK):
                 src = scal[4 + jnp.minimum(base + j, last_block)]
-                for part in range(BLK // PART):
-                    row = pl.multiple_of(src * PART + part * part_stride, PART)
-                    at = j * BLK + part * PART
-                    kbuf[at : at + PART, :] = lat[pl.ds(row, PART), :]
+                for part in range(PARTS):
+                    row = j * BLK + part // across * ROWS
+                    lane = part % across * LANES
+                    kbuf[row : row + ROWS, lane : lane + LANES] = lat[src + part * slices]
             keys = kbuf[...]
             s = lax.dot_general(q, keys, (((1,), (1,)), ((), ())), preferred_element_type=jnp.float32)
             kp = base * BLK + lax.broadcasted_iota(jnp.int32, (1, KEYS), 1)
@@ -79,27 +70,23 @@
         ).astype(jnp.bfloat16)
 
 
-def attention(scal, lo, q, vup, pieces, part_stride):
+def attention(scal, lo, q, vup, lat):
     heads, toks, width = q.shape
     vh = vup.shape[2]
-    total_rows = sum(p.shape[0] for p in pieces)
     vmem = pl.BlockSpec(memory_space=pltpu.VMEM)
     return pl.pallas_call(
-        functools.partial(attention_kernel, len(pieces), part_stride),
+        attention_kernel,
         out_shape=jax.ShapeDtypeStruct((toks, heads * vh), jnp.bfloat16),
-        in_specs=[pl.BlockSpec(memory_space=pltpu.SMEM), vmem, vmem, vmem]
-        + [pl.BlockSpec(memory_space=pl.ANY)] * len(pieces),
+        in_specs=[pl.BlockSpec(memory_space=pltpu.SMEM)] + [vmem] * 4,
         out_specs=vmem,
         scratch_shapes=[
-            pltpu.VMEM((total_rows, width), jnp.bfloat16),
             pltpu.VMEM((KEYS, width), jnp.bfloat16),
             pltpu.VMEM((heads * BLK, width), jnp.float32),
             pltpu.VMEM((heads, toks, width), jnp.bfloat16),
-            pltpu.SemaphoreType.DMA((len(pieces),)),
         ],
         compiler_params=pltpu.CompilerParams(vmem_limit_bytes=40 * 2**20),
         name="latent_attention",
-    )(scal, lo, q, vup, *pieces)
+    )(scal, lo, q, vup, lat)
 
 
 def prepare(query, segment_ids, block_of_slot, value_up, seq_index):
@@ -128,28 +115,42 @@
     x, y, zh = (lax.axis_index(a) for a in ("x", "y", "zh"))
     zl, core = lax.axis_index("zl"), lax.axis_index("core")
     seq_index = (x * ny + y) * nzh + zh
+    toks, width = latent.shape
+    halves, across = toks // BLK, width // LANES
 
-    part = lax.dynamic_slice_in_dim(latent, (zl * nc + core) * PART, PART, 0)
+    part = latent.reshape(halves, BLK // ROWS, ROWS, across, LANES).transpose(1, 3, 0, 2, 4)
+    part = part.reshape(PARTS, halves, ROWS, LANES)
+    part = lax.dynamic_index_in_dim(part, zl * nc + core, 0, keepdims=False)
     spread = jnp.broadcast_to(part[None], (plane,) + part.shape)
     plane_rows = lax.all_to_all(spread, ("x", "y"), 0, 0, tiled=True)
-    plane_rows = plane_rows.reshape(plane * PART, latent.shape[1])
-    gathered = lax.all_gather(plane_rows, ("zh", "zl", "core"), axis=0, tiled=True)
+    out_proj, plane_rows = lax.optimization_barrier((out_proj, plane_rows))
+    gathered = lax.all_gather(
+        plane_rows.reshape(plane * halves * ROWS, LANES), ("zh", "zl", "core"), axis=0, tiled=True
+    )
+    gathered = gathered.reshape(-1, ROWS, LANES)
 
     cols = out_proj.T
     other = lax.ppermute(cols, "zh", [(i, nzh - 1 - i) for i in range(nzh)])
-    pair = jnp.where(zh == 0, jnp.stack([cols, other]), jnp.stack([other, cols]))
-    columns = lax.all_gather(pair.reshape(-1, cols.shape[1]), "y", axis=0, tiled=True)
+
+    def over_y(piece):
+        return lax.all_to_all(jnp.broadcast_to(piece[None], (ny,) + piece.shape), "y", 0, 0, tiled=True)
+
+    mine = over_y(cols)
+    theirs = over_y(other)
+    columns = jnp.where(zh == 0, jnp.stack([mine, theirs], 1), jnp.stack([theirs, mine], 1))
+    columns = columns.reshape(-1, cols.shape[1])
 
     my_blocks, first, slot_of_block, lo_rows, q, vup = prepare(
         query, segment_ids, block_of_slot, value_up, seq_index
     )
     slot_seq, slot_half = slot_of_block // 2, slot_of_block % 2
-    parts = BLK // PART
-    start = ((slot_seq % nzh) * 2 * parts + slot_half * parts) * plane + slot_seq // nzh
+    slices = plane * halves
+    start = (slot_seq % nzh) * PARTS * slices + slot_seq // nzh * halves + slot_half
     scal = jnp.concatenate([my_blocks, first, start]).astype(jnp.int32)
-    head_values = attention(scal, lo_rows, q, vup, [gathered], plane * PART)
+    scal, columns = lax.optimization_barrier((scal, columns))
+    head_values = attention(scal, lo_rows, q, vup, gathered)
 
-    toks, wide = head_values.shape
+    wide = head_values.shape[1]
     spread = jnp.broadcast_to(head_values[None], (nx, toks, wide))
     rows = lax.all_to_all(spread, "x", 0, 0, tiled=True).reshape(nx * toks, wide)
     partial_value = lax.dot_general(

time: 175 us -> 170 us (0.971)
  the two profiles are of different devices: /device:TPU:1 before, /device:TPU:48 now
where the time goes in v2:
time: 170 us; the launch traced here: 169 us
  blocking collectives  46.6 us (27%)
  waiting for transfers between devices  45.7 us (27%)
  starting transfers between devices  37.5 us (22%)
  between operations  14.9 us (9%)
  local copies, waits for them, and re-layouts  12.2 us (7%)
  Pallas kernels  5.91 us (3%)
  other arithmetic  5.08 us (3%)
    all_to_all x1, blocking collectives, per_device(): plane_rows = lax.all_to_all(spread, ('x', 'y'), 0, 0, tiled=True)  25 us
    all_to_all x1, blocking collectives, per_device(): terms = lax.all_to_all(chip, ('x', 'zl'), 0, 0, tiled=True)  21.5 us
    all_to_all x2, waiting for transfers between devices, over_y(): lax.all_to_all(jnp.broadcast_to(piece[None], (ny,) + piece.shape), 'y', 0...  19.1 us
    all_to_all x1, waiting for transfers between devices, per_device(): lax.all_to_all(spread, 'x', 0, 0, tiled=True).reshape(nx * toks, wide)  15.5 us
    all_to_all x2, starting transfers between devices, over_y(): lax.all_to_all(jnp.broadcast_to(piece[None], (ny,) + piece.shape), 'y', 0...  13.9 us
    ppermute x1, starting transfers between devices, per_device(): other = lax.ppermute(cols, 'zh', [(i, nzh - 1 - i) for i in range(nzh)])  11 us
    all_to_all x1, starting transfers between devices, per_device(): lax.all_to_all(spread, 'x', 0, 0, tiled=True).reshape(nx * toks, wide)  10.6 us
    ppermute x1, waiting for transfers between devices, per_device(): other = lax.ppermute(cols, 'zh', [(i, nzh - 1 - i) for i in range(nzh)])  6.38 us
  transfers between devices with their start and end apart: 6, of which 6 were waited for; matrix products, arithmetic and copies ran while one was open for 5% of the time, Pallas kernels for 0%

profile of v2, /device:TPU:48, one launch (start us, length us, event | category | flops | bytes accessed | tf_op | source)
XLA Modules:
  0.0 169.1 jit_solution(4305349242016304303)
XLA Ops:
  6.5 1.0 reshape.48
  7.7 25.0 %all_to_all.25 = bf16[32,2,32,128]{3,2,1,0:T(8,128)(2,1)} all-to-all(bf16[32,2,32,128]{3,2,1,0:T(8,128)(2,1)S(1)} %broadcast_in_dim.27), channel_id=1, replica_groups=mesh['x'=4,'y'=8,'zh'=2,'zl'=4,'core'=2] {'x','y'}, dimensions={0} | all-to-all | bytes 1048576 | tf_op jit(solution)/shard_map/all_to_all | solution.py:125
  32.7 1.1 broadcast_in_dim.28
  33.9 6.0 %all-to-all-start.1 = ((bf16[8,56,1024]{2,1,0:T(8,128)(2,1)}), bf16[8,56,1024]{2,1,0:T(8,128)(2,1)S(1)}, u32[]{:S(2)}, u32[]{:S(2)}) async-start(bf16[8,56,1024]{2,1,0:T(8,128)(2,1)} %broadcast_in_dim.28), calls=%async_computation.1 | async-start | bytes 1835008 | tf_op jit(solution)/shard_map/all_to_all | solution.py:136
  39.8 11.0 %collective-permute-start = (bf16[56,1024]{1,0:T(8,128)(2,1)S(1)}, bf16[56,1024]{1,0:T(8,128)(2,1)S(1)}, u32[]{:S(2)}, u32[]{:S(2)}) collective-permute-start(bf16[56,1024]{1,0:T(8,128)(2,1)S(1)} %bitcast.41), channel_id=1, source_target_pairs={{0,8},{8,0},{1,9},{9,1},{2,10},{10,2},{3,11},{11,3},{4,12},{12,4},... | collective-permute-start | bytes 344072 | tf_op jit(solution)/shard_map/ppermute | solution.py:133
  50.9 6.4 %collective-permute-done = bf16[56,1024]{1,0:T(8,128)(2,1)S(1)} collective-permute-done((bf16[56,1024]{1,0:T(8,128)(2,1)S(1)}, bf16[56,1024]{1,0:T(8,128)(2,1)S(1)}, u32[]{:S(2)}, u32[]{:S(2)}) %collective-permute-start) | collective-permute-done | bytes 114720 | tf_op jit(solution)/shard_map/ppermute | solution.py:133
  57.3 3.2 %all-to-all-done.1 = bf16[8,56,1024]{2,1,0:T(8,128)(2,1)S(1)} async-done(((bf16[8,56,1024]{2,1,0:T(8,128)(2,1)}), bf16[8,56,1024]{2,1,0:T(8,128)(2,1)S(1)}, u32[]{:S(2)}, u32[]{:S(2)}) %all-to-all-start.1) | async-done | bytes 917536 | tf_op jit(solution)/shard_map/all_to_all | solution.py:136
  60.5 1.1 broadcast_in_dim.29
  61.6 7.9 %all-to-all-start.2 = ((bf16[8,56,1024]{2,1,0:T(8,128)(2,1)}), bf16[8,56,1024]{2,1,0:T(8,128)(2,1)}, u32[]{:S(2)}, u32[]{:S(2)}) async-start(bf16[8,56,1024]{2,1,0:T(8,128)(2,1)} %broadcast_in_dim.29), calls=%async_computation.2 | async-start | bytes 1835008 | tf_op jit(solution)/shard_map/all_to_all | solution.py:136
  72.8 1.3 pad.4.vup_ref
  74.4 15.9 %all-to-all-done.2 = bf16[8,56,1024]{2,1,0:T(8,128)(2,1)} async-done(((bf16[8,56,1024]{2,1,0:T(8,128)(2,1)}), bf16[8,56,1024]{2,1,0:T(8,128)(2,1)}, u32[]{:S(2)}, u32[]{:S(2)}) %all-to-all-start.2) | async-done | bytes 917536 | tf_op jit(solution)/shard_map/all_to_all | solution.py:136
  90.3 3.0 %maximum_select_fusion = bf16[8,2,56,1024]{3,2,1,0:T(8,128)(2,1)} fusion(bf16[8,1,56,1024]{3,2,1,0:T(8,128)(2,1)} %bitcast.7, bf16[8,1,56,1024]{3,2,1,0:T(8,128)(2,1)S(1)} %bitcast.31, pred[]{:T(512)S(6)} %eq.22), kind=kLoop, calls=%fused_computation.1 | loop fusion | flops 2752512 | bytes 3670017 | tf_op jit(solution)/shard_map/jit(_where)/select_n | solution.py:140
  93.3 3.0 %all-gather.2.cloned.1.call-done = bf16[32768,128]{1,0:T(8,128)(2,1)} async-done(((bf16[2048,128]{1,0:T(8,128)(2,1)}), bf16[32768,128]{1,0:T(8,128)(2,1)}) %all-gather.2.cloned.1.call-update) | async-done | bytes 8388624 | tf_op jit(solution)/shard_map/all_gather | solution.py:127
  96.3 3.4 %copy-done = bf16[32768,128]{1,0:T(8,128)(2,1)S(1)} copy-done((bf16[32768,128]{1,0:T(8,128)(2,1)S(1)}, bf16[32768,128]{1,0:T(8,128)(2,1)}, u32[]{:S(2)}) %copy-start) | copy-done | bytes 8388632
  99.7 5.9 %latent_attention.1 = bf16[128,1024]{1,0:T(8,128)(2,1)S(1)} custom-call(s32[132]{0:T(256)S(1)} %pad_add_fusion.scal, s32[8,128,1]{2,1,0:T(8,128)S(1)} %broadcast_in_dim.30.lo_ref, bf16[8,128,512]{2,1,0:T(8,128)(2,1)S(1)} %bitcast.30, bf16[8,512,128]{2,1,0:T(8,128)(2,1)S(1)} %pad.4.vup_ref, bf16[1024,32,128]{2,1,0:T(8,128)(2,1)S(1)} %bitcast.29), custom_call_target="tpu_custom_call" | custom-call | tf_op jit(solution)/shard_map/latent_attention/pallas_call | solution.py:77
  105.7 1.1 broadcast_in_dim.31
  106.7 10.6 %all-to-all-start.3 = ((bf16[4,128,1024]{2,1,0:T(8,128)(2,1)}), bf16[4,128,1024]{2,1,0:T(8,128)(2,1)S(1)}, u32[]{:S(2)}, u32[]{:S(2)}) async-start(bf16[4,128,1024]{2,1,0:T(8,128)(2,1)} %broadcast_in_dim.31), calls=%async_computation.3 | async-start | bytes 2097152 | tf_op jit(solution)/shard_map/all_to_all | solution.py:155
  117.4 15.5 %all-to-all-done.3 = bf16[4,128,1024]{2,1,0:T(8,128)(2,1)S(1)} async-done(((bf16[4,128,1024]{2,1,0:T(8,128)(2,1)}), bf16[4,128,1024]{2,1,0:T(8,128)(2,1)S(1)}, u32[]{:S(2)}, u32[]{:S(2)}) %all-to-all-start.3) | async-done | bytes 1048608 | tf_op jit(solution)/shard_map/all_to_all | solution.py:155
  132.9 1.3 convolution_convert_fusion
  134.2 0.9 copy-done.3
  135.1 1.9 %collective-permute-start.1 = (bf16[16,16,896]{2,1,0:T(8,128)(2,1)S(1)}, bf16[16,16,896]{2,1,0:T(8,128)(2,1)S(1)}, u32[]{:S(2)}, u32[]{:S(2)}) collective-permute-start(bf16[16,16,896]{2,1,0:T(8,128)(2,1)S(1)} %dynamic-slice_bitcast_fusion), channel_id=1, source_target_pairs={{0,1},{1,0},{2,3},{3,2},{4,5},{5,4},{6,7},{7,6},{8,9},{9,8},{10,11... | collective-permute-start | bytes 1376264 | tf_op jit(solution)/shard_map/ppermute | solution.py:164
  137.1 1.8 %collective-permute-done.1 = bf16[16,16,896]{2,1,0:T(8,128)(2,1)S(1)} collective-permute-done((bf16[16,16,896]{2,1,0:T(8,128)(2,1)S(1)}, bf16[16,16,896]{2,1,0:T(8,128)(2,1)S(1)}, u32[]{:S(2)}, u32[]{:S(2)}) %collective-permute-start.1) | collective-permute-done | bytes 458784 | tf_op jit(solution)/shard_map/ppermute | solution.py:164
  138.9 1.1 fusion
  140.0 21.5 %all_to_all.26 = bf16[16,16,896]{2,1,0:T(8,128)(2,1)S(1)} all-to-all(bf16[16,16,896]{2,1,0:T(8,128)(2,1)S(1)} %fusion), channel_id=1, replica_groups=mesh['x'=4,'y'=8,'zh'=2,'zl'=4,'core'=2] {'x','zl'}, dimensions={0} | all-to-all | bytes 917504 | tf_op jit(solution)/shard_map/all_to_all | solution.py:166
  (33 shorter events, 3.3 us)
Async XLA Ops:
  6.5 26.2 %copy-start.4 = (bf16[1024,56]{0,1:T(8,128)(2,1)S(1)}, bf16[1024,56]{0,1:T(8,128)(2,1)}, u32[]{:S(2)}) copy-start(bf16[1024,56]{0,1:T(8,128)(2,1)} %param.11) | copy-start | bytes 344068
  6.5 89.7 %all-gather.2.cloned.1.call-start = ((), (), s32[]{:S(2)}) async-start(), calls=%async_computation.5 | async-start | bytes 8912896 | tf_op jit(solution)/shard_map/all_gather | solution.py:127
  33.9 26.6 %all-to-all-start.1 = ((bf16[8,56,1024]{2,1,0:T(8,128)(2,1)}), bf16[8,56,1024]{2,1,0:T(8,128)(2,1)S(1)}, u32[]{:S(2)}, u32[]{:S(2)}) async-start(bf16[8,56,1024]{2,1,0:T(8,128)(2,1)} %broadcast_in_dim.28), calls=%async_computation.1 | async-start | bytes 1835008 | tf_op jit(solution)/shard_map/all_to_all | solution.py:136
  39.8 29.6 %copy-start.6 = (s32[128]{0:T(128)S(1)}, s32[128]{0:T(128)}, u32[]{:S(2)}) copy-start(s32[128]{0:T(128)} %param.9) | copy-start | bytes 1540
  39.8 31.7 %copy-start.5 = (s32[8192]{0:T(1024)S(1)}, s32[8192]{0:T(1024)}, u32[]{:S(2)}) copy-start(s32[8192]{0:T(1024)} %param.8) | copy-start | bytes 98308
  39.8 32.6 %copy-start.2 = (bf16[128,8,512]{2,1,0:T(8,128)(2,1)S(1)}, bf16[128,8,512]{2,1,0:T(8,128)(2,1)}, u32[]{:S(2)}) copy-start(bf16[128,8,512]{2,1,0:T(8,128)(2,1)} %param.6) | copy-start | bytes 3145732
  39.8 17.4 %collective-permute-start = (bf16[56,1024]{1,0:T(8,128)(2,1)S(1)}, bf16[56,1024]{1,0:T(8,128)(2,1)S(1)}, u32[]{:S(2)}, u32[]{:S(2)}) collective-permute-start(bf16[56,1024]{1,0:T(8,128)(2,1)S(1)} %bitcast.41), channel_id=1, source_target_pairs={{0,8},{8,0},{1,9},{9,1},{2,10},{10,2},{3,11},{11,3},{4,12},{12,4},... | collective-permute-start | bytes 344072 | tf_op jit(solution)/shard_map/ppermute | solution.py:133
  61.6 28.7 %all-to-all-start.2 = ((bf16[8,56,1024]{2,1,0:T(8,128)(2,1)}), bf16[8,56,1024]{2,1,0:T(8,128)(2,1)}, u32[]{:S(2)}, u32[]{:S(2)}) async-start(bf16[8,56,1024]{2,1,0:T(8,128)(2,1)} %broadcast_in_dim.29), calls=%async_computation.2 | async-start | bytes 1835008 | tf_op jit(solution)/shard_map/all_to_all | solution.py:136
  96.3 3.4 %copy-start = (bf16[32768,128]{1,0:T(8,128)(2,1)S(1)}, bf16[32768,128]{1,0:T(8,128)(2,1)}, u32[]{:S(2)}) copy-start(bf16[32768,128]{1,0:T(8,128)(2,1)} %all-gather.2.cloned.1.call-done) | copy-start | bytes 25165828
  105.6 27.2 %copy-start.1 = (bf16[8,2,56,1024]{3,2,1,0:T(8,128)(2,1)S(1)}, bf16[8,2,56,1024]{3,2,1,0:T(8,128)(2,1)}, u32[]{:S(2)}) copy-start(bf16[8,2,56,1024]{3,2,1,0:T(8,128)(2,1)} %maximum_select_fusion) | copy-start | bytes 5505028
  106.7 26.1 %all-to-all-start.3 = ((bf16[4,128,1024]{2,1,0:T(8,128)(2,1)}), bf16[4,128,1024]{2,1,0:T(8,128)(2,1)S(1)}, u32[]{:S(2)}, u32[]{:S(2)}) async-start(bf16[4,128,1024]{2,1,0:T(8,128)(2,1)} %broadcast_in_dim.31), calls=%async_computation.3 | async-start | bytes 2097152 | tf_op jit(solution)/shard_map/all_to_all | solution.py:155
  134.2 0.9 copy-start.3
  135.1 3.7 %collective-permute-start.1 = (bf16[16,16,896]{2,1,0:T(8,128)(2,1)S(1)}, bf16[16,16,896]{2,1,0:T(8,128)(2,1)S(1)}, u32[]{:S(2)}, u32[]{:S(2)}) collective-permute-start(bf16[16,16,896]{2,1,0:T(8,128)(2,1)S(1)} %dynamic-slice_bitcast_fusion), channel_id=1, source_target_pairs={{0,1},{1,0},{2,3},{3,2},{4,5},{5,4},{6,7},{7,6},{8,9},{9,8},{10,11... | collective-permute-start | bytes 1376264 | tf_op jit(solution)/shard_map/ppermute | solution.py:164
Sparse Core Ops, SparseCore 0:
  32.9 63.3 all-gather.1

commit v3 on v2

--- a/solution.py
+++ b/solution.py
@@ -14,6 +14,7 @@
 KEYS = BLK * CHUNK
 ROWS, LANES = 32, 128
 PARTS = 8
+FEW = 44
 exp2_scale = 192 ** (-0.5) * math.log2(math.e)
 floor_max = -1e30
 masked_score = -2e30
@@ -108,6 +109,25 @@
     return my_blocks, first, slot_of_block, lo_rows, q, vup
 
 
+def need_tables(segment_ids, block_of_slot, plane, nzh, halves):
+    n = block_of_slot.shape[0]
+    firsts = segment_ids.reshape(n, BLK)[:, 0]
+    block_first = jnp.sum((segment_ids[None, :] < firsts[:, None]).astype(jnp.int32), axis=1) // BLK
+    blocks = jnp.arange(n, dtype=jnp.int32)
+    slot_first = jnp.sum(
+        jnp.where(block_of_slot[:, None] == blocks[None, :], block_first[None, :], 0), axis=1
+    )
+    pair = (slot_first[:, None] <= block_of_slot[None, :]) & (
+        block_of_slot[None, :] <= block_of_slot[:, None]
+    )
+    need = jnp.any(pair.reshape(plane, nzh * halves, n), axis=1)
+    slot_plane = blocks // halves % nzh
+    before = (blocks[:, None] < blocks[None, :]) & (slot_plane[:, None] == slot_plane[None, :])
+    rank = jnp.dot(need.astype(jnp.bfloat16), before.astype(jnp.bfloat16), preferred_element_type=jnp.float32)
+    most = jnp.max(jnp.where(need, rank, -1.0)) + 1.0
+    return need, rank, most <= FEW
+
+
 def per_device(query, latent, segment_ids, block_of_slot, value_up, out_proj):
     nx, ny, nzh = (lax.axis_size(a) for a in ("x", "y", "zh"))
     nzl, nc = lax.axis_size("zl"), lax.axis_size("core")
@@ -117,38 +137,67 @@
     seq_index = (x * ny + y) * nzh + zh
     toks, width = latent.shape
     halves, across = toks // BLK, width // LANES
+    slices = plane * halves
+
+    cols = out_proj.T
+    other = lax.ppermute(cols, "zh", [(i, nzh - 1 - i) for i in range(nzh)])
 
     part = latent.reshape(halves, BLK // ROWS, ROWS, across, LANES).transpose(1, 3, 0, 2, 4)
     part = part.reshape(PARTS, halves, ROWS, LANES)
     part = lax.dynamic_index_in_dim(part, zl * nc + core, 0, keepdims=False)
     spread = jnp.broadcast_to(part[None], (plane,) + part.shape)
     plane_rows = lax.all_to_all(spread, ("x", "y"), 0, 0, tiled=True)
-    out_proj, plane_rows = lax.optimization_barrier((out_proj, plane_rows))
-    gathered = lax.all_gather(
-        plane_rows.reshape(plane * halves * ROWS, LANES), ("zh", "zl", "core"), axis=0, tiled=True
-    )
-    gathered = gathered.reshape(-1, ROWS, LANES)
-
-    cols = out_proj.T
-    other = lax.ppermute(cols, "zh", [(i, nzh - 1 - i) for i in range(nzh)])
+    plane_rows = plane_rows.reshape(slices, ROWS * LANES)
+
+    need, rank, fits = need_tables(segment_ids, block_of_slot, plane, nzh, halves)
+    my_need = lax.dynamic_index_in_dim(need, x * ny + y, 0, keepdims=False)
+    my_rank = lax.dynamic_index_in_dim(rank, x * ny + y, 0, keepdims=False).astype(jnp.int32)
+    row_need = lax.dynamic_index_in_dim(my_need.reshape(plane, nzh, halves), zh, 1, keepdims=False)
+    row_rank = lax.dynamic_index_in_dim(my_rank.reshape(plane, nzh, halves), zh, 1, keepdims=False)
+    row_rank = jnp.where(row_need, row_rank, -1).reshape(1, slices)
 
     def over_y(piece):
         return lax.all_to_all(jnp.broadcast_to(piece[None], (ny,) + piece.shape), "y", 0, 0, tiled=True)
 
-    mine = over_y(cols)
-    theirs = over_y(other)
-    columns = jnp.where(zh == 0, jnp.stack([mine, theirs], 1), jnp.stack([theirs, mine], 1))
-    columns = columns.reshape(-1, cols.shape[1])
-
-    my_blocks, first, slot_of_block, lo_rows, q, vup = prepare(
-        query, segment_ids, block_of_slot, value_up, seq_index
-    )
-    slot_seq, slot_half = slot_of_block // 2, slot_of_block % 2
-    slices = plane * halves
-    start = (slot_seq % nzh) * PARTS * slices + slot_seq // nzh * halves + slot_half
-    scal = jnp.concatenate([my_blocks, first, start]).astype(jnp.int32)
-    scal, columns = lax.optimization_barrier((scal, columns))
-    head_values = attention(scal, lo_rows, q, vup, gathered)
+    def attend(few, operands):
+        plane_rows, cols, other, query, segment_ids, block_of_slot, value_up, my_rank, row_rank = operands
+        if few:
+            kept = FEW
+            pick = (row_rank == jnp.arange(kept, dtype=jnp.int32)[:, None]).astype(jnp.bfloat16)
+            sent = jnp.dot(pick, plane_rows, preferred_element_type=jnp.float32).astype(jnp.bfloat16)
+        else:
+            kept = slices
+            sent = plane_rows
+        gathered = lax.all_gather(sent.reshape(kept * ROWS, LANES), ("zh", "zl", "core"), axis=0, tiled=True)
+        gathered = gathered.reshape(-1, ROWS, LANES)
+
+        cols, other, sent = lax.optimization_barrier((cols, other, sent))
+        mine = over_y(cols)
+        theirs = over_y(other)
+        columns = jnp.where(zh == 0, jnp.stack([mine, theirs], 1), jnp.stack([theirs, mine], 1))
+        columns = columns.reshape(-1, cols.shape[1])
+
+        my_blocks, first, slot_of_block, lo_rows, q, vup = prepare(
+            query, segment_ids, block_of_slot, value_up, seq_index
+        )
+        slot_seq, slot_half = slot_of_block // halves, slot_of_block % halves
+        if few:
+            slots = jnp.arange(block_of_slot.shape[0], dtype=jnp.int32)
+            place = jnp.sum(jnp.where(slot_of_block[:, None] == slots[None, :], my_rank[None, :], 0), axis=1)
+            place = jnp.minimum(place, kept - 1)
+        else:
+            place = slot_seq // nzh * halves + slot_half
+        start = (slot_seq % nzh) * PARTS * kept + place
+        scal = jnp.concatenate([my_blocks, first, start]).astype(jnp.int32)
+        scal, columns = lax.optimization_barrier((scal, columns))
+        return attention(scal, lo_rows, q, vup, gathered), columns
+
+    head_values, columns = lax.cond(
+        fits,
+        functools.partial(attend, True),
+        functools.partial(attend, False),
+        (plane_rows, cols, other, query, segment_ids, block_of_slot, value_up, my_rank, row_rank),
+    )
 
     wide = head_values.shape[1]
     spread = jnp.broadcast_to(head_values[None], (nx, toks, wide))

time: 170 us -> 166 us (0.976)
  the two profiles are of different devices: /device:TPU:48 before, /device:TPU:1 now
where the time goes in v3:
time: 166 us; the launch traced here: 165 us
  blocking collectives  53.9 us (32%)
  starting transfers between devices  39.3 us (24%)
  waiting for transfers between devices  29.9 us (18%)
  between operations  14.2 us (9%)
  local copies, waits for them, and re-layouts  11.1 us (7%)
  other arithmetic  7.39 us (4%)
  matrix products  4.46 us (3%)
  Pallas kernels  3.64 us (2%)
    all_to_all x1, blocking collectives, over_y(): lax.all_to_all(jnp.broadcast_to(piece[None], (ny,) + piece.shape), 'y', 0...  29 us
    all_to_all x1, blocking collectives, per_device(): terms = lax.all_to_all(chip, ('x', 'zl'), 0, 0, tiled=True)  24.9 us
    all_to_all x1, waiting for transfers between devices, over_y(): lax.all_to_all(jnp.broadcast_to(piece[None], (ny,) + piece.shape), 'y', 0...  18.1 us
    ppermute x1, starting transfers between devices, per_device(): other = lax.ppermute(cols, 'zh', [(i, nzh - 1 - i) for i in range(nzh)])  10.6 us
    all_to_all x1, starting transfers between devices, per_device(): plane_rows = lax.all_to_all(spread, ('x', 'y'), 0, 0, tiled=True)  10.5 us
    all_to_all x1, waiting for transfers between devices, per_device(): lax.all_to_all(spread, 'x', 0, 0, tiled=True).reshape(nx * toks, wide)  10.3 us
    ppermute x1, starting transfers between devices, per_device(): got = lax.ppermute(give, 'core', [(i, nc - 1 - i) for i in range(nc)])  7.63 us
    all_to_all x1, starting transfers between devices, per_device(): lax.all_to_all(spread, 'x', 0, 0, tiled=True).reshape(nx * toks, wide)  6.25 us
  transfers between devices with their start and end apart: 6, of which 3 were waited for; matrix products, arithmetic and copies ran while one was open for 7% of the time, Pallas kernels for 0%

profile of v3, /device:TPU:1, one launch (start us, length us, event | category | flops | bytes accessed | tf_op | source)
XLA Modules:
  0.0 165.5 jit_solution(14037195327582777075)
XLA Ops:
  6.6 1.1 reshape.191
  7.7 0.9 broadcast_in_dim.104
  8.6 10.5 %all-to-all-start.4 = ((bf16[32,2,32,128]{3,2,1,0:T(8,128)(2,1)}), bf16[32,2,32,128]{3,2,1,0:T(8,128)(2,1)S(1)}, u32[]{:S(2)}, u32[]{:S(2)}) async-start(bf16[32,2,32,128]{3,2,1,0:T(8,128)(2,1)} %broadcast_in_dim.104), calls=%async_computation.4 | async-start | bytes 1048576 | tf_op jit(solution)/shard_map/all_to_all | solution.py:149
  19.1 10.6 %collective-permute-start = (bf16[56,1024]{1,0:T(8,128)(2,1)S(1)}, bf16[56,1024]{1,0:T(8,128)(2,1)S(1)}, u32[]{:S(2)}, u32[]{:S(2)}) collective-permute-start(bf16[56,1024]{1,0:T(8,128)(2,1)S(1)} %bitcast.59), channel_id=1, source_target_pairs={{0,8},{8,0},{1,9},{9,1},{2,10},{10,2},{3,11},{11,3},{4,12},{12,4},... | collective-permute-start | bytes 344072 | tf_op jit(solution)/shard_map/ppermute | solution.py:143
  31.3 1.4 select_reduce_fusion.4
  33.4 69.9 %conditional.1 = (bf16[128,1024]{1,0:T(8,128)(2,1)S(1)}, bf16[896,1024]{1,0:T(8,128)(2,1)}) conditional(s32[]{:T(128)} %convert_element_type.51, (s32[]{:T(128)}, s32[128]{0:T(128)S(1)}, s32[8192]{0:T(1024)S(1)}, s32[]{:T(128)}, bf16[56,1024]{1,0:T(8,128)(2,1)S(1)}, /*index=5*/bf16[56,1024]{1,0:T(8,128)(2,1)S(1)}, ...), branch_computations={%region_4.7_spmd, %region_7.11_spmd} | conditional | flops 29252344 | bytes 76820368 | solution.py:195
  33.5 0.7 fusion.11
  35.1 0.9 reshape.180
  36.2 29.0 %all_to_all.32 = bf16[8,56,1024]{2,1,0:T(8,128)(2,1)} all-to-all(bf16[8,56,1024]{2,1,0:T(8,128)(2,1)S(1)} %broadcast_in_dim.70), channel_id=1, replica_groups=mesh['x'=4,'y'=8,'zh'=2,'zl'=4,'core'=2] {'y'}, dimensions={0} | all-to-all | bytes 1835008 | tf_op jit(solution)/shard_map/cond/branch_1_fun/all_to_all | solution.py:160
  65.2 1.1 broadcast_in_dim.71
  66.3 4.2 %all-to-all-start.3 = ((bf16[8,56,1024]{2,1,0:T(8,128)(2,1)}), bf16[8,56,1024]{2,1,0:T(8,128)(2,1)}, u32[]{:S(2)}, u32[]{:S(2)}) async-start(bf16[8,56,1024]{2,1,0:T(8,128)(2,1)} %broadcast_in_dim.71), calls=%async_computation.3 | async-start | bytes 1835008 | tf_op jit(solution)/shard_map/cond/branch_1_fun/all_to_all | solution.py:160
  73.9 0.7 fusion.12
  75.1 18.1 %all-to-all-done.3 = bf16[8,56,1024]{2,1,0:T(8,128)(2,1)} async-done(((bf16[8,56,1024]{2,1,0:T(8,128)(2,1)}), bf16[8,56,1024]{2,1,0:T(8,128)(2,1)}, u32[]{:S(2)}, u32[]{:S(2)}) %all-to-all-start.3) | async-done | bytes 917536 | tf_op jit(solution)/shard_map/cond/branch_1_fun/all_to_all | solution.py:160
  93.2 3.7 %maximum_select_fusion.1 = bf16[8,2,56,1024]{3,2,1,0:T(8,128)(2,1)} fusion(bf16[8,1,56,1024]{3,2,1,0:T(8,128)(2,1)} %bitcast.12, bf16[8,1,56,1024]{3,2,1,0:T(8,128)(2,1)} %bitcast.52, pred[]{:T(512)S(6)} %eq.44), kind=kLoop, calls=%fused_computation.27 | loop fusion | flops 2752512 | bytes 3670017 | tf_op jit(solution)/shard_map/cond/branch_1_fun/jit(_where)/select_n | solution.py:177
  97.0 2.6 %copy-done.1 = bf16[22528,128]{1,0:T(8,128)(2,1)S(1)} copy-done((bf16[22528,128]{1,0:T(8,128)(2,1)S(1)}, bf16[22528,128]{1,0:T(8,128)(2,1)}, u32[]{:S(2)}) %copy-start.1) | copy-done | bytes 5767192 | tf_op jit(solution)/shard_map/cond
  99.7 3.6 %latent_attention.3 = bf16[128,1024]{1,0:T(8,128)(2,1)S(1)} custom-call(s32[132]{0:T(256)S(1)} %pad_add_fusion.2.scal, s32[8,128,1]{2,1,0:T(8,128)S(1)} %broadcast_in_dim.72.lo_ref, bf16[8,128,512]{2,1,0:T(8,128)(2,1)S(1)} %bitcast.48, bf16[8,512,128]{2,1,0:T(8,128)(2,1)S(1)} %pad.6.vup_ref, bf16[704,32,128]{2,1,0:T(8,128)(2,1)S(1)} %bitcast.47), custom_call_target="tpu_custom_call" | custom-call | tf_op jit(solution)/shard_map/cond/branch_1_fun/latent_attention/pallas_call | solution.py:78
  103.3 1.1 broadcast_in_dim.105
  104.4 6.2 %all-to-all-start.5 = ((bf16[4,128,1024]{2,1,0:T(8,128)(2,1)}), bf16[4,128,1024]{2,1,0:T(8,128)(2,1)S(1)}, u32[]{:S(2)}, u32[]{:S(2)}) async-start(bf16[4,128,1024]{2,1,0:T(8,128)(2,1)} %broadcast_in_dim.105), calls=%async_computation.5 | async-start | bytes 2097152 | tf_op jit(solution)/shard_map/all_to_all | solution.py:204
  110.7 10.3 %all-to-all-done.5 = bf16[4,128,1024]{2,1,0:T(8,128)(2,1)S(1)} async-done(((bf16[4,128,1024]{2,1,0:T(8,128)(2,1)}), bf16[4,128,1024]{2,1,0:T(8,128)(2,1)S(1)}, u32[]{:S(2)}, u32[]{:S(2)}) %all-to-all-start.5) | async-done | bytes 1048608 | tf_op jit(solution)/shard_map/all_to_all | solution.py:204
  121.0 2.8 %convolution_convert_fusion.1 = bf16[512,896]{1,0:T(8,128)(2,1)S(1)} fusion(bf16[512,1024]{1,0:T(8,128)(2,1)S(1)} %bitcast.54, bf16[896,1024]{1,0:T(8,128)(2,1)} %get-tuple-element.116), kind=kOutput, calls=%fused_computation.62 | convolution fusion | flops 939982848 | bytes 3801088 | tf_op jit(solution)/shard_map/dot_general | solution.py:205
  123.8 7.6 %collective-permute-start.1 = (bf16[16,16,896]{2,1,0:T(8,128)(2,1)S(1)}, bf16[16,16,896]{2,1,0:T(8,128)(2,1)S(1)}, u32[]{:S(2)}, u32[]{:S(2)}) collective-permute-start(bf16[16,16,896]{2,1,0:T(8,128)(2,1)S(1)} %dynamic-slice_bitcast_fusion), channel_id=1, source_target_pairs={{0,1},{1,0},{2,3},{3,2},{4,5},{5,4},{6,7},{7,6},{8,9},{9,8},{10,11... | collective-permute-start | bytes 1376264 | tf_op jit(solution)/shard_map/ppermute | solution.py:213
  131.5 1.4 collective-permute-done.1
  133.0 24.9 %all_to_all.33 = bf16[16,16,896]{2,1,0:T(8,128)(2,1)S(1)} all-to-all(bf16[16,16,896]{2,1,0:T(8,128)(2,1)S(1)} %fusion.13), channel_id=1, replica_groups=mesh['x'=4,'y'=8,'zh'=2,'zl'=4,'core'=2] {'x','zl'}, dimensions={0} | all-to-all | bytes 917504 | tf_op jit(solution)/shard_map/all_to_all | solution.py:215
  158.0 0.7 copy.28
  (65 shorter events, 5.4 us)
Async XLA Ops:
  6.5 12.6 %copy-start.8 = (bf16[1024,56]{0,1:T(8,128)(2,1)S(1)}, bf16[1024,56]{0,1:T(8,128)(2,1)}, u32[]{:S(2)}) copy-start(bf16[1024,56]{0,1:T(8,128)(2,1)} %param.13) | copy-start | bytes 344068
  6.5 23.2 %copy-start.5 = (s32[8192]{0:T(1024)S(1)}, s32[8192]{0:T(1024)}, u32[]{:S(2)}) copy-start(s32[8192]{0:T(1024)} %param.10) | copy-start | bytes 98308
  6.5 23.3 %copy-start.13 = (s32[128]{0:T(128)S(1)}, s32[128]{0:T(128)}, u32[]{:S(2)}) copy-start(s32[128]{0:T(128)} %param.11) | copy-start | bytes 1540
  6.5 26.9 %copy-start.4 = (bf16[8,448,128]{2,1,0:T(8,128)(2,1)S(1)}, bf16[8,448,128]{2,1,0:T(8,128)(2,1)}, u32[]{:S(2)}) copy-start(bf16[8,448,128]{2,1,0:T(8,128)(2,1)} %param.12) | copy-start | bytes 2752516
  6.5 26.9 %copy-start.3 = (bf16[128,8,512]{2,1,0:T(8,128)(2,1)S(1)}, bf16[128,8,512]{2,1,0:T(8,128)(2,1)}, u32[]{:S(2)}) copy-start(bf16[128,8,512]{2,1,0:T(8,128)(2,1)} %param.8) | copy-start | bytes 3145732
  8.6 24.8 %all-to-all-start.4 = ((bf16[32,2,32,128]{3,2,1,0:T(8,128)(2,1)}), bf16[32,2,32,128]{3,2,1,0:T(8,128)(2,1)S(1)}, u32[]{:S(2)}, u32[]{:S(2)}) async-start(bf16[32,2,32,128]{3,2,1,0:T(8,128)(2,1)} %broadcast_in_dim.104), calls=%async_computation.4 | async-start | bytes 1048576 | tf_op jit(solution)/shard_map/all_to_all | solution.py:149
  19.1 14.3 %collective-permute-start = (bf16[56,1024]{1,0:T(8,128)(2,1)S(1)}, bf16[56,1024]{1,0:T(8,128)(2,1)S(1)}, u32[]{:S(2)}, u32[]{:S(2)}) collective-permute-start(bf16[56,1024]{1,0:T(8,128)(2,1)S(1)} %bitcast.59), channel_id=1, source_target_pairs={{0,8},{8,0},{1,9},{9,1},{2,10},{10,2},{3,11},{11,3},{4,12},{12,4},... | collective-permute-start | bytes 344072 | tf_op jit(solution)/shard_map/ppermute | solution.py:143
  33.4 1.4 copy-start.6
  33.4 1.4 copy-start.9
  33.4 1.4 copy-start.11
  33.5 63.5 %all-gather.5.cloned.1.call-start = ((), (), s32[]{:S(2)}) async-start(), calls=%async_computation.8 | async-start | bytes 6127616 | tf_op jit(solution)/shard_map/cond/branch_1_fun/all_gather | solution.py:171
  34.8 1.3 copy-start.10
  35.1 30.1 %copy-start.12 = (bf16[56,1024]{1,0:T(8,128)(2,1)S(1)}, bf16[56,1024]{1,0:T(8,128)(2,1)}, u32[]{:S(2)}) copy-start(bf16[56,1024]{1,0:T(8,128)(2,1)} %copy-done.11) | copy-start | bytes 344068 | tf_op jit(solution)/shard_map/cond
  65.2 7.4 %copy-start.7 = (s32[8192]{0:T(1024)S(1)}, s32[8192]{0:T(1024)}, u32[]{:S(2)}) copy-start(s32[8192]{0:T(1024)} %copy-done.6) | copy-start | bytes 98308 | tf_op jit(solution)/shard_map/cond
  66.3 26.9 %all-to-all-start.3 = ((bf16[8,56,1024]{2,1,0:T(8,128)(2,1)}), bf16[8,56,1024]{2,1,0:T(8,128)(2,1)}, u32[]{:S(2)}, u32[]{:S(2)}) async-start(bf16[8,56,1024]{2,1,0:T(8,128)(2,1)} %broadcast_in_dim.71), calls=%async_computation.3 | async-start | bytes 1835008 | tf_op jit(solution)/shard_map/cond/branch_1_fun/all_to_all | solution.py:160
  97.0 2.6 %copy-start.1 = (bf16[22528,128]{1,0:T(8,128)(2,1)S(1)}, bf16[22528,128]{1,0:T(8,128)(2,1)}, u32[]{:S(2)}) copy-start(bf16[22528,128]{1,0:T(8,128)(2,1)} %all-gather.5.cloned.1.call-done) | copy-start | bytes 17301508 | tf_op jit(solution)/shard_map/cond
  104.4 16.6 %all-to-all-start.5 = ((bf16[4,128,1024]{2,1,0:T(8,128)(2,1)}), bf16[4,128,1024]{2,1,0:T(8,128)(2,1)S(1)}, u32[]{:S(2)}, u32[]{:S(2)}) async-start(bf16[4,128,1024]{2,1,0:T(8,128)(2,1)} %broadcast_in_dim.105), calls=%async_computation.5 | async-start | bytes 2097152 | tf_op jit(solution)/shard_map/all_to_all | solution.py:204
  123.8 9.1 %collective-permute-start.1 = (bf16[16,16,896]{2,1,0:T(8,128)(2,1)S(1)}, bf16[16,16,896]{2,1,0:T(8,128)(2,1)S(1)}, u32[]{:S(2)}, u32[]{:S(2)}) collective-permute-start(bf16[16,16,896]{2,1,0:T(8,128)(2,1)S(1)} %dynamic-slice_bitcast_fusion), channel_id=1, source_target_pairs={{0,1},{1,0},{2,3},{3,2},{4,5},{5,4},{6,7},{7,6},{8,9},{9,8},{10,11... | collective-permute-start | bytes 1376264 | tf_op jit(solution)/shard_map/ppermute | solution.py:213
Sparse Core Ops, SparseCore 0:
  36.4 51.5 all-gather.4

commit v4 on v3

--- a/solution.py
+++ b/solution.py
@@ -66,18 +66,18 @@
 
     vh = vup_ref.shape[2]
     for h in range(heads):
-        out_ref[:, h * vh : (h + 1) * vh] = jnp.dot(
-            done[h], vup_ref[h], preferred_element_type=jnp.float32
-        ).astype(jnp.bfloat16)
-
-
-def attention(scal, lo, q, vup, lat):
+        values = jnp.dot(done[h], vup_ref[h], preferred_element_type=jnp.float32).astype(jnp.bfloat16)
+        for copy in range(out_ref.shape[0]):
+            out_ref[copy, :, h * vh : (h + 1) * vh] = values
+
+
+def attention(scal, lo, q, vup, lat, copies):
     heads, toks, width = q.shape
     vh = vup.shape[2]
     vmem = pl.BlockSpec(memory_space=pltpu.VMEM)
     return pl.pallas_call(
         attention_kernel,
-        out_shape=jax.ShapeDtypeStruct((toks, heads * vh), jnp.bfloat16),
+        out_shape=jax.ShapeDtypeStruct((copies, toks, heads * vh), jnp.bfloat16),
         in_specs=[pl.BlockSpec(memory_space=pltpu.SMEM)] + [vmem] * 4,
         out_specs=vmem,
         scratch_shapes=[
@@ -86,6 +86,9 @@
             pltpu.VMEM((heads, toks, width), jnp.bfloat16),
         ],
         compiler_params=pltpu.CompilerParams(vmem_limit_bytes=40 * 2**20),
+        cost_estimate=pl.CostEstimate(
+            flops=6 * 2**30, bytes_accessed=2 * lat.size, transcendentals=2**21
+        ),
         name="latent_attention",
     )(scal, lo, q, vup, lat)
 
@@ -142,9 +145,9 @@
     cols = out_proj.T
     other = lax.ppermute(cols, "zh", [(i, nzh - 1 - i) for i in range(nzh)])
 
-    part = latent.reshape(halves, BLK // ROWS, ROWS, across, LANES).transpose(1, 3, 0, 2, 4)
-    part = part.reshape(PARTS, halves, ROWS, LANES)
-    part = lax.dynamic_index_in_dim(part, zl * nc + core, 0, keepdims=False)
+    number = zl * nc + core
+    corner = (0, number // across * ROWS, number % across * LANES)
+    part = lax.dynamic_slice(latent.reshape(halves, BLK, width), corner, (halves, ROWS, LANES))
     spread = jnp.broadcast_to(part[None], (plane,) + part.shape)
     plane_rows = lax.all_to_all(spread, ("x", "y"), 0, 0, tiled=True)
     plane_rows = plane_rows.reshape(slices, ROWS * LANES)
@@ -155,15 +158,16 @@
     row_need = lax.dynamic_index_in_dim(my_need.reshape(plane, nzh, halves), zh, 1, keepdims=False)
     row_rank = lax.dynamic_index_in_dim(my_rank.reshape(plane, nzh, halves), zh, 1, keepdims=False)
     row_rank = jnp.where(row_need, row_rank, -1).reshape(1, slices)
+    pick = (row_rank == jnp.arange(FEW, dtype=jnp.int32)[:, None]).astype(jnp.bfloat16)
+    pick, my_rank = lax.optimization_barrier((pick, my_rank))
 
     def over_y(piece):
         return lax.all_to_all(jnp.broadcast_to(piece[None], (ny,) + piece.shape), "y", 0, 0, tiled=True)
 
     def attend(few, operands):
-        plane_rows, cols, other, query, segment_ids, block_of_slot, value_up, my_rank, row_rank = operands
+        plane_rows, cols, other, query, segment_ids, block_of_slot, value_up, my_rank, pick = operands
         if few:
             kept = FEW
-            pick = (row_rank == jnp.arange(kept, dtype=jnp.int32)[:, None]).astype(jnp.bfloat16)
             sent = jnp.dot(pick, plane_rows, preferred_element_type=jnp.float32).astype(jnp.bfloat16)
         else:
             kept = slices
@@ -174,8 +178,6 @@
         cols, other, sent = lax.optimization_barrier((cols, other, sent))
         mine = over_y(cols)
         theirs = over_y(other)
-        columns = jnp.where(zh == 0, jnp.stack([mine, theirs], 1), jnp.stack([theirs, mine], 1))
-        columns = columns.reshape(-1, cols.shape[1])
 
         my_blocks, first, slot_of_block, lo_rows, q, vup = prepare(
             query, segment_ids, block_of_slot, value_up, seq_index
@@ -189,19 +191,19 @@
             place = slot_seq // nzh * halves + slot_half
         start = (slot_seq % nzh) * PARTS * kept + place
         scal = jnp.concatenate([my_blocks, first, start]).astype(jnp.int32)
-        scal, columns = lax.optimization_barrier((scal, columns))
-        return attention(scal, lo_rows, q, vup, gathered), columns
-
-    head_values, columns = lax.cond(
+        return attention(scal, lo_rows, q, vup, gathered, nx), mine, theirs
+
+    head_values, mine, theirs = lax.cond(
         fits,
         functools.partial(attend, True),
         functools.partial(attend, False),
-        (plane_rows, cols, other, query, segment_ids, block_of_slot, value_up, my_rank, row_rank),
-    )
-
-    wide = head_values.shape[1]
-    spread = jnp.broadcast_to(head_values[None], (nx, toks, wide))
-    rows = lax.all_to_all(spread, "x", 0, 0, tiled=True).reshape(nx * toks, wide)
+        (plane_rows, cols, other, query, segment_ids, block_of_slot, value_up, my_rank, pick),
+    )
+
+    wide = head_values.shape[2]
+    rows = lax.all_to_all(head_values, "x", 0, 0, tiled=True).reshape(nx * toks, wide)
+    columns = jnp.where(zh == 0, jnp.stack([mine, theirs], 1), jnp.stack([theirs, mine], 1))
+    columns = columns.reshape(-1, cols.shape[1])
     partial_value = lax.dot_general(
         rows, columns, (((1,), (1,)), ((), ())), preferred_element_type=jnp.float32
     ).astype(jnp.bfloat16)

time: 166 us -> 159 us (0.958)
  blocking collectives: 53.9 us -> 18.5 us
  waiting for transfers between devices: 29.9 us -> 50.7 us
  Pallas kernels: 3.64 us -> 9.28 us
  starting transfers between devices: 39.3 us -> 43.5 us
  other arithmetic: 7.39 us -> 5.02 us
    all_to_all x1 -> x0, blocking collectives: 29 us -> none  [over_y(): lax.all_to_all(jnp.broadcast_to(piece[None], (ny,) + piece.shape), 'y', 0...]
    all_gather x1, waiting for transfers between devices: 0.01 us -> 13.7 us  [attend(): lax.all_gather(sent.reshape(kept * ROWS, LANES), ('zh', 'zl', 'core'), ax...]
    all_to_all x1 -> x2, starting transfers between devices: 4.23 us -> 10.7 us  [over_y(): lax.all_to_all(jnp.broadcast_to(piece[None], (ny,) + piece.shape), 'y', 0...]
    all_to_all x1, blocking collectives: 24.9 us -> 18.5 us  [per_device(): terms = lax.all_to_all(chip, ('x', 'zl'), 0, 0, tiled=True)]
    pallas_call x1, Pallas kernels: 3.64 us -> 9.28 us  [attention(): pl.pallas_call(attention_kernel, out_shape=jax.ShapeDtypeStruct((copies,...]
    all_to_all x1 -> x2, waiting for transfers between devices: 18.1 us -> 22.5 us  [over_y(): lax.all_to_all(jnp.broadcast_to(piece[None], (ny,) + piece.shape), 'y', 0...]
    ppermute x1, starting transfers between devices: 7.63 us -> 3.3 us  [per_device(): got = lax.ppermute(give, 'core', [(i, nc - 1 - i) for i in range(nc)])]
    all_to_all x1, waiting for transfers between devices: 10.3 us -> 13.1 us  [per_device(): lax.all_to_all(head_values, 'x', 0, 0, tiled=True).reshape(nx * toks, wide)]
  transfers between devices with their start and end apart: 6 -> 7, of which waited for: 3 -> 4; matrix products, arithmetic and copies ran while one was open for 7% -> 6% of each run, Pallas kernels for 0% -> 6%
where the time goes in v4:
time: 159 us; the launch traced here: 158 us
  waiting for transfers between devices  50.7 us (32%)
  starting transfers between devices  43.5 us (27%)
  blocking collectives  18.5 us (12%)
  between operations  14.3 us (9%)
  local copies, waits for them, and re-layouts  11.5 us (7%)
  Pallas kernels  9.28 us (6%)
  other arithmetic  5.02 us (3%)
  matrix products  3.61 us (2%)
    all_to_all x2, waiting for transfers between devices, over_y(): lax.all_to_all(jnp.broadcast_to(piece[None], (ny,) + piece.shape), 'y', 0...  22.5 us
    all_to_all x1, blocking collectives, per_device(): terms = lax.all_to_all(chip, ('x', 'zl'), 0, 0, tiled=True)  18.5 us
    all_gather x1, waiting for transfers between devices, attend(): lax.all_gather(sent.reshape(kept * ROWS, LANES), ('zh', 'zl', 'core'), ax...  13.7 us
    all_to_all x1, waiting for transfers between devices, per_device(): lax.all_to_all(head_values, 'x', 0, 0, tiled=True).reshape(nx * toks, wide)  13.1 us
    all_to_all x2, starting transfers between devices, over_y(): lax.all_to_all(jnp.broadcast_to(piece[None], (ny,) + piece.shape), 'y', 0...  10.7 us
    ppermute x1, starting transfers between devices, per_device(): other = lax.ppermute(cols, 'zh', [(i, nzh - 1 - i) for i in range(nzh)])  10.6 us
    all_to_all x1, starting transfers between devices, per_device(): plane_rows = lax.all_to_all(spread, ('x', 'y'), 0, 0, tiled=True)  10.5 us
    pallas_call x1, Pallas kernels, attention(): pl.pallas_call(attention_kernel, out_shape=jax.ShapeDtypeStruct((copies,...  9.28 us
  transfers between devices with their start and end apart: 7, of which 4 were waited for; matrix products, arithmetic and copies ran while one was open for 6% of the time, Pallas kernels for 6%

profile of v4, /device:TPU:1, one launch (start us, length us, event | category | flops | bytes accessed | tf_op | source)
XLA Modules:
  0.0 157.8 jit_solution(17553781192464791637)
XLA Ops:
  6.6 0.9 copy-done
  7.5 0.9 broadcast_in_dim.78
  8.4 10.5 %all-to-all-start.4 = ((bf16[32,2,32,128]{3,2,1,0:T(8,128)(2,1)}), bf16[32,2,32,128]{3,2,1,0:T(8,128)(2,1)S(1)}, u32[]{:S(2)}, u32[]{:S(2)}) async-start(bf16[32,2,32,128]{3,2,1,0:T(8,128)(2,1)} %broadcast_in_dim.78), calls=%async_computation.4 | async-start | bytes 1048576 | tf_op jit(solution)/shard_map/all_to_all | solution.py:152
  18.9 10.6 %collective-permute-start = (bf16[56,1024]{1,0:T(8,128)(2,1)}, bf16[56,1024]{1,0:T(8,128)(2,1)S(1)}, u32[]{:S(2)}, u32[]{:S(2)}) collective-permute-start(bf16[56,1024]{1,0:T(8,128)(2,1)} %bitcast.61), channel_id=1, source_target_pairs={{0,8},{8,0},{1,9},{9,1},{2,10},{10,2},{3,11},{11,3},{4,12},{12,4},... | collective-permute-start | bytes 344072 | tf_op jit(solution)/shard_map/ppermute | solution.py:146
  29.5 0.8 reshape.186
  31.9 0.8 select_reduce_fusion.4
  34.0 66.2 %conditional.1 = (bf16[4,128,1024]{2,1,0:T(8,128)(2,1)}, bf16[8,1,56,1024]{3,2,0,1:T(8,128)(2,1)}, bf16[8,1,56,1024]{3,2,0,1:T(8,128)(2,1)}) conditional(s32[]{:T(128)} %convert_element_type.51, (s32[]{:T(128)}, s32[128]{0:T(128)S(1)}, s32[8192]{0:T(1024)S(1)}, bf16[128,8,512]{2,1,0:T(8,128)(2,1)S(1)}, bf16[8,448,128]{2,1,0:T(8,128)(2,1)S(1)}, ...), branch_computations={%region_4.7_spmd, %region_7.11_spmd} | conditional | flops 6468947456 | bytes 86126544 | solution.py:196
  34.3 0.9 reshape.176
  35.3 1.0 broadcast_in_dim.68
  36.3 6.4 %all-to-all-start.2 = ((bf16[8,56,1024]{2,1,0:T(8,128)(2,1)}), bf16[8,56,1024]{2,1,0:T(8,128)(2,1)S(1)}, u32[]{:S(2)}, u32[]{:S(2)}) async-start(bf16[8,56,1024]{2,1,0:T(8,128)(2,1)} %broadcast_in_dim.68), calls=%async_computation.2 | async-start | bytes 1835008 | tf_op jit(solution)/shard_map/cond/branch_1_fun/all_to_all | solution.py:165
  44.9 22.5 %all-to-all-done.2 = bf16[8,56,1024]{2,1,0:T(8,128)(2,1)S(1)} async-done(((bf16[8,56,1024]{2,1,0:T(8,128)(2,1)}), bf16[8,56,1024]{2,1,0:T(8,128)(2,1)S(1)}, u32[]{:S(2)}, u32[]{:S(2)}) %all-to-all-start.2) | async-done | bytes 917536 | tf_op jit(solution)/shard_map/cond/branch_1_fun/all_to_all | solution.py:165
  67.4 1.2 broadcast_in_dim.69
  68.5 4.2 %all-to-all-start.3 = ((bf16[8,56,1024]{2,1,0:T(8,128)(2,1)}), bf16[8,56,1024]{2,1,0:T(8,128)(2,1)}, u32[]{:S(2)}, u32[]{:S(2)}) async-start(bf16[8,56,1024]{2,1,0:T(8,128)(2,1)} %broadcast_in_dim.69), calls=%async_computation.3 | async-start | bytes 1835008 | tf_op jit(solution)/shard_map/cond/branch_1_fun/all_to_all | solution.py:165
  74.4 13.7 %all-gather.5.cloned.1.call-done = bf16[22528,128]{1,0:T(8,128)(2,1)} async-done(((bf16[1408,128]{1,0:T(8,128)(2,1)}), bf16[22528,128]{1,0:T(8,128)(2,1)}) %all-gather.5.cloned.1.call-update) | async-done | bytes 5767184 | tf_op jit(solution)/shard_map/cond/branch_1_fun/all_gather | solution.py:175
  88.2 2.6 %copy-done.2 = bf16[22528,128]{1,0:T(8,128)(2,1)S(1)} copy-done((bf16[22528,128]{1,0:T(8,128)(2,1)S(1)}, bf16[22528,128]{1,0:T(8,128)(2,1)}, u32[]{:S(2)}) %copy-start.2) | copy-done | bytes 5767192 | tf_op jit(solution)/shard_map/cond
  90.9 9.3 %latent_attention.3 = bf16[4,128,1024]{2,1,0:T(8,128)(2,1)} custom-call(s32[132]{0:T(256)S(1)} %pad_add_fusion.2.scal, s32[8,128,1]{2,1,0:T(8,128)S(1)} %broadcast_in_dim.67.lo_ref, bf16[8,128,512]{2,1,0:T(8,128)(2,1)S(1)} %bitcast.48, bf16[8,512,128]{2,1,0:T(8,128)(2,1)S(1)} %pad.6.vup_ref, bf16[704,32,128]{2,1,0:T(8,128)(2,1)S(1)} %bitcast.51), custom_call_target="tpu_custom_call" | custom-call | flops 6442450944 | bytes 5767168 | tf_op jit(solution)/shard_map/cond/branch_1_fun/latent_attention/pallas_call | solution.py:78
  100.2 8.4 %all-to-all-start.5 = ((bf16[4,128,1024]{2,1,0:T(8,128)(2,1)}), bf16[4,128,1024]{2,1,0:T(8,128)(2,1)}, u32[]{:S(2)}, u32[]{:S(2)}) async-start(bf16[4,128,1024]{2,1,0:T(8,128)(2,1)} %get-tuple-element.73), calls=%async_computation.5 | async-start | bytes 2097152 | tf_op jit(solution)/shard_map/all_to_all | solution.py:204
  108.6 1.7 %maximum_select_fusion = bf16[8,2,56,1024]{3,2,1,0:T(8,128)(2,1)S(1)} fusion(bf16[8,1,56,1024]{3,2,1,0:T(8,128)(2,1)} %bitcast.18, bf16[8,1,56,1024]{3,2,1,0:T(8,128)(2,1)S(1)} %bitcast.56, pred[]{:T(512)S(6)} %eq.104), kind=kLoop, calls=%fused_computation.51 | loop fusion | flops 2752512 | bytes 3670017 | tf_op jit(solution)/shard_map/jit(_where)/select_n | solution.py:205
  110.2 13.1 %all-to-all-done.5 = bf16[4,128,1024]{2,1,0:T(8,128)(2,1)} async-done(((bf16[4,128,1024]{2,1,0:T(8,128)(2,1)}), bf16[4,128,1024]{2,1,0:T(8,128)(2,1)}, u32[]{:S(2)}, u32[]{:S(2)}) %all-to-all-start.5) | async-done | bytes 1048608 | tf_op jit(solution)/shard_map/all_to_all | solution.py:204
  123.3 2.5 %convolution_convert_fusion.1 = bf16[512,896]{1,0:T(8,128)(2,1)S(1)} fusion(bf16[512,1024]{1,0:T(8,128)(2,1)} %bitcast.16, bf16[896,1024]{1,0:T(8,128)(2,1)S(1)} %bitcast.57), kind=kOutput, calls=%fused_computation.52 | convolution fusion | flops 939982848 | bytes 3801088 | tf_op jit(solution)/shard_map/dot_general | solution.py:207
  125.9 3.3 %collective-permute-start.1 = (bf16[16,16,896]{2,1,0:T(8,128)(2,1)S(1)}, bf16[16,16,896]{2,1,0:T(8,128)(2,1)S(1)}, u32[]{:S(2)}, u32[]{:S(2)}) collective-permute-start(bf16[16,16,896]{2,1,0:T(8,128)(2,1)S(1)} %dynamic-slice_bitcast_fusion), channel_id=1, source_target_pairs={{0,1},{1,0},{2,3},{3,2},{4,5},{5,4},{6,7},{7,6},{8,9},{9,8},{10,11... | collective-permute-start | bytes 1376264 | tf_op jit(solution)/shard_map/ppermute | solution.py:215
  129.2 1.4 collective-permute-done.1
  130.6 1.1 fusion.8
  131.8 18.5 %all_to_all.31 = bf16[16,16,896]{2,1,0:T(8,128)(2,1)S(1)} all-to-all(bf16[16,16,896]{2,1,0:T(8,128)(2,1)S(1)} %fusion.8), channel_id=1, replica_groups=mesh['x'=4,'y'=8,'zh'=2,'zl'=4,'core'=2] {'x','zl'}, dimensions={0} | all-to-all | bytes 917504 | tf_op jit(solution)/shard_map/all_to_all | solution.py:217
  (60 shorter events, 5.7 us)
Async XLA Ops:
  6.5 0.9 copy-start
  6.5 27.4 %copy-start.11 = (bf16[1024,56]{0,1:T(8,128)(2,1)S(1)}, bf16[1024,56]{0,1:T(8,128)(2,1)}, u32[]{:S(2)}) copy-start(bf16[1024,56]{0,1:T(8,128)(2,1)} %param.13) | copy-start | bytes 344068
  6.5 24.0 %copy-start.10 = (s32[8192]{0:T(1024)S(1)}, s32[8192]{0:T(1024)}, u32[]{:S(2)}) copy-start(s32[8192]{0:T(1024)} %param.10) | copy-start | bytes 98308
  6.5 24.6 %copy-start.12 = (s32[128]{0:T(128)S(1)}, s32[128]{0:T(128)}, u32[]{:S(2)}) copy-start(s32[128]{0:T(128)} %param.11) | copy-start | bytes 1540
  6.5 27.4 %copy-start.5 = (bf16[8,448,128]{2,1,0:T(8,128)(2,1)S(1)}, bf16[8,448,128]{2,1,0:T(8,128)(2,1)}, u32[]{:S(2)}) copy-start(bf16[8,448,128]{2,1,0:T(8,128)(2,1)} %param.12) | copy-start | bytes 2752516
  6.5 27.4 %copy-start.4 = (bf16[128,8,512]{2,1,0:T(8,128)(2,1)S(1)}, bf16[128,8,512]{2,1,0:T(8,128)(2,1)}, u32[]{:S(2)}) copy-start(bf16[128,8,512]{2,1,0:T(8,128)(2,1)} %param.8) | copy-start | bytes 3145732
  8.4 25.5 %all-to-all-start.4 = ((bf16[32,2,32,128]{3,2,1,0:T(8,128)(2,1)}), bf16[32,2,32,128]{3,2,1,0:T(8,128)(2,1)S(1)}, u32[]{:S(2)}, u32[]{:S(2)}) async-start(bf16[32,2,32,128]{3,2,1,0:T(8,128)(2,1)} %broadcast_in_dim.78), calls=%async_computation.4 | async-start | bytes 1048576 | tf_op jit(solution)/shard_map/all_to_all | solution.py:152
  18.9 15.0 %collective-permute-start = (bf16[56,1024]{1,0:T(8,128)(2,1)}, bf16[56,1024]{1,0:T(8,128)(2,1)S(1)}, u32[]{:S(2)}, u32[]{:S(2)}) collective-permute-start(bf16[56,1024]{1,0:T(8,128)(2,1)} %bitcast.61), channel_id=1, source_target_pairs={{0,8},{8,0},{1,9},{9,1},{2,10},{10,2},{3,11},{11,3},{4,12},{12,4},... | collective-permute-start | bytes 344072 | tf_op jit(solution)/shard_map/ppermute | solution.py:146
  34.0 54.1 %all-gather.5.cloned.1.call-start = ((), (), s32[]{:S(2)}) async-start(), calls=%async_computation.8 | async-start | bytes 6127616 | tf_op jit(solution)/shard_map/cond/branch_1_fun/all_gather | solution.py:175
  36.3 31.0 %all-to-all-start.2 = ((bf16[8,56,1024]{2,1,0:T(8,128)(2,1)}), bf16[8,56,1024]{2,1,0:T(8,128)(2,1)S(1)}, u32[]{:S(2)}, u32[]{:S(2)}) async-start(bf16[8,56,1024]{2,1,0:T(8,128)(2,1)} %broadcast_in_dim.68), calls=%async_computation.2 | async-start | bytes 1835008 | tf_op jit(solution)/shard_map/cond/branch_1_fun/all_to_all | solution.py:165
  67.4 6.1 %copy-start.7 = (bf16[8,56,1024]{2,1,0:T(8,128)(2,1)}, bf16[8,56,1024]{2,1,0:T(8,128)(2,1)S(1)}, u32[]{:S(2)}) copy-start(bf16[8,56,1024]{2,1,0:T(8,128)(2,1)S(1)} %all-to-all-done.2) | copy-start | bytes 2752516 | tf_op jit(solution)/shard_map/cond
  68.5 31.6 %all-to-all-start.3 = ((bf16[8,56,1024]{2,1,0:T(8,128)(2,1)}), bf16[8,56,1024]{2,1,0:T(8,128)(2,1)}, u32[]{:S(2)}, u32[]{:S(2)}) async-start(bf16[8,56,1024]{2,1,0:T(8,128)(2,1)} %broadcast_in_dim.69), calls=%async_computation.3 | async-start | bytes 1835008 | tf_op jit(solution)/shard_map/cond/branch_1_fun/all_to_all | solution.py:165
  88.2 2.6 %copy-start.2 = (bf16[22528,128]{1,0:T(8,128)(2,1)S(1)}, bf16[22528,128]{1,0:T(8,128)(2,1)}, u32[]{:S(2)}) copy-start(bf16[22528,128]{1,0:T(8,128)(2,1)} %all-gather.5.cloned.1.call-done) | copy-start | bytes 17301508 | tf_op jit(solution)/shard_map/cond
  100.2 8.4 %copy-start.8 = (bf16[8,1,56,1024]{3,2,0,1:T(8,128)(2,1)S(1)}, bf16[8,1,56,1024]{3,2,0,1:T(8,128)(2,1)}, u32[]{:S(2)}) copy-start(bf16[8,1,56,1024]{3,2,0,1:T(8,128)(2,1)} %get-tuple-element.74) | copy-start | bytes 2752516
  100.2 23.2 %all-to-all-start.5 = ((bf16[4,128,1024]{2,1,0:T(8,128)(2,1)}), bf16[4,128,1024]{2,1,0:T(8,128)(2,1)}, u32[]{:S(2)}, u32[]{:S(2)}) async-start(bf16[4,128,1024]{2,1,0:T(8,128)(2,1)} %get-tuple-element.73), calls=%async_computation.5 | async-start | bytes 2097152 | tf_op jit(solution)/shard_map/all_to_all | solution.py:204
  125.8 3.4 %copy-start.9 = (bf16[512,896]{1,0:T(8,128)(2,1)}, bf16[512,896]{1,0:T(8,128)(2,1)S(1)}, u32[]{:S(2)}) copy-start(bf16[512,896]{1,0:T(8,128)(2,1)S(1)} %convolution_convert_fusion.1) | copy-start | bytes 2752516
  125.9 4.7 %collective-permute-start.1 = (bf16[16,16,896]{2,1,0:T(8,128)(2,1)S(1)}, bf16[16,16,896]{2,1,0:T(8,128)(2,1)S(1)}, u32[]{:S(2)}, u32[]{:S(2)}) collective-permute-start(bf16[16,16,896]{2,1,0:T(8,128)(2,1)S(1)} %dynamic-slice_bitcast_fusion), channel_id=1, source_target_pairs={{0,1},{1,0},{2,3},{3,2},{4,5},{5,4},{6,7},{7,6},{8,9},{9,8},{10,11... | collective-permute-start | bytes 1376264 | tf_op jit(solution)/shard_map/ppermute | solution.py:215
Sparse Core Ops, SparseCore 0:
  36.9 51.1 all-gather.4

commit v5 on v4

--- a/solution.py
+++ b/solution.py
@@ -11,56 +11,79 @@
 
 BLK = 64
 CHUNK = 8
-KEYS = BLK * CHUNK
 ROWS, LANES = 32, 128
 PARTS = 8
+OWN = 16
 FEW = 44
 exp2_scale = 192 ** (-0.5) * math.log2(math.e)
 floor_max = -1e30
 masked_score = -2e30
 
 
-def attention_kernel(scal, lo_ref, q_ref, vup_ref, lat, out_ref, kbuf, acc, done):
+def attention_kernel(scal, lo_ref, q_ref, vup_ref, lat, out_ref, kbuf, acc, top, mass, done):
     heads, toks, width = q_ref.shape
     rows = heads * BLK
     slices = lat.shape[0] // 16
     across = width // LANES
-    last_block = scal.shape[0] - 5
+    n_blocks = scal.shape[0] - 6
+
+    def attend(b, base, size, masked):
+        for j in range(size):
+            src = scal[6 + jnp.minimum(base + j, n_blocks - 1)]
+            for part in range(PARTS):
+                row = j * BLK + part // across * ROWS
+                lane = part % across * LANES
+                kbuf[row : row + ROWS, lane : lane + LANES] = lat[src + part * slices]
+        keys = kbuf[: size * BLK, :]
+        q = q_ref[:, b * BLK : (b + 1) * BLK, :].reshape(rows, width)
+        s = lax.dot_general(q, keys, (((1,), (1,)), ((), ())), preferred_element_type=jnp.float32)
+        if masked:
+            lo = lo_ref[:, b * BLK : (b + 1) * BLK, :].reshape(rows, 1)
+            pos = scal[b] * BLK + lax.broadcasted_iota(jnp.int32, (heads, BLK, 1), 1).reshape(rows, 1)
+            kp = base * BLK + lax.broadcasted_iota(jnp.int32, (1, size * BLK), 1)
+            s = jnp.where((kp <= pos) & (kp >= lo), s, masked_score)
+        tiles = [s[:, t : t + LANES] for t in range(0, size * BLK, LANES)]
+        old = top[...]
+        new = jnp.maximum(old, jnp.max(functools.reduce(jnp.maximum, tiles), axis=1, keepdims=True))
+        factor = jnp.exp2((old - new) * exp2_scale)
+        w = [jnp.exp2((tile - new) * exp2_scale) for tile in tiles]
+        top[...] = new
+        mass[...] = mass[...] * factor + functools.reduce(jnp.add, w)
+        added = jnp.dot(
+            jnp.concatenate([x.astype(jnp.bfloat16) for x in w], axis=1),
+            keys,
+            preferred_element_type=jnp.float32,
+        )
+        for t in range(across):
+            lanes = slice(t * LANES, (t + 1) * LANES)
+            acc[:, lanes] = acc[:, lanes] * factor + added[:, lanes]
 
     for b in range(toks // BLK):
-        block = scal[b]
-        first = scal[2 + b]
-        q = q_ref[:, b * BLK : (b + 1) * BLK, :].reshape(rows, width)
-        lo = lo_ref[:, b * BLK : (b + 1) * BLK, :].reshape(rows, 1)
-        pos = block * BLK + lax.broadcasted_iota(jnp.int32, (heads, BLK, 1), 1).reshape(rows, 1)
+        block, first, clean = scal[b], scal[2 + b], scal[4 + b]
         acc[...] = jnp.zeros_like(acc)
-
-        def step(i, carry):
-            m, total = carry
-            base = first + i * CHUNK
-            for j in range(CHUNK):
-                src = scal[4 + jnp.minimum(base + j, last_block)]
-                for part in range(PARTS):
-                    row = j * BLK + part // across * ROWS
-                    lane = part % across * LANES
-                    kbuf[row : row + ROWS, lane : lane + LANES] = lat[src + part * slices]
-            keys = kbuf[...]
-            s = lax.dot_general(q, keys, (((1,), (1,)), ((), ())), preferred_element_type=jnp.float32)
-            kp = base * BLK + lax.broadcasted_iota(jnp.int32, (1, KEYS), 1)
-            allowed = (kp <= pos) & (kp >= lo)
-            s = jnp.where(allowed, s * exp2_scale, masked_score)
-            new = jnp.maximum(m, jnp.max(s, axis=1, keepdims=True))
-            w = jnp.exp2(s - new)
-            factor = jnp.exp2(m - new)
-            total = total * factor + jnp.sum(w, axis=1, keepdims=True)
-            acc[...] = acc[...] * factor + jnp.dot(
-                w.astype(jnp.bfloat16), keys, preferred_element_type=jnp.float32
-            )
-            return new, total
-
-        count = (block - first + CHUNK) // CHUNK
-        init = (jnp.full((rows, 1), floor_max, jnp.float32), jnp.zeros((rows, 1), jnp.float32))
-        _, total = lax.fori_loop(0, count, step, init)
+        top[...] = jnp.full_like(top, floor_max)
+        mass[...] = jnp.zeros_like(mass)
+        count = block - first + 1
+        wide = (count + CHUNK - 1) // (2 * CHUNK)
+
+        @pl.loop(0, wide)
+        def _(i):
+            base = first + i * 2 * CHUNK
+            whole = (base >= clean) & (base + 2 * CHUNK <= block)
+
+            @pl.when(whole)
+            def _():
+                attend(b, base, 2 * CHUNK, False)
+
+            @pl.when(jnp.logical_not(whole))
+            def _():
+                attend(b, base, 2 * CHUNK, True)
+
+        @pl.when(wide * 2 * CHUNK < count)
+        def _():
+            attend(b, first + wide * 2 * CHUNK, CHUNK, True)
+
+        total = jnp.sum(mass[...], axis=1, keepdims=True)
         latent_out = (acc[...] / total).astype(jnp.bfloat16)
         done[:, b * BLK : (b + 1) * BLK, :] = latent_out.reshape(heads, BLK, width)
 
@@ -68,7 +91,9 @@
     for h in range(heads):
         values = jnp.dot(done[h], vup_ref[h], preferred_element_type=jnp.float32).astype(jnp.bfloat16)
         for copy in range(out_ref.shape[0]):
-            out_ref[copy, :, h * vh : (h + 1) * vh] = values
+            for at in range(0, toks, OWN):
+                to = (at // OWN % 2) * (toks // 2) + at // OWN // 2 * OWN
+                out_ref[copy, to : to + OWN, h * vh : (h + 1) * vh] = values[at : at + OWN, :]
 
 
 def attention(scal, lo, q, vup, lat, copies):
@@ -81,8 +106,10 @@
         in_specs=[pl.BlockSpec(memory_space=pltpu.SMEM)] + [vmem] * 4,
         out_specs=vmem,
         scratch_shapes=[
-            pltpu.VMEM((KEYS, width), jnp.bfloat16),
+            pltpu.VMEM((2 * CHUNK * BLK, width), jnp.bfloat16),
             pltpu.VMEM((heads * BLK, width), jnp.float32),
+            pltpu.VMEM((heads * BLK, LANES), jnp.float32),
+            pltpu.VMEM((heads * BLK, LANES), jnp.float32),
             pltpu.VMEM((heads, toks, width), jnp.bfloat16),
         ],
         compiler_params=pltpu.CompilerParams(vmem_limit_bytes=40 * 2**20),
@@ -101,6 +128,8 @@
     )
     lo = jnp.sum((segment_ids[None, :] < segs[:, None]).astype(jnp.int32), axis=1)
     first = lo.reshape(2, BLK)[:, 0] // BLK
+    clean = (lo.reshape(2, BLK)[:, BLK - 1] + BLK - 1) // BLK
+    first = jnp.concatenate([first, clean])
     n = block_of_slot.shape[0]
     slots = jnp.arange(n, dtype=jnp.int32)
     slot_of_block = jnp.sum(
@@ -201,19 +230,22 @@
     )
 
     wide = head_values.shape[2]
-    rows = lax.all_to_all(head_values, "x", 0, 0, tiled=True).reshape(nx * toks, wide)
+    rows = lax.all_to_all(head_values, "x", 0, 0, tiled=True).reshape(nx, nc, toks // nc, wide)
     columns = jnp.where(zh == 0, jnp.stack([mine, theirs], 1), jnp.stack([theirs, mine], 1))
     columns = columns.reshape(-1, cols.shape[1])
-    partial_value = lax.dot_general(
-        rows, columns, (((1,), (1,)), ((), ())), preferred_element_type=jnp.float32
-    ).astype(jnp.bfloat16)
     n_cols = columns.shape[0]
     own = toks // (nzl * nc)
-    partial_value = partial_value.reshape(nx * nzl, nc, own, n_cols)
-    keep = lax.dynamic_index_in_dim(partial_value, core, 1, keepdims=False)
-    give = lax.dynamic_index_in_dim(partial_value, nc - 1 - core, 1, keepdims=False)
+
+    def project(which):
+        part = lax.dynamic_index_in_dim(rows, which, 1, keepdims=False)
+        return lax.dot_general(
+            part.reshape(-1, wide), columns, (((1,), (1,)), ((), ())), preferred_element_type=jnp.float32
+        )
+
+    give = project(nc - 1 - core).astype(jnp.bfloat16)
     got = lax.ppermute(give, "core", [(i, nc - 1 - i) for i in range(nc)])
-    chip = (keep.astype(jnp.float32) + got.astype(jnp.float32)).astype(jnp.bfloat16)
+    chip = (project(core) + got.astype(jnp.float32)).astype(jnp.bfloat16)
+    chip = chip.reshape(nx * nzl, own, n_cols)
     terms = lax.all_to_all(chip, ("x", "zl"), 0, 0, tiled=True)
     terms = terms.reshape(nx, nzl, own, n_cols).astype(jnp.float32)
     mixed = jnp.sum(terms, axis=1).astype(jnp.bfloat16)

time: 159 us -> 154 us (0.969)
  starting transfers between devices: 43.5 us -> 38.7 us
  Pallas kernels: 9.28 us -> 11.6 us
    all_to_all x1, starting transfers between devices: 8.39 us -> 3.65 us  [per_device(): lax.all_to_all(head_values, 'x', 0, 0, tiled=True)]
    pallas_call x1, Pallas kernels: 9.28 us -> 11.6 us  [attention(): pl.pallas_call(attention_kernel, out_shape=jax.ShapeDtypeStruct((copies,...]
  transfers between devices with their start and end apart: 7 -> 7, of which waited for: 4 -> 4; matrix products, arithmetic and copies ran while one was open for 6% -> 7% of each run, Pallas kernels for 6% -> 8%
where the time goes in v5:
time: 154 us; the launch traced here: 153 us
  waiting for transfers between devices  49.2 us (32%)
  starting transfers between devices  38.7 us (25%)
  blocking collectives  18.7 us (12%)
  between operations  14.3 us (9%)
  Pallas kernels  11.6 us (8%)
  local copies, waits for them, and re-layouts  11.4 us (7%)
  other arithmetic  5.33 us (3%)
  matrix products  2.58 us (2%)
    all_to_all x2, waiting for transfers between devices, over_y(): lax.all_to_all(jnp.broadcast_to(piece[None], (ny,) + piece.shape), 'y', 0...  22.5 us
    all_to_all x1, blocking collectives, per_device(): terms = lax.all_to_all(chip, ('x', 'zl'), 0, 0, tiled=True)  18.7 us
    all_gather x1, waiting for transfers between devices, attend(): lax.all_gather(sent.reshape(kept * ROWS, LANES), ('zh', 'zl', 'core'), ax...  13.3 us
    all_to_all x1, waiting for transfers between devices, per_device(): lax.all_to_all(head_values, 'x', 0, 0, tiled=True)  12 us
    pallas_call x1, Pallas kernels, attention(): pl.pallas_call(attention_kernel, out_shape=jax.ShapeDtypeStruct((copies,...  11.6 us
    all_to_all x2, starting transfers between devices, over_y(): lax.all_to_all(jnp.broadcast_to(piece[None], (ny,) + piece.shape), 'y', 0...  10.7 us
    ppermute x1, starting transfers between devices, per_device(): other = lax.ppermute(cols, 'zh', [(i, nzh - 1 - i) for i in range(nzh)])  10.6 us
    all_to_all x1, starting transfers between devices, per_device(): plane_rows = lax.all_to_all(spread, ('x', 'y'), 0, 0, tiled=True)  10.5 us
  transfers between devices with their start and end apart: 7, of which 4 were waited for; matrix products, arithmetic and copies ran while one was open for 7% of the time, Pallas kernels for 8%

profile of v5, /device:TPU:1, one launch (start us, length us, event | category | flops | bytes accessed | tf_op | source)
XLA Modules:
  0.0 153.3 jit_solution(8792880976404404023)
XLA Ops:
  6.6 0.9 copy-done
  7.5 0.9 broadcast_in_dim.78
  8.4 10.5 %all-to-all-start.4 = ((bf16[32,2,32,128]{3,2,1,0:T(8,128)(2,1)}), bf16[32,2,32,128]{3,2,1,0:T(8,128)(2,1)S(1)}, u32[]{:S(2)}, u32[]{:S(2)}) async-start(bf16[32,2,32,128]{3,2,1,0:T(8,128)(2,1)} %broadcast_in_dim.78), calls=%async_computation.4 | async-start | bytes 1048576 | tf_op jit(solution)/shard_map/all_to_all | solution.py:181
  18.9 10.6 %collective-permute-start = (bf16[56,1024]{1,0:T(8,128)(2,1)}, bf16[56,1024]{1,0:T(8,128)(2,1)S(1)}, u32[]{:S(2)}, u32[]{:S(2)}) collective-permute-start(bf16[56,1024]{1,0:T(8,128)(2,1)} %bitcast.63), channel_id=1, source_target_pairs={{0,8},{8,0},{1,9},{9,1},{2,10},{10,2},{3,11},{11,3},{4,12},{12,4},... | collective-permute-start | bytes 344072 | tf_op jit(solution)/shard_map/ppermute | solution.py:175
  29.5 0.8 reshape.202
  31.9 0.8 select_reduce_fusion.4
  34.0 68.4 %conditional.1 = (bf16[4,128,1024]{2,1,0:T(8,128)(2,1)}, bf16[8,1,56,1024]{3,2,0,1:T(8,128)(2,1)}, bf16[8,1,56,1024]{3,2,0,1:T(8,128)(2,1)}) conditional(s32[]{:T(128)} %convert_element_type.45, (s32[]{:T(128)}, s32[128]{0:T(128)S(1)}, s32[8192]{0:T(1024)S(1)}, bf16[128,8,512]{2,1,0:T(8,128)(2,1)S(1)}, bf16[8,448,128]{2,1,0:T(8,128)(2,1)S(1)}, ...), branch_computations={%region_4.7_spmd, %region_7.11_spmd} | conditional | flops 6468947968 | bytes 86126592 | solution.py:225
  34.5 0.9 reshape.190
  35.5 1.0 broadcast_in_dim.68
  36.5 6.4 %all-to-all-start.2 = ((bf16[8,56,1024]{2,1,0:T(8,128)(2,1)}), bf16[8,56,1024]{2,1,0:T(8,128)(2,1)S(1)}, u32[]{:S(2)}, u32[]{:S(2)}) async-start(bf16[8,56,1024]{2,1,0:T(8,128)(2,1)} %broadcast_in_dim.68), calls=%async_computation.2 | async-start | bytes 1835008 | tf_op jit(solution)/shard_map/cond/branch_1_fun/all_to_all | solution.py:194
  45.1 22.5 %all-to-all-done.2 = bf16[8,56,1024]{2,1,0:T(8,128)(2,1)S(1)} async-done(((bf16[8,56,1024]{2,1,0:T(8,128)(2,1)}), bf16[8,56,1024]{2,1,0:T(8,128)(2,1)S(1)}, u32[]{:S(2)}, u32[]{:S(2)}) %all-to-all-start.2) | async-done | bytes 917536 | tf_op jit(solution)/shard_map/cond/branch_1_fun/all_to_all | solution.py:194
  67.6 1.2 broadcast_in_dim.69
  68.7 4.2 %all-to-all-start.3 = ((bf16[8,56,1024]{2,1,0:T(8,128)(2,1)}), bf16[8,56,1024]{2,1,0:T(8,128)(2,1)}, u32[]{:S(2)}, u32[]{:S(2)}) async-start(bf16[8,56,1024]{2,1,0:T(8,128)(2,1)} %broadcast_in_dim.69), calls=%async_computation.3 | async-start | bytes 1835008 | tf_op jit(solution)/shard_map/cond/branch_1_fun/all_to_all | solution.py:194
  74.7 13.3 %all-gather.5.cloned.1.call-done = bf16[22528,128]{1,0:T(8,128)(2,1)} async-done(((bf16[1408,128]{1,0:T(8,128)(2,1)}), bf16[22528,128]{1,0:T(8,128)(2,1)}) %all-gather.5.cloned.1.call-update) | async-done | bytes 5767184 | tf_op jit(solution)/shard_map/cond/branch_1_fun/all_gather | solution.py:204
  88.1 2.6 %copy-done.2 = bf16[22528,128]{1,0:T(8,128)(2,1)S(1)} copy-done((bf16[22528,128]{1,0:T(8,128)(2,1)S(1)}, bf16[22528,128]{1,0:T(8,128)(2,1)}, u32[]{:S(2)}) %copy-start.2) | copy-done | bytes 5767192 | tf_op jit(solution)/shard_map/cond
  90.8 11.6 %latent_attention.3 = bf16[4,128,1024]{2,1,0:T(8,128)(2,1)} custom-call(s32[134]{0:T(256)S(1)} %pad_add_fusion.2.scal, s32[8,128,1]{2,1,0:T(8,128)S(1)} %broadcast_in_dim.67.lo_ref, bf16[8,128,512]{2,1,0:T(8,128)(2,1)S(1)} %bitcast.47, bf16[8,512,128]{2,1,0:T(8,128)(2,1)S(1)} %pad.6.vup_ref, bf16[704,32,128]{2,1,0:T(8,128)(2,1)S(1)} %bitcast.50), custom_call_target="tpu_custom_call" | custom-call | flops 6442450944 | bytes 5767168 | tf_op jit(solution)/shard_map/cond/branch_1_fun/latent_attention/pallas_call | solution.py:103
  102.4 3.6 %all-to-all-start.5 = ((bf16[4,128,1024]{2,1,0:T(8,128)(2,1)}), bf16[4,128,1024]{2,1,0:T(8,128)(2,1)S(1)}, u32[]{:S(2)}, u32[]{:S(2)}) async-start(bf16[4,128,1024]{2,1,0:T(8,128)(2,1)} %get-tuple-element.73), calls=%async_computation.5 | async-start | bytes 2097152 | tf_op jit(solution)/shard_map/all_to_all | solution.py:233
  106.1 2.9 %maximum_select_fusion = bf16[8,2,56,1024]{3,2,1,0:T(8,128)(2,1)} fusion(bf16[8,1,56,1024]{3,2,1,0:T(8,128)(2,1)} %bitcast.19, bf16[8,1,56,1024]{3,2,1,0:T(8,128)(2,1)S(1)} %bitcast.56, pred[]{:T(512)S(6)} %eq.104), kind=kLoop, calls=%fused_computation.61 | loop fusion | flops 2752512 | bytes 3670017 | tf_op jit(solution)/shard_map/jit(_where)/select_n | solution.py:234
  109.0 12.0 %all-to-all-done.5 = bf16[4,128,1024]{2,1,0:T(8,128)(2,1)S(1)} async-done(((bf16[4,128,1024]{2,1,0:T(8,128)(2,1)}), bf16[4,128,1024]{2,1,0:T(8,128)(2,1)S(1)}, u32[]{:S(2)}, u32[]{:S(2)}) %all-to-all-start.5) | async-done | bytes 1048608 | tf_op jit(solution)/shard_map/all_to_all | solution.py:233
  121.1 0.7 convolution_convert_fusion.1
  121.8 3.0 %collective-permute-start.1 = (bf16[256,896]{1,0:T(8,128)(2,1)S(1)}, bf16[256,896]{1,0:T(8,128)(2,1)S(1)}, u32[]{:S(2)}, u32[]{:S(2)}) collective-permute-start(bf16[256,896]{1,0:T(8,128)(2,1)S(1)} %convolution_convert_fusion.1), channel_id=1, source_target_pairs={{0,1},{1,0},{2,3},{3,2},{4,5},{5,4},{6,7},{7,6},{8,9},{9,8},{10,11... | collective-permute-start | bytes 1376264 | tf_op jit(solution)/shard_map/ppermute | solution.py:246
  124.8 1.4 collective-permute-done.1
  126.3 0.7 add_convert_fusion
  127.0 18.7 %all_to_all.31 = bf16[16,16,896]{2,1,0:T(8,128)(2,1)S(1)} all-to-all(bf16[16,16,896]{2,1,0:T(8,128)(2,1)S(1)} %bitcast.61), channel_id=1, replica_groups=mesh['x'=4,'y'=8,'zh'=2,'zl'=4,'core'=2] {'x','zl'}, dimensions={0} | all-to-all | bytes 917504 | tf_op jit(solution)/shard_map/all_to_all | solution.py:249
  (60 shorter events, 6.0 us)
Async XLA Ops:
  6.5 0.9 copy-start
  6.5 27.4 %copy-start.11 = (bf16[1024,56]{0,1:T(8,128)(2,1)S(1)}, bf16[1024,56]{0,1:T(8,128)(2,1)}, u32[]{:S(2)}) copy-start(bf16[1024,56]{0,1:T(8,128)(2,1)} %param.13) | copy-start | bytes 344068
  6.5 24.0 %copy-start.10 = (s32[8192]{0:T(1024)S(1)}, s32[8192]{0:T(1024)}, u32[]{:S(2)}) copy-start(s32[8192]{0:T(1024)} %param.10) | copy-start | bytes 98308
  6.5 24.6 %copy-start.12 = (s32[128]{0:T(128)S(1)}, s32[128]{0:T(128)}, u32[]{:S(2)}) copy-start(s32[128]{0:T(128)} %param.11) | copy-start | bytes 1540
  6.5 27.4 %copy-start.5 = (bf16[8,448,128]{2,1,0:T(8,128)(2,1)S(1)}, bf16[8,448,128]{2,1,0:T(8,128)(2,1)}, u32[]{:S(2)}) copy-start(bf16[8,448,128]{2,1,0:T(8,128)(2,1)} %param.12) | copy-start | bytes 2752516
  6.5 27.4 %copy-start.4 = (bf16[128,8,512]{2,1,0:T(8,128)(2,1)S(1)}, bf16[128,8,512]{2,1,0:T(8,128)(2,1)}, u32[]{:S(2)}) copy-start(bf16[128,8,512]{2,1,0:T(8,128)(2,1)} %param.8) | copy-start | bytes 3145732
  8.4 25.5 %all-to-all-start.4 = ((bf16[32,2,32,128]{3,2,1,0:T(8,128)(2,1)}), bf16[32,2,32,128]{3,2,1,0:T(8,128)(2,1)S(1)}, u32[]{:S(2)}, u32[]{:S(2)}) async-start(bf16[32,2,32,128]{3,2,1,0:T(8,128)(2,1)} %broadcast_in_dim.78), calls=%async_computation.4 | async-start | bytes 1048576 | tf_op jit(solution)/shard_map/all_to_all | solution.py:181
  18.9 15.0 %collective-permute-start = (bf16[56,1024]{1,0:T(8,128)(2,1)}, bf16[56,1024]{1,0:T(8,128)(2,1)S(1)}, u32[]{:S(2)}, u32[]{:S(2)}) collective-permute-start(bf16[56,1024]{1,0:T(8,128)(2,1)} %bitcast.63), channel_id=1, source_target_pairs={{0,8},{8,0},{1,9},{9,1},{2,10},{10,2},{3,11},{11,3},{4,12},{12,4},... | collective-permute-start | bytes 344072 | tf_op jit(solution)/shard_map/ppermute | solution.py:175
  34.0 54.0 %all-gather.5.cloned.1.call-start = ((), (), s32[]{:S(2)}) async-start(), calls=%async_computation.8 | async-start | bytes 6127616 | tf_op jit(solution)/shard_map/cond/branch_1_fun/all_gather | solution.py:204
  36.5 31.0 %all-to-all-start.2 = ((bf16[8,56,1024]{2,1,0:T(8,128)(2,1)}), bf16[8,56,1024]{2,1,0:T(8,128)(2,1)S(1)}, u32[]{:S(2)}, u32[]{:S(2)}) async-start(bf16[8,56,1024]{2,1,0:T(8,128)(2,1)} %broadcast_in_dim.68), calls=%async_computation.2 | async-start | bytes 1835008 | tf_op jit(solution)/shard_map/cond/branch_1_fun/all_to_all | solution.py:194
  67.6 6.1 %copy-start.7 = (bf16[8,56,1024]{2,1,0:T(8,128)(2,1)}, bf16[8,56,1024]{2,1,0:T(8,128)(2,1)S(1)}, u32[]{:S(2)}) copy-start(bf16[8,56,1024]{2,1,0:T(8,128)(2,1)S(1)} %all-to-all-done.2) | copy-start | bytes 2752516 | tf_op jit(solution)/shard_map/cond
  68.7 33.7 %all-to-all-start.3 = ((bf16[8,56,1024]{2,1,0:T(8,128)(2,1)}), bf16[8,56,1024]{2,1,0:T(8,128)(2,1)}, u32[]{:S(2)}, u32[]{:S(2)}) async-start(bf16[8,56,1024]{2,1,0:T(8,128)(2,1)} %broadcast_in_dim.69), calls=%async_computation.3 | async-start | bytes 1835008 | tf_op jit(solution)/shard_map/cond/branch_1_fun/all_to_all | solution.py:194
  88.1 2.6 %copy-start.2 = (bf16[22528,128]{1,0:T(8,128)(2,1)S(1)}, bf16[22528,128]{1,0:T(8,128)(2,1)}, u32[]{:S(2)}) copy-start(bf16[22528,128]{1,0:T(8,128)(2,1)} %all-gather.5.cloned.1.call-done) | copy-start | bytes 17301508 | tf_op jit(solution)/shard_map/cond
  102.4 3.7 %copy-start.8 = (bf16[8,1,56,1024]{3,2,0,1:T(8,128)(2,1)S(1)}, bf16[8,1,56,1024]{3,2,0,1:T(8,128)(2,1)}, u32[]{:S(2)}) copy-start(bf16[8,1,56,1024]{3,2,0,1:T(8,128)(2,1)} %get-tuple-element.74) | copy-start | bytes 2752516
  102.4 18.6 %all-to-all-start.5 = ((bf16[4,128,1024]{2,1,0:T(8,128)(2,1)}), bf16[4,128,1024]{2,1,0:T(8,128)(2,1)S(1)}, u32[]{:S(2)}, u32[]{:S(2)}) async-start(bf16[4,128,1024]{2,1,0:T(8,128)(2,1)} %get-tuple-element.73), calls=%async_computation.5 | async-start | bytes 2097152 | tf_op jit(solution)/shard_map/all_to_all | solution.py:233
  109.0 12.1 %copy-start.9 = (bf16[8,2,56,1024]{3,2,1,0:T(8,128)(2,1)S(1)}, bf16[8,2,56,1024]{3,2,1,0:T(8,128)(2,1)}, u32[]{:S(2)}) copy-start(bf16[8,2,56,1024]{3,2,1,0:T(8,128)(2,1)} %maximum_select_fusion) | copy-start | bytes 5505028
  121.8 4.4 %collective-permute-start.1 = (bf16[256,896]{1,0:T(8,128)(2,1)S(1)}, bf16[256,896]{1,0:T(8,128)(2,1)S(1)}, u32[]{:S(2)}, u32[]{:S(2)}) collective-permute-start(bf16[256,896]{1,0:T(8,128)(2,1)S(1)} %convolution_convert_fusion.1), channel_id=1, source_target_pairs={{0,1},{1,0},{2,3},{3,2},{4,5},{5,4},{6,7},{7,6},{8,9},{9,8},{10,11... | collective-permute-start | bytes 1376264 | tf_op jit(solution)/shard_map/ppermute | solution.py:246
Sparse Core Ops, SparseCore 0:
  36.9 51.0 all-gather.4

commit v6 on v5

--- a/solution.py
+++ b/solution.py
@@ -14,7 +14,7 @@
 ROWS, LANES = 32, 128
 PARTS = 8
 OWN = 16
-FEW = 44
+LEVELS = (40, 48)
 exp2_scale = 192 ** (-0.5) * math.log2(math.e)
 floor_max = -1e30
 masked_score = -2e30
@@ -157,7 +157,8 @@
     before = (blocks[:, None] < blocks[None, :]) & (slot_plane[:, None] == slot_plane[None, :])
     rank = jnp.dot(need.astype(jnp.bfloat16), before.astype(jnp.bfloat16), preferred_element_type=jnp.float32)
     most = jnp.max(jnp.where(need, rank, -1.0)) + 1.0
-    return need, rank, most <= FEW
+    level = sum((most > kept).astype(jnp.int32) for kept in LEVELS)
+    return need, rank, level
 
 
 def per_device(query, latent, segment_ids, block_of_slot, value_up, out_proj):
@@ -181,26 +182,24 @@
     plane_rows = lax.all_to_all(spread, ("x", "y"), 0, 0, tiled=True)
     plane_rows = plane_rows.reshape(slices, ROWS * LANES)
 
-    need, rank, fits = need_tables(segment_ids, block_of_slot, plane, nzh, halves)
+    need, rank, level = need_tables(segment_ids, block_of_slot, plane, nzh, halves)
     my_need = lax.dynamic_index_in_dim(need, x * ny + y, 0, keepdims=False)
     my_rank = lax.dynamic_index_in_dim(rank, x * ny + y, 0, keepdims=False).astype(jnp.int32)
     row_need = lax.dynamic_index_in_dim(my_need.reshape(plane, nzh, halves), zh, 1, keepdims=False)
     row_rank = lax.dynamic_index_in_dim(my_rank.reshape(plane, nzh, halves), zh, 1, keepdims=False)
     row_rank = jnp.where(row_need, row_rank, -1).reshape(1, slices)
-    pick = (row_rank == jnp.arange(FEW, dtype=jnp.int32)[:, None]).astype(jnp.bfloat16)
+    pick = (row_rank == jnp.arange(LEVELS[-1], dtype=jnp.int32)[:, None]).astype(jnp.bfloat16)
     pick, my_rank = lax.optimization_barrier((pick, my_rank))
 
     def over_y(piece):
         return lax.all_to_all(jnp.broadcast_to(piece[None], (ny,) + piece.shape), "y", 0, 0, tiled=True)
 
-    def attend(few, operands):
+    def attend(kept, operands):
         plane_rows, cols, other, query, segment_ids, block_of_slot, value_up, my_rank, pick = operands
+        few = kept < slices
+        sent = plane_rows
         if few:
-            kept = FEW
-            sent = jnp.dot(pick, plane_rows, preferred_element_type=jnp.float32).astype(jnp.bfloat16)
-        else:
-            kept = slices
-            sent = plane_rows
+            sent = jnp.dot(pick[:kept], plane_rows, preferred_element_type=jnp.float32).astype(jnp.bfloat16)
         gathered = lax.all_gather(sent.reshape(kept * ROWS, LANES), ("zh", "zl", "core"), axis=0, tiled=True)
         gathered = gathered.reshape(-1, ROWS, LANES)
 
@@ -222,10 +221,9 @@
         scal = jnp.concatenate([my_blocks, first, start]).astype(jnp.int32)
         return attention(scal, lo_rows, q, vup, gathered, nx), mine, theirs
 
-    head_values, mine, theirs = lax.cond(
-        fits,
-        functools.partial(attend, True),
-        functools.partial(attend, False),
+    head_values, mine, theirs = lax.switch(
+        level,
+        [functools.partial(attend, kept) for kept in (*LEVELS, slices)],
         (plane_rows, cols, other, query, segment_ids, block_of_slot, value_up, my_rank, pick),
     )
 
@@ -244,12 +242,13 @@
 
     give = project(nc - 1 - core).astype(jnp.bfloat16)
     got = lax.ppermute(give, "core", [(i, nc - 1 - i) for i in range(nc)])
-    chip = (project(core) + got.astype(jnp.float32)).astype(jnp.bfloat16)
+    keep = lax.optimization_barrier(project(core))
+    chip = (keep + got.astype(jnp.float32)).astype(jnp.bfloat16)
     chip = chip.reshape(nx * nzl, own, n_cols)
     terms = lax.all_to_all(chip, ("x", "zl"), 0, 0, tiled=True)
-    terms = terms.reshape(nx, nzl, own, n_cols).astype(jnp.float32)
-    mixed = jnp.sum(terms, axis=1).astype(jnp.bfloat16)
-    return mixed.transpose(1, 0, 2).reshape(own, nx * n_cols)
+    terms = terms.reshape(nx, nzl, own, n_cols)
+    sums = [functools.reduce(jnp.add, [terms[i, j].astype(jnp.float32) for j in range(nzl)]) for i in range(nx)]
+    return jnp.concatenate([each.astype(jnp.bfloat16) for each in sums], axis=1)
 
 
 AXES = {"x": 4, "y": 8, "zh": 2, "zl": 4, "core": 2}

time: 154 us -> 155 us (level)
  Pallas kernels: 11.6 us -> 4.55 us
  starting transfers between devices: 38.7 us -> 41.9 us
  other arithmetic: 5.33 us -> 7.69 us
  local copies, waits for them, and re-layouts: 11.4 us -> 13.4 us
    all_to_all x2, waiting for transfers between devices: 22.5 us -> 32.3 us  [over_y(): lax.all_to_all(jnp.broadcast_to(piece[None], (ny,) + piece.shape), 'y', 0...]
    all_gather x1, waiting for transfers between devices: 13.3 us -> 5.94 us  [attend(): lax.all_gather(sent.reshape(kept * ROWS, LANES), ('zh', 'zl', 'core'), ax...]
    pallas_call x1, Pallas kernels: 11.6 us -> 4.55 us  [attention(): pl.pallas_call(attention_kernel, out_shape=jax.ShapeDtypeStruct((copies,...]
    ppermute x1, starting transfers between devices: 3.01 us -> 6.1 us  [per_device(): got = lax.ppermute(give, 'core', [(i, nc - 1 - i) for i in range(nc)])]
    all_to_all x1, waiting for transfers between devices: 12 us -> 9.32 us  [per_device(): lax.all_to_all(head_values, 'x', 0, 0, tiled=True)]
  transfers between devices with their start and end apart: 7 -> 7, of which waited for: 4 -> 5; matrix products, arithmetic and copies ran while one was open for 7% -> 11% of each run, Pallas kernels for 8% -> 3%
where the time goes in v6:
time: 155 us; the launch traced here: 153 us
  waiting for transfers between devices  48.2 us (31%)
  starting transfers between devices  41.9 us (27%)
  blocking collectives  19.2 us (12%)
  between operations  14.2 us (9%)
  local copies, waits for them, and re-layouts  13.4 us (9%)
  other arithmetic  7.69 us (5%)
  Pallas kernels  4.55 us (3%)
  matrix products  2.57 us (2%)
    all_to_all x2, waiting for transfers between devices, over_y(): lax.all_to_all(jnp.broadcast_to(piece[None], (ny,) + piece.shape), 'y', 0...  32.3 us
    all_to_all x1, blocking collectives, per_device(): terms = lax.all_to_all(chip, ('x', 'zl'), 0, 0, tiled=True)  19.2 us
    all_to_all x2, starting transfers between devices, over_y(): lax.all_to_all(jnp.broadcast_to(piece[None], (ny,) + piece.shape), 'y', 0...  10.7 us
    ppermute x1, starting transfers between devices, per_device(): other = lax.ppermute(cols, 'zh', [(i, nzh - 1 - i) for i in range(nzh)])  10.6 us
    all_to_all x1, starting transfers between devices, per_device(): plane_rows = lax.all_to_all(spread, ('x', 'y'), 0, 0, tiled=True)  10.5 us
    all_to_all x1, waiting for transfers between devices, per_device(): lax.all_to_all(head_values, 'x', 0, 0, tiled=True)  9.32 us
    ppermute x1, starting transfers between devices, per_device(): got = lax.ppermute(give, 'core', [(i, nc - 1 - i) for i in range(nc)])  6.1 us
    all_gather x1, waiting for transfers between devices, attend(): lax.all_gather(sent.reshape(kept * ROWS, LANES), ('zh', 'zl', 'core'), ax...  5.94 us
  transfers between devices with their start and end apart: 7, of which 5 were waited for; matrix products, arithmetic and copies ran while one was open for 11% of the time, Pallas kernels for 3%

profile of v6, /device:TPU:1, one launch (start us, length us, event | category | flops | bytes accessed | tf_op | source)
XLA Modules:
  0.0 153.2 jit_solution(18369585756006557461)
XLA Ops:
  6.5 0.9 copy-done
  7.4 0.9 broadcast_in_dim.124
  8.4 10.5 %all-to-all-start.6 = ((bf16[32,2,32,128]{3,2,1,0:T(8,128)(2,1)}), bf16[32,2,32,128]{3,2,1,0:T(8,128)(2,1)S(1)}, u32[]{:S(2)}, u32[]{:S(2)}) async-start(bf16[32,2,32,128]{3,2,1,0:T(8,128)(2,1)} %broadcast_in_dim.124), calls=%async_computation.6 | async-start | bytes 1048576 | tf_op jit(solution)/shard_map/all_to_all | solution.py:182
  18.9 10.6 %collective-permute-start = (bf16[56,1024]{1,0:T(8,128)(2,1)}, bf16[56,1024]{1,0:T(8,128)(2,1)S(1)}, u32[]{:S(2)}, u32[]{:S(2)}) collective-permute-start(bf16[56,1024]{1,0:T(8,128)(2,1)} %bitcast.83), channel_id=1, source_target_pairs={{0,8},{8,0},{1,9},{9,1},{2,10},{10,2},{3,11},{11,3},{4,12},{12,4},... | collective-permute-start | bytes 344072 | tf_op jit(solution)/shard_map/ppermute | solution.py:176
  29.5 0.8 reshape.257
  30.5 1.3 convert_reduce_fusion.3
  32.6 0.8 select_reduce_fusion.5
  36.6 65.6 %conditional.1 = (bf16[4,128,1024]{2,1,0:T(8,128)(2,1)}, bf16[8,1,56,1024]{3,2,0,1:T(8,128)(2,1)}, bf16[8,1,56,1024]{3,2,0,1:T(8,128)(2,1)}) conditional(s32[]{:T(128)} %clamp.3, (s32[]{:T(128)}, s32[128]{0:T(128)}, s32[8192]{0:T(1024)}, s32[128]{0:T(128)S(1)}, bf16[128,8,512]{2,1,0:T(8,128)(2,1)}, ...), branch_computations={%region_4.8_spmd, %region_8.12_spmd, %region_12.15_spmd} | conditional | flops 6471061504 | bytes 90454096 | solution.py:224
  37.0 0.9 reshape.241
  37.9 2.0 %broadcast_in_dim.81 = bf16[8,56,1024]{2,1,0:T(8,128)(2,1)} broadcast(bf16[56,1024]{1,0:T(8,128)(2,1)} %get-tuple-element.74), dimensions={1,2} | broadcast | bytes 1032192 | tf_op jit(solution)/shard_map/cond/branch_0_fun/broadcast_in_dim | solution.py:195
  39.8 6.4 %all-to-all-start = ((bf16[8,56,1024]{2,1,0:T(8,128)(2,1)}), bf16[8,56,1024]{2,1,0:T(8,128)(2,1)S(1)}, u32[]{:S(2)}, u32[]{:S(2)}) async-start(bf16[8,56,1024]{2,1,0:T(8,128)(2,1)} %broadcast_in_dim.81), calls=%async_computation | async-start | bytes 1835008 | tf_op jit(solution)/shard_map/cond/branch_0_fun/all_to_all | solution.py:195
  48.5 24.1 %all-to-all-done = bf16[8,56,1024]{2,1,0:T(8,128)(2,1)S(1)} async-done(((bf16[8,56,1024]{2,1,0:T(8,128)(2,1)}), bf16[8,56,1024]{2,1,0:T(8,128)(2,1)S(1)}, u32[]{:S(2)}, u32[]{:S(2)}) %all-to-all-start) | async-done | bytes 917536 | tf_op jit(solution)/shard_map/cond/branch_0_fun/all_to_all | solution.py:195
  72.6 1.1 broadcast_in_dim.82
  73.8 4.2 %all-to-all-start.1 = ((bf16[8,56,1024]{2,1,0:T(8,128)(2,1)}), bf16[8,56,1024]{2,1,0:T(8,128)(2,1)}, u32[]{:S(2)}, u32[]{:S(2)}) async-start(bf16[8,56,1024]{2,1,0:T(8,128)(2,1)} %broadcast_in_dim.82), calls=%async_computation.1 | async-start | bytes 1835008 | tf_op jit(solution)/shard_map/cond/branch_0_fun/all_to_all | solution.py:195
  79.0 1.3 pad.7.vup_ref
  81.0 5.9 %all-gather.4.cloned.1.call-done = bf16[20480,128]{1,0:T(8,128)(2,1)} async-done(((bf16[1280,128]{1,0:T(8,128)(2,1)}), bf16[20480,128]{1,0:T(8,128)(2,1)}) %all-gather.4.cloned.1.call-update) | async-done | bytes 5242896 | tf_op jit(solution)/shard_map/cond/branch_0_fun/all_gather | solution.py:203
  87.0 2.5 %copy-done.3 = bf16[20480,128]{1,0:T(8,128)(2,1)S(1)} copy-done((bf16[20480,128]{1,0:T(8,128)(2,1)S(1)}, bf16[20480,128]{1,0:T(8,128)(2,1)}, u32[]{:S(2)}) %copy-start.3) | copy-done | bytes 5242904 | tf_op jit(solution)/shard_map/cond
  89.5 4.5 %latent_attention.3 = bf16[4,128,1024]{2,1,0:T(8,128)(2,1)} custom-call(s32[134]{0:T(256)S(1)} %pad_add_fusion.scal, s32[8,128,1]{2,1,0:T(8,128)S(1)} %broadcast_in_dim.80.lo_ref, bf16[8,128,512]{2,1,0:T(8,128)(2,1)S(1)} %bitcast.64, bf16[8,512,128]{2,1,0:T(8,128)(2,1)S(1)} %pad.7.vup_ref, bf16[640,32,128]{2,1,0:T(8,128)(2,1)S(1)} %bitcast.69), custom_call_target="tpu_custom_call" | custom-call | flops 6442450944 | bytes 5242880 | tf_op jit(solution)/shard_map/cond/branch_0_fun/latent_attention/pallas_call | solution.py:103
  94.0 8.1 %all-to-all-done.1 = bf16[8,56,1024]{2,1,0:T(8,128)(2,1)} async-done(((bf16[8,56,1024]{2,1,0:T(8,128)(2,1)}), bf16[8,56,1024]{2,1,0:T(8,128)(2,1)}, u32[]{:S(2)}, u32[]{:S(2)}) %all-to-all-start.1) | async-done | bytes 917536 | tf_op jit(solution)/shard_map/cond/branch_0_fun/all_to_all | solution.py:195
  102.2 4.0 %all-to-all-start.7 = ((bf16[4,128,1024]{2,1,0:T(8,128)(2,1)}), bf16[4,128,1024]{2,1,0:T(8,128)(2,1)S(1)}, u32[]{:S(2)}, u32[]{:S(2)}) async-start(bf16[4,128,1024]{2,1,0:T(8,128)(2,1)} %get-tuple-element.105), calls=%async_computation.7 | async-start | bytes 2097152 | tf_op jit(solution)/shard_map/all_to_all | solution.py:231
  106.2 2.5 %maximum_select_fusion = bf16[8,2,56,1024]{3,2,1,0:T(8,128)(2,1)S(1)} fusion(bf16[8,1,56,1024]{3,2,1,0:T(8,128)(2,1)} %bitcast.25, bf16[8,1,56,1024]{3,2,1,0:T(8,128)(2,1)} %bitcast.79, pred[]{:T(512)S(6)} %eq.129), kind=kLoop, calls=%fused_computation.93 | loop fusion | flops 2752512 | bytes 3670017 | tf_op jit(solution)/shard_map/jit(_where)/select_n | solution.py:232
  108.7 9.3 %all-to-all-done.7 = bf16[4,128,1024]{2,1,0:T(8,128)(2,1)S(1)} async-done(((bf16[4,128,1024]{2,1,0:T(8,128)(2,1)}), bf16[4,128,1024]{2,1,0:T(8,128)(2,1)S(1)}, u32[]{:S(2)}, u32[]{:S(2)}) %all-to-all-start.7) | async-done | bytes 1048608 | tf_op jit(solution)/shard_map/all_to_all | solution.py:231
  118.9 6.1 %collective-permute-start.1 = (bf16[256,896]{1,0:T(8,128)(2,1)S(1)}, bf16[256,896]{1,0:T(8,128)(2,1)S(1)}, u32[]{:S(2)}, u32[]{:S(2)}) collective-permute-start(bf16[256,896]{1,0:T(8,128)(2,1)S(1)} %convolution_convert_fusion.2), channel_id=1, source_target_pairs={{0,1},{1,0},{2,3},{3,2},{4,5},{5,4},{6,7},{7,6},{8,9},{9,8},{10,11... | collective-permute-start | bytes 1376264 | tf_op jit(solution)/shard_map/ppermute | solution.py:244
  126.5 19.2 %all_to_all.39 = bf16[16,16,896]{2,1,0:T(8,128)(2,1)S(1)} all-to-all(bf16[16,16,896]{2,1,0:T(8,128)(2,1)S(1)} %bitcast.81), channel_id=1, replica_groups=mesh['x'=4,'y'=8,'zh'=2,'zl'=4,'core'=2] {'x','zl'}, dimensions={0} | all-to-all | bytes 917504 | tf_op jit(solution)/shard_map/all_to_all | solution.py:248
  (53 shorter events, 9.3 us)
Async XLA Ops:
  6.5 0.9 copy-start
  8.4 28.2 %all-to-all-start.6 = ((bf16[32,2,32,128]{3,2,1,0:T(8,128)(2,1)}), bf16[32,2,32,128]{3,2,1,0:T(8,128)(2,1)S(1)}, u32[]{:S(2)}, u32[]{:S(2)}) async-start(bf16[32,2,32,128]{3,2,1,0:T(8,128)(2,1)} %broadcast_in_dim.124), calls=%async_computation.6 | async-start | bytes 1048576 | tf_op jit(solution)/shard_map/all_to_all | solution.py:182
  18.9 17.7 %collective-permute-start = (bf16[56,1024]{1,0:T(8,128)(2,1)}, bf16[56,1024]{1,0:T(8,128)(2,1)S(1)}, u32[]{:S(2)}, u32[]{:S(2)}) collective-permute-start(bf16[56,1024]{1,0:T(8,128)(2,1)} %bitcast.83), channel_id=1, source_target_pairs={{0,8},{8,0},{1,9},{9,1},{2,10},{10,2},{3,11},{11,3},{4,12},{12,4},... | collective-permute-start | bytes 344072 | tf_op jit(solution)/shard_map/ppermute | solution.py:176
  36.6 9.6 %copy-start.14 = (s32[128]{0:T(128)S(1)}, s32[128]{0:T(128)}, u32[]{:S(2)}) copy-start(s32[128]{0:T(128)} %get-tuple-element.64) | copy-start | bytes 1540 | tf_op jit(solution)/shard_map/cond
  36.6 11.7 %copy-start.11 = (s32[8192]{0:T(1024)S(1)}, s32[8192]{0:T(1024)}, u32[]{:S(2)}) copy-start(s32[8192]{0:T(1024)} %get-tuple-element.66) | copy-start | bytes 98308 | tf_op jit(solution)/shard_map/cond
  36.6 42.1 %copy-start.4 = (bf16[128,8,512]{2,1,0:T(8,128)(2,1)S(1)}, bf16[128,8,512]{2,1,0:T(8,128)(2,1)}, u32[]{:S(2)}) copy-start(bf16[128,8,512]{2,1,0:T(8,128)(2,1)} %get-tuple-element.198) | copy-start | bytes 3145732 | tf_op jit(solution)/shard_map/cond
  36.6 50.3 %all-gather.4.cloned.1.call-start = ((), (), s32[]{:S(2)}) async-start(), calls=%async_computation.9 | async-start | bytes 5570560 | tf_op jit(solution)/shard_map/cond/branch_0_fun/all_gather | solution.py:203
  39.8 32.8 %all-to-all-start = ((bf16[8,56,1024]{2,1,0:T(8,128)(2,1)}), bf16[8,56,1024]{2,1,0:T(8,128)(2,1)S(1)}, u32[]{:S(2)}, u32[]{:S(2)}) async-start(bf16[8,56,1024]{2,1,0:T(8,128)(2,1)} %broadcast_in_dim.81), calls=%async_computation | async-start | bytes 1835008 | tf_op jit(solution)/shard_map/cond/branch_0_fun/all_to_all | solution.py:195
  72.6 6.1 %copy-start.8 = (bf16[8,56,1024]{2,1,0:T(8,128)(2,1)}, bf16[8,56,1024]{2,1,0:T(8,128)(2,1)S(1)}, u32[]{:S(2)}) copy-start(bf16[8,56,1024]{2,1,0:T(8,128)(2,1)S(1)} %all-to-all-done) | copy-start | bytes 2752516 | tf_op jit(solution)/shard_map/cond
  73.8 28.4 %all-to-all-start.1 = ((bf16[8,56,1024]{2,1,0:T(8,128)(2,1)}), bf16[8,56,1024]{2,1,0:T(8,128)(2,1)}, u32[]{:S(2)}, u32[]{:S(2)}) async-start(bf16[8,56,1024]{2,1,0:T(8,128)(2,1)} %broadcast_in_dim.82), calls=%async_computation.1 | async-start | bytes 1835008 | tf_op jit(solution)/shard_map/cond/branch_0_fun/all_to_all | solution.py:195
  87.0 2.5 %copy-start.3 = (bf16[20480,128]{1,0:T(8,128)(2,1)S(1)}, bf16[20480,128]{1,0:T(8,128)(2,1)}, u32[]{:S(2)}) copy-start(bf16[20480,128]{1,0:T(8,128)(2,1)} %all-gather.4.cloned.1.call-done) | copy-start | bytes 15728644 | tf_op jit(solution)/shard_map/cond
  102.2 15.8 %all-to-all-start.7 = ((bf16[4,128,1024]{2,1,0:T(8,128)(2,1)}), bf16[4,128,1024]{2,1,0:T(8,128)(2,1)S(1)}, u32[]{:S(2)}, u32[]{:S(2)}) async-start(bf16[4,128,1024]{2,1,0:T(8,128)(2,1)} %get-tuple-element.105), calls=%async_computation.7 | async-start | bytes 2097152 | tf_op jit(solution)/shard_map/all_to_all | solution.py:231
  118.9 7.5 %collective-permute-start.1 = (bf16[256,896]{1,0:T(8,128)(2,1)S(1)}, bf16[256,896]{1,0:T(8,128)(2,1)S(1)}, u32[]{:S(2)}, u32[]{:S(2)}) collective-permute-start(bf16[256,896]{1,0:T(8,128)(2,1)S(1)} %convolution_convert_fusion.2), channel_id=1, source_target_pairs={{0,1},{1,0},{2,3},{3,2},{4,5},{5,4},{6,7},{7,6},{8,9},{9,8},{10,11... | collective-permute-start | bytes 1376264 | tf_op jit(solution)/shard_map/ppermute | solution.py:244
Sparse Core Ops, SparseCore 0:
  39.6 47.2 all-gather.3

commit v7 on v6

--- a/solution.py
+++ b/solution.py
@@ -192,7 +192,7 @@
     pick, my_rank = lax.optimization_barrier((pick, my_rank))
 
     def over_y(piece):
-        return lax.all_to_all(jnp.broadcast_to(piece[None], (ny,) + piece.shape), "y", 0, 0, tiled=True)
+        return lax.all_gather(piece, "y", axis=0)
 
     def attend(kept, operands):
         plane_rows, cols, other, query, segment_ids, block_of_slot, value_up, my_rank, pick = operands

time: 155 us -> 164 us (1.058)
  the two profiles are of different devices: /device:TPU:1 before, /device:TPU:32 now
where the time goes in v7:
time: 164 us; the launch traced here: 163 us
  blocking collectives  77.5 us (47%)
  starting transfers between devices  29.2 us (18%)
  between operations  14.2 us (9%)
  local copies, waits for them, and re-layouts  12.9 us (8%)
  waiting for transfers between devices  9.41 us (6%)
  other arithmetic  8.4 us (5%)
  Pallas kernels  7.54 us (5%)
  matrix products  2.57 us (2%)
    all_gather x2, blocking collectives, over_y(): return lax.all_gather(piece, 'y', axis=0)  56.8 us
    all_to_all x1, blocking collectives, per_device(): terms = lax.all_to_all(chip, ('x', 'zl'), 0, 0, tiled=True)  20.7 us
    ppermute x1, starting transfers between devices, per_device(): other = lax.ppermute(cols, 'zh', [(i, nzh - 1 - i) for i in range(nzh)])  10.9 us
    all_to_all x1, starting transfers between devices, per_device(): plane_rows = lax.all_to_all(spread, ('x', 'y'), 0, 0, tiled=True)  9.82 us
    all_to_all x1, waiting for transfers between devices, per_device(): lax.all_to_all(head_values, 'x', 0, 0, tiled=True)  8.35 us
    pallas_call x1, Pallas kernels, attention(): pl.pallas_call(attention_kernel, out_shape=jax.ShapeDtypeStruct((copies,...  7.54 us
    all_to_all x1, starting transfers between devices, per_device(): lax.all_to_all(head_values, 'x', 0, 0, tiled=True)  6.45 us
  transfers between devices with their start and end apart: 5, of which 2 were waited for; matrix products, arithmetic and copies ran while one was open for 10% of the time, Pallas kernels for 0%

profile of v7, /device:TPU:32, one launch (start us, length us, event | category | flops | bytes accessed | tf_op | source)
XLA Modules:
  0.0 163.1 jit_solution(4005188636443495957)
XLA Ops:
  6.5 0.9 copy-done
  7.4 0.9 broadcast_in_dim.122
  8.4 9.8 %all-to-all-start = ((bf16[32,2,32,128]{3,2,1,0:T(8,128)(2,1)}), bf16[32,2,32,128]{3,2,1,0:T(8,128)(2,1)S(1)}, u32[]{:S(2)}, u32[]{:S(2)}) async-start(bf16[32,2,32,128]{3,2,1,0:T(8,128)(2,1)} %broadcast_in_dim.122), calls=%async_computation | async-start | bytes 1048576 | tf_op jit(solution)/shard_map/all_to_all | solution.py:182
  18.2 10.9 %collective-permute-start = (bf16[56,1024]{1,0:T(8,128)(2,1)}, bf16[56,1024]{1,0:T(8,128)(2,1)S(1)}, u32[]{:S(2)}, u32[]{:S(2)}) collective-permute-start(bf16[56,1024]{1,0:T(8,128)(2,1)} %bitcast.79), channel_id=1, source_target_pairs={{0,8},{8,0},{1,9},{9,1},{2,10},{10,2},{3,11},{11,3},{4,12},{12,4},... | collective-permute-start | bytes 344072 | tf_op jit(solution)/shard_map/ppermute | solution.py:176
  29.1 0.8 reshape.251
  30.1 1.3 convert_reduce_fusion.3
  32.2 0.8 select_reduce_fusion.5
  34.1 0.8 select_reduce_fusion.6
  36.2 76.7 %conditional.1 = (bf16[4,128,1024]{2,1,0:T(8,128)(2,1)}, bf16[8,1,56,1024]{3,2,0,1:T(8,128)(2,1)}, bf16[8,1,56,1024]{3,2,0,1:T(8,128)(2,1)}) conditional(s32[]{:T(128)} %clamp.3, (s32[]{:T(128)}, s32[128]{0:T(128)}, s32[8192]{0:T(1024)}, s32[128]{0:T(128)S(1)}, bf16[128,8,512]{2,1,0:T(8,128)(2,1)}, ...), branch_computations={%region_4.8_spmd, %region_8.12_spmd, %region_12.15_spmd} | conditional | flops 6471061504 | bytes 77412304 | solution.py:224
  36.6 0.9 reshape.235
  40.2 0.8 fusion.29
  41.1 1.3 convert_reduce_fusion
  42.5 1.5 copy.46
  44.0 1.3 pad.7.vup_ref
  45.9 28.3 %all-gather = bf16[448,1024]{1,0:T(8,128)(2,1)} all-gather(bf16[56,1024]{1,0:T(8,128)(2,1)S(1)} %copy-done.5), channel_id=2, replica_groups=mesh['x'=4,'y'=8,'zh'=2,'zl'=4,'core'=2] {'y'}, dimensions={0}, use_global_device_ids=true | all-gather | bytes 1032192 | tf_op jit(solution)/shard_map/cond/branch_0_fun/all_gather | solution.py:195
  74.2 28.5 %all-gather.1 = bf16[448,1024]{1,0:T(8,128)(2,1)} all-gather(bf16[56,1024]{1,0:T(8,128)(2,1)S(1)} %get-tuple-element.75), channel_id=3, replica_groups=mesh['x'=4,'y'=8,'zh'=2,'zl'=4,'core'=2] {'y'}, dimensions={0}, use_global_device_ids=true | all-gather | bytes 1032192 | tf_op jit(solution)/shard_map/cond/branch_0_fun/all_gather | solution.py:195
  102.9 2.5 %copy-done.3 = bf16[20480,128]{1,0:T(8,128)(2,1)S(1)} copy-done((bf16[20480,128]{1,0:T(8,128)(2,1)S(1)}, bf16[20480,128]{1,0:T(8,128)(2,1)}, u32[]{:S(2)}) %copy-start.3) | copy-done | bytes 5242904 | tf_op jit(solution)/shard_map/cond
  105.3 7.5 %latent_attention.3 = bf16[4,128,1024]{2,1,0:T(8,128)(2,1)} custom-call(s32[134]{0:T(256)S(1)} %pad_add_fusion.scal, s32[8,128,1]{2,1,0:T(8,128)S(1)} %broadcast_in_dim.78.lo_ref, bf16[8,128,512]{2,1,0:T(8,128)(2,1)S(1)} %bitcast.64, bf16[8,512,128]{2,1,0:T(8,128)(2,1)S(1)} %pad.7.vup_ref, bf16[640,32,128]{2,1,0:T(8,128)(2,1)S(1)} %bitcast.69), custom_call_target="tpu_custom_call" | custom-call | flops 6442450944 | bytes 5242880 | tf_op jit(solution)/shard_map/cond/branch_0_fun/latent_attention/pallas_call | solution.py:103
  112.9 6.5 %all-to-all-start.1 = ((bf16[4,128,1024]{2,1,0:T(8,128)(2,1)}), bf16[4,128,1024]{2,1,0:T(8,128)(2,1)S(1)}, u32[]{:S(2)}, u32[]{:S(2)}) async-start(bf16[4,128,1024]{2,1,0:T(8,128)(2,1)} %get-tuple-element.105), calls=%async_computation.1 | async-start | bytes 2097152 | tf_op jit(solution)/shard_map/all_to_all | solution.py:231
  119.3 2.5 %maximum_select_fusion = bf16[8,2,56,1024]{3,2,1,0:T(8,128)(2,1)S(1)} fusion(bf16[8,1,56,1024]{3,2,1,0:T(8,128)(2,1)} %bitcast.25, bf16[8,1,56,1024]{3,2,1,0:T(8,128)(2,1)} %bitcast.24, pred[]{:T(512)S(6)} %eq.129), kind=kLoop, calls=%fused_computation.93 | loop fusion | flops 2752512 | bytes 3670017 | tf_op jit(solution)/shard_map/jit(_where)/select_n | solution.py:232
  121.9 8.4 %all-to-all-done.1 = bf16[4,128,1024]{2,1,0:T(8,128)(2,1)S(1)} async-done(((bf16[4,128,1024]{2,1,0:T(8,128)(2,1)}), bf16[4,128,1024]{2,1,0:T(8,128)(2,1)S(1)}, u32[]{:S(2)}, u32[]{:S(2)}) %all-to-all-start.1) | async-done | bytes 1048608 | tf_op jit(solution)/shard_map/all_to_all | solution.py:231
  131.1 1.9 %collective-permute-start.1 = (bf16[256,896]{1,0:T(8,128)(2,1)S(1)}, bf16[256,896]{1,0:T(8,128)(2,1)S(1)}, u32[]{:S(2)}, u32[]{:S(2)}) collective-permute-start(bf16[256,896]{1,0:T(8,128)(2,1)S(1)} %convolution_convert_fusion.2), channel_id=1, source_target_pairs={{0,1},{1,0},{2,3},{3,2},{4,5},{5,4},{6,7},{7,6},{8,9},{9,8},{10,11... | collective-permute-start | bytes 1376264 | tf_op jit(solution)/shard_map/ppermute | solution.py:244
  133.7 1.0 collective-permute-done.1
  134.9 20.7 %all_to_all.15 = bf16[16,16,896]{2,1,0:T(8,128)(2,1)S(1)} all-to-all(bf16[16,16,896]{2,1,0:T(8,128)(2,1)S(1)} %bitcast.77), channel_id=1, replica_groups=mesh['x'=4,'y'=8,'zh'=2,'zl'=4,'core'=2] {'x','zl'}, dimensions={0} | all-to-all | bytes 917504 | tf_op jit(solution)/shard_map/all_to_all | solution.py:248
  (45 shorter events, 7.4 us)
Async XLA Ops:
  6.5 0.9 copy-start
  8.4 27.8 %all-to-all-start = ((bf16[32,2,32,128]{3,2,1,0:T(8,128)(2,1)}), bf16[32,2,32,128]{3,2,1,0:T(8,128)(2,1)S(1)}, u32[]{:S(2)}, u32[]{:S(2)}) async-start(bf16[32,2,32,128]{3,2,1,0:T(8,128)(2,1)} %broadcast_in_dim.122), calls=%async_computation | async-start | bytes 1048576 | tf_op jit(solution)/shard_map/all_to_all | solution.py:182
  18.2 18.0 %collective-permute-start = (bf16[56,1024]{1,0:T(8,128)(2,1)}, bf16[56,1024]{1,0:T(8,128)(2,1)S(1)}, u32[]{:S(2)}, u32[]{:S(2)}) collective-permute-start(bf16[56,1024]{1,0:T(8,128)(2,1)} %bitcast.79), channel_id=1, source_target_pairs={{0,8},{8,0},{1,9},{9,1},{2,10},{10,2},{3,11},{11,3},{4,12},{12,4},... | collective-permute-start | bytes 344072 | tf_op jit(solution)/shard_map/ppermute | solution.py:176
  36.2 9.3 %copy-start.8 = (s32[128]{0:T(128)S(1)}, s32[128]{0:T(128)}, u32[]{:S(2)}) copy-start(s32[128]{0:T(128)} %get-tuple-element.64) | copy-start | bytes 1540 | tf_op jit(solution)/shard_map/cond
  36.2 9.7 %copy-start.5 = (bf16[56,1024]{1,0:T(8,128)(2,1)S(1)}, bf16[56,1024]{1,0:T(8,128)(2,1)}, u32[]{:S(2)}) copy-start(bf16[56,1024]{1,0:T(8,128)(2,1)} %get-tuple-element.74) | copy-start | bytes 344068 | tf_op jit(solution)/shard_map/cond
  36.2 66.5 %all-gather.10.cloned.1.call-start = ((), (), s32[]{:S(2)}) async-start(), calls=%async_computation.3 | async-start | bytes 5570560 | tf_op jit(solution)/shard_map/cond/branch_0_fun/all_gather | solution.py:203
  102.8 2.5 %copy-start.3 = (bf16[20480,128]{1,0:T(8,128)(2,1)S(1)}, bf16[20480,128]{1,0:T(8,128)(2,1)}, u32[]{:S(2)}) copy-start(bf16[20480,128]{1,0:T(8,128)(2,1)} %all-gather.10.cloned.1.call-done) | copy-start | bytes 15728644 | tf_op jit(solution)/shard_map/cond
  112.9 17.3 %all-to-all-start.1 = ((bf16[4,128,1024]{2,1,0:T(8,128)(2,1)}), bf16[4,128,1024]{2,1,0:T(8,128)(2,1)S(1)}, u32[]{:S(2)}, u32[]{:S(2)}) async-start(bf16[4,128,1024]{2,1,0:T(8,128)(2,1)} %get-tuple-element.105), calls=%async_computation.1 | async-start | bytes 2097152 | tf_op jit(solution)/shard_map/all_to_all | solution.py:231
  131.1 3.7 %collective-permute-start.1 = (bf16[256,896]{1,0:T(8,128)(2,1)S(1)}, bf16[256,896]{1,0:T(8,128)(2,1)S(1)}, u32[]{:S(2)}, u32[]{:S(2)}) collective-permute-start(bf16[256,896]{1,0:T(8,128)(2,1)S(1)} %convolution_convert_fusion.2), channel_id=1, source_target_pairs={{0,1},{1,0},{2,3},{3,2},{4,5},{5,4},{6,7},{7,6},{8,9},{9,8},{10,11... | collective-permute-start | bytes 1376264 | tf_op jit(solution)/shard_map/ppermute | solution.py:244
Sparse Core Ops, SparseCore 0:
  39.2 46.0 all-gather.9

commit v8 on v7

--- a/solution.py
+++ b/solution.py
@@ -173,7 +173,6 @@
     slices = plane * halves
 
     cols = out_proj.T
-    other = lax.ppermute(cols, "zh", [(i, nzh - 1 - i) for i in range(nzh)])
 
     number = zl * nc + core
     corner = (0, number // across * ROWS, number % across * LANES)
@@ -191,11 +190,16 @@
     pick = (row_rank == jnp.arange(LEVELS[-1], dtype=jnp.int32)[:, None]).astype(jnp.bfloat16)
     pick, my_rank = lax.optimization_barrier((pick, my_rank))
 
-    def over_y(piece):
-        return lax.all_gather(piece, "y", axis=0)
+    def spread_y(piece):
+        return jnp.broadcast_to(piece[None], (ny,) + piece.shape)
+
+    def over_y(spread):
+        return lax.all_to_all(spread, "y", 0, 0, tiled=True)
+
+    cols, ready = lax.optimization_barrier((cols, spread_y(cols)))
 
     def attend(kept, operands):
-        plane_rows, cols, other, query, segment_ids, block_of_slot, value_up, my_rank, pick = operands
+        plane_rows, cols, ready, query, segment_ids, block_of_slot, value_up, my_rank, pick = operands
         few = kept < slices
         sent = plane_rows
         if few:
@@ -203,9 +207,10 @@
         gathered = lax.all_gather(sent.reshape(kept * ROWS, LANES), ("zh", "zl", "core"), axis=0, tiled=True)
         gathered = gathered.reshape(-1, ROWS, LANES)
 
-        cols, other, sent = lax.optimization_barrier((cols, other, sent))
-        mine = over_y(cols)
-        theirs = over_y(other)
+        cols, ready, sent = lax.optimization_barrier((cols, ready, sent))
+        mine = over_y(ready)
+        other = lax.ppermute(cols, "zh", [(i, nzh - 1 - i) for i in range(nzh)])
+        theirs = over_y(spread_y(other))
 
         my_blocks, first, slot_of_block, lo_rows, q, vup = prepare(
             query, segment_ids, block_of_slot, value_up, seq_index
@@ -224,7 +229,7 @@
     head_values, mine, theirs = lax.switch(
         level,
         [functools.partial(attend, kept) for kept in (*LEVELS, slices)],
-        (plane_rows, cols, other, query, segment_ids, block_of_slot, value_up, my_rank, pick),
+        (plane_rows, cols, ready, query, segment_ids, block_of_slot, value_up, my_rank, pick),
     )
 
     wide = head_values.shape[2]

time: 164 us -> 151 us (0.921)
  the two profiles are of different devices: /device:TPU:32 before, /device:TPU:1 now
where the time goes in v8:
time: 151 us; the launch traced here: 149 us
  waiting for transfers between devices  43.6 us (29%)
  starting transfers between devices  41.3 us (27%)
  blocking collectives  18.9 us (13%)
  local copies, waits for them, and re-layouts  14.7 us (10%)
  between operations  14.2 us (9%)
  other arithmetic  7.51 us (5%)
  Pallas kernels  4.55 us (3%)
  matrix products  2.57 us (2%)
    all_to_all x1, blocking collectives, per_device(): terms = lax.all_to_all(chip, ('x', 'zl'), 0, 0, tiled=True)  18.9 us
    all_gather x1, waiting for transfers between devices, attend(): lax.all_gather(sent.reshape(kept * ROWS, LANES), ('zh', 'zl', 'core'), ax...  15 us
    all_to_all x1, waiting for transfers between devices, per_device(): lax.all_to_all(head_values, 'x', 0, 0, tiled=True)  12.3 us
    ppermute x1, starting transfers between devices, attend(): other = lax.ppermute(cols, 'zh', [(i, nzh - 1 - i) for i in range(nzh)])  10.6 us
    all_to_all x1, starting transfers between devices, per_device(): plane_rows = lax.all_to_all(spread, ('x', 'y'), 0, 0, tiled=True)  10.5 us
    all_to_all x2, waiting for transfers between devices, over_y(): return lax.all_to_all(spread, 'y', 0, 0, tiled=True)  10.4 us
    all_to_all x2, starting transfers between devices, over_y(): return lax.all_to_all(spread, 'y', 0, 0, tiled=True)  9.65 us
    all_to_all x1, starting transfers between devices, per_device(): lax.all_to_all(head_values, 'x', 0, 0, tiled=True)  7.28 us
  transfers between devices with their start and end apart: 7, of which 5 were waited for; matrix products, arithmetic and copies ran while one was open for 12% of the time, Pallas kernels for 3%

profile of v8, /device:TPU:1, one launch (start us, length us, event | category | flops | bytes accessed | tf_op | source)
XLA Modules:
  0.0 148.7 jit_solution(16971591756290132285)
XLA Ops:
  6.5 0.9 copy-done
  7.4 0.9 broadcast_in_dim.146
  8.3 10.5 %all-to-all-start.6 = ((bf16[32,2,32,128]{3,2,1,0:T(8,128)(2,1)}), bf16[32,2,32,128]{3,2,1,0:T(8,128)(2,1)S(1)}, u32[]{:S(2)}, u32[]{:S(2)}) async-start(bf16[32,2,32,128]{3,2,1,0:T(8,128)(2,1)} %broadcast_in_dim.146), calls=%async_computation.6 | async-start | bytes 1048576 | tf_op jit(solution)/shard_map/all_to_all | solution.py:181
  18.9 2.0 %broadcast_in_dim.147 = bf16[8,56,1024]{2,1,0:T(8,128)(2,1)} broadcast(bf16[56,1024]{1,0:T(8,128)(2,1)} %bitcast.84), dimensions={1,2} | broadcast | bytes 1032192 | tf_op jit(solution)/shard_map/broadcast_in_dim | solution.py:194
  20.9 0.8 reshape.255
  21.8 1.3 convert_reduce_fusion.3
  24.0 0.8 select_reduce_fusion.5
  27.9 5.3 %all-to-all-done.6 = bf16[32,2,32,128]{3,2,1,0:T(8,128)(2,1)S(1)} async-done(((bf16[32,2,32,128]{3,2,1,0:T(8,128)(2,1)}), bf16[32,2,32,128]{3,2,1,0:T(8,128)(2,1)S(1)}, u32[]{:S(2)}, u32[]{:S(2)}) %all-to-all-start.6) | async-done | bytes 524320 | tf_op jit(solution)/shard_map/all_to_all | solution.py:181
  33.2 61.5 %conditional.1 = (bf16[4,128,1024]{2,1,0:T(8,128)(2,1)}, bf16[8,1,56,1024]{3,2,0,1:T(8,128)(2,1)}, bf16[8,1,56,1024]{3,2,0,1:T(8,128)(2,1)}) conditional(s32[]{:T(128)} %clamp.3, (s32[]{:T(128)}, s32[128]{0:T(128)}, s32[8192]{0:T(1024)}, s32[128]{0:T(128)S(1)}, bf16[128,8,512]{2,1,0:T(8,128)(2,1)}, ...), branch_computations={%region_4.8_spmd, %region_8.12_spmd, %region_12.15_spmd} | conditional | flops 6471061504 | bytes 89880696 | solution.py:229
  33.5 0.9 reshape.239
  34.4 5.4 %all-to-all-start = ((bf16[8,56,1024]{2,1,0:T(8,128)(2,1)}), bf16[8,56,1024]{2,1,0:T(8,128)(2,1)S(1)}, u32[]{:S(2)}, u32[]{:S(2)}) async-start(bf16[8,56,1024]{2,1,0:T(8,128)(2,1)} %get-tuple-element.74), calls=%async_computation | async-start | bytes 1835008 | tf_op jit(solution)/shard_map/cond/branch_0_fun/all_to_all | solution.py:197
  39.8 10.6 %collective-permute-start = (bf16[56,1024]{1,0:T(8,128)(2,1)}, bf16[56,1024]{1,0:T(8,128)(2,1)S(1)}, u32[]{:S(2)}, u32[]{:S(2)}) collective-permute-start(bf16[56,1024]{1,0:T(8,128)(2,1)} %get-tuple-element.75), channel_id=1, source_target_pairs={{0,8},{8,0},{1,9},{9,1},{2,10},{10,2},{3,11},{11,3},{4,12},{12,4},... | collective-permute-start | bytes 344072 | tf_op jit(solution)/shard_map/cond/branch_0_fun/ppermute | solution.py:212
  53.8 10.4 %all-to-all-done = bf16[8,56,1024]{2,1,0:T(8,128)(2,1)S(1)} async-done(((bf16[8,56,1024]{2,1,0:T(8,128)(2,1)}), bf16[8,56,1024]{2,1,0:T(8,128)(2,1)S(1)}, u32[]{:S(2)}, u32[]{:S(2)}) %all-to-all-start) | async-done | bytes 917536 | tf_op jit(solution)/shard_map/cond/branch_0_fun/all_to_all | solution.py:197
  64.2 1.2 broadcast_in_dim.75
  65.4 4.2 %all-to-all-start.1 = ((bf16[8,56,1024]{2,1,0:T(8,128)(2,1)}), bf16[8,56,1024]{2,1,0:T(8,128)(2,1)}, u32[]{:S(2)}, u32[]{:S(2)}) async-start(bf16[8,56,1024]{2,1,0:T(8,128)(2,1)} %broadcast_in_dim.75), calls=%async_computation.1 | async-start | bytes 1835008 | tf_op jit(solution)/shard_map/cond/branch_0_fun/all_to_all | solution.py:197
  70.6 1.3 pad.7.vup_ref
  72.5 15.0 %all-gather.4.cloned.1.call-done = bf16[20480,128]{1,0:T(8,128)(2,1)} async-done(((bf16[1280,128]{1,0:T(8,128)(2,1)}), bf16[20480,128]{1,0:T(8,128)(2,1)}) %all-gather.4.cloned.1.call-update) | async-done | bytes 5242896 | tf_op jit(solution)/shard_map/cond/branch_0_fun/all_gather | solution.py:207
  87.6 2.5 %copy-done.3 = bf16[20480,128]{1,0:T(8,128)(2,1)S(1)} copy-done((bf16[20480,128]{1,0:T(8,128)(2,1)S(1)}, bf16[20480,128]{1,0:T(8,128)(2,1)}, u32[]{:S(2)}) %copy-start.3) | copy-done | bytes 5242904 | tf_op jit(solution)/shard_map/cond
  90.1 4.5 %latent_attention.3 = bf16[4,128,1024]{2,1,0:T(8,128)(2,1)} custom-call(s32[134]{0:T(256)S(1)} %pad_add_fusion.scal, s32[8,128,1]{2,1,0:T(8,128)S(1)} %broadcast_in_dim.74.lo_ref, bf16[8,128,512]{2,1,0:T(8,128)(2,1)S(1)} %bitcast.64, bf16[8,512,128]{2,1,0:T(8,128)(2,1)S(1)} %pad.7.vup_ref, bf16[640,32,128]{2,1,0:T(8,128)(2,1)S(1)} %bitcast.69), custom_call_target="tpu_custom_call" | custom-call | flops 6442450944 | bytes 5242880 | tf_op jit(solution)/shard_map/cond/branch_0_fun/latent_attention/pallas_call | solution.py:103
  94.6 7.3 %all-to-all-start.7 = ((bf16[4,128,1024]{2,1,0:T(8,128)(2,1)}), bf16[4,128,1024]{2,1,0:T(8,128)(2,1)S(1)}, u32[]{:S(2)}, u32[]{:S(2)}) async-start(bf16[4,128,1024]{2,1,0:T(8,128)(2,1)} %get-tuple-element.109), calls=%async_computation.7 | async-start | bytes 2097152 | tf_op jit(solution)/shard_map/all_to_all | solution.py:236
  101.9 2.4 %maximum_select_fusion = bf16[8,2,56,1024]{3,2,1,0:T(8,128)(2,1)S(1)} fusion(bf16[8,1,56,1024]{3,2,1,0:T(8,128)(2,1)} %bitcast.25, bf16[8,1,56,1024]{3,2,1,0:T(8,128)(2,1)} %bitcast.79, pred[]{:T(512)S(6)} %eq.129), kind=kLoop, calls=%fused_computation.93 | loop fusion | flops 2752512 | bytes 3670017 | tf_op jit(solution)/shard_map/jit(_where)/select_n | solution.py:237
  104.3 12.3 %all-to-all-done.7 = bf16[4,128,1024]{2,1,0:T(8,128)(2,1)S(1)} async-done(((bf16[4,128,1024]{2,1,0:T(8,128)(2,1)}), bf16[4,128,1024]{2,1,0:T(8,128)(2,1)S(1)}, u32[]{:S(2)}, u32[]{:S(2)}) %all-to-all-start.7) | async-done | bytes 1048608 | tf_op jit(solution)/shard_map/all_to_all | solution.py:236
  117.4 3.3 %collective-permute-start.3 = (bf16[256,896]{1,0:T(8,128)(2,1)S(1)}, bf16[256,896]{1,0:T(8,128)(2,1)S(1)}, u32[]{:S(2)}, u32[]{:S(2)}) collective-permute-start(bf16[256,896]{1,0:T(8,128)(2,1)S(1)} %convolution_convert_fusion.2), channel_id=1, source_target_pairs={{0,1},{1,0},{2,3},{3,2},{4,5},{5,4},{6,7},{7,6},{8,9},{9,8},{10,11... | collective-permute-start | bytes 1376264 | tf_op jit(solution)/shard_map/ppermute | solution.py:249
  122.2 18.9 %all_to_all.39 = bf16[16,16,896]{2,1,0:T(8,128)(2,1)S(1)} all-to-all(bf16[16,16,896]{2,1,0:T(8,128)(2,1)S(1)} %bitcast.81), channel_id=1, replica_groups=mesh['x'=4,'y'=8,'zh'=2,'zl'=4,'core'=2] {'x','zl'}, dimensions={0} | all-to-all | bytes 917504 | tf_op jit(solution)/shard_map/all_to_all | solution.py:253
  (53 shorter events, 10.6 us)
Async XLA Ops:
  6.5 0.9 copy-start
  8.3 24.8 %all-to-all-start.6 = ((bf16[32,2,32,128]{3,2,1,0:T(8,128)(2,1)}), bf16[32,2,32,128]{3,2,1,0:T(8,128)(2,1)S(1)}, u32[]{:S(2)}, u32[]{:S(2)}) async-start(bf16[32,2,32,128]{3,2,1,0:T(8,128)(2,1)} %broadcast_in_dim.146), calls=%async_computation.6 | async-start | bytes 1048576 | tf_op jit(solution)/shard_map/all_to_all | solution.py:181
  33.2 36.4 %copy-start.11 = (s32[8192]{0:T(1024)S(1)}, s32[8192]{0:T(1024)}, u32[]{:S(2)}) copy-start(s32[8192]{0:T(1024)} %get-tuple-element.66) | copy-start | bytes 98308 | tf_op jit(solution)/shard_map/cond
  33.2 37.1 %copy-start.4 = (bf16[128,8,512]{2,1,0:T(8,128)(2,1)S(1)}, bf16[128,8,512]{2,1,0:T(8,128)(2,1)}, u32[]{:S(2)}) copy-start(bf16[128,8,512]{2,1,0:T(8,128)(2,1)} %get-tuple-element.202) | copy-start | bytes 3145732 | tf_op jit(solution)/shard_map/cond
  33.2 54.3 %all-gather.4.cloned.1.call-start = ((), (), s32[]{:S(2)}) async-start(), calls=%async_computation.9 | async-start | bytes 5570560 | tf_op jit(solution)/shard_map/cond/branch_0_fun/all_gather | solution.py:207
  34.4 37.7 %copy-start.14 = (s32[128]{0:T(128)S(1)}, s32[128]{0:T(128)}, u32[]{:S(2)}) copy-start(s32[128]{0:T(128)} %get-tuple-element.64) | copy-start | bytes 1540 | tf_op jit(solution)/shard_map/cond
  34.4 29.8 %all-to-all-start = ((bf16[8,56,1024]{2,1,0:T(8,128)(2,1)}), bf16[8,56,1024]{2,1,0:T(8,128)(2,1)S(1)}, u32[]{:S(2)}, u32[]{:S(2)}) async-start(bf16[8,56,1024]{2,1,0:T(8,128)(2,1)} %get-tuple-element.74), calls=%async_computation | async-start | bytes 1835008 | tf_op jit(solution)/shard_map/cond/branch_0_fun/all_to_all | solution.py:197
  39.8 14.0 %collective-permute-start = (bf16[56,1024]{1,0:T(8,128)(2,1)}, bf16[56,1024]{1,0:T(8,128)(2,1)S(1)}, u32[]{:S(2)}, u32[]{:S(2)}) collective-permute-start(bf16[56,1024]{1,0:T(8,128)(2,1)} %get-tuple-element.75), channel_id=1, source_target_pairs={{0,8},{8,0},{1,9},{9,1},{2,10},{10,2},{3,11},{11,3},{4,12},{12,4},... | collective-permute-start | bytes 344072 | tf_op jit(solution)/shard_map/cond/branch_0_fun/ppermute | solution.py:212
  64.2 6.1 %copy-start.8 = (bf16[8,56,1024]{2,1,0:T(8,128)(2,1)}, bf16[8,56,1024]{2,1,0:T(8,128)(2,1)S(1)}, u32[]{:S(2)}) copy-start(bf16[8,56,1024]{2,1,0:T(8,128)(2,1)S(1)} %all-to-all-done) | copy-start | bytes 2752516 | tf_op jit(solution)/shard_map/cond
  65.4 29.3 %all-to-all-start.1 = ((bf16[8,56,1024]{2,1,0:T(8,128)(2,1)}), bf16[8,56,1024]{2,1,0:T(8,128)(2,1)}, u32[]{:S(2)}, u32[]{:S(2)}) async-start(bf16[8,56,1024]{2,1,0:T(8,128)(2,1)} %broadcast_in_dim.75), calls=%async_computation.1 | async-start | bytes 1835008 | tf_op jit(solution)/shard_map/cond/branch_0_fun/all_to_all | solution.py:197
  87.6 2.5 %copy-start.3 = (bf16[20480,128]{1,0:T(8,128)(2,1)S(1)}, bf16[20480,128]{1,0:T(8,128)(2,1)}, u32[]{:S(2)}) copy-start(bf16[20480,128]{1,0:T(8,128)(2,1)} %all-gather.4.cloned.1.call-done) | copy-start | bytes 15728644 | tf_op jit(solution)/shard_map/cond
  94.6 21.9 %all-to-all-start.7 = ((bf16[4,128,1024]{2,1,0:T(8,128)(2,1)}), bf16[4,128,1024]{2,1,0:T(8,128)(2,1)S(1)}, u32[]{:S(2)}, u32[]{:S(2)}) async-start(bf16[4,128,1024]{2,1,0:T(8,128)(2,1)} %get-tuple-element.109), calls=%async_computation.7 | async-start | bytes 2097152 | tf_op jit(solution)/shard_map/all_to_all | solution.py:236
  117.4 4.7 %collective-permute-start.3 = (bf16[256,896]{1,0:T(8,128)(2,1)S(1)}, bf16[256,896]{1,0:T(8,128)(2,1)S(1)}, u32[]{:S(2)}, u32[]{:S(2)}) collective-permute-start(bf16[256,896]{1,0:T(8,128)(2,1)S(1)} %convolution_convert_fusion.2), channel_id=1, source_target_pairs={{0,1},{1,0},{2,3},{3,2},{4,5},{5,4},{6,7},{7,6},{8,9},{9,8},{10,11... | collective-permute-start | bytes 1376264 | tf_op jit(solution)/shard_map/ppermute | solution.py:249
Sparse Core Ops, SparseCore 0:
  36.1 51.3 all-gather.3

commit v9 on v8

--- a/solution.py
+++ b/solution.py
@@ -177,8 +177,9 @@
     number = zl * nc + core
     corner = (0, number // across * ROWS, number % across * LANES)
     part = lax.dynamic_slice(latent.reshape(halves, BLK, width), corner, (halves, ROWS, LANES))
-    spread = jnp.broadcast_to(part[None], (plane,) + part.shape)
-    plane_rows = lax.all_to_all(spread, ("x", "y"), 0, 0, tiled=True)
+    line_rows = lax.all_to_all(jnp.broadcast_to(part[None], (ny,) + part.shape), "y", 0, 0, tiled=True)
+    spread = jnp.broadcast_to(line_rows[None], (nx,) + line_rows.shape)
+    plane_rows = lax.all_to_all(spread, "x", 0, 0, tiled=True)
     plane_rows = plane_rows.reshape(slices, ROWS * LANES)
 
     need, rank, level = need_tables(segment_ids, block_of_slot, plane, nzh, halves)

time: 151 us -> 152 us (level)
  starting transfers between devices: 41.3 us -> 39.1 us
  waiting for transfers between devices: 43.6 us -> 45.2 us
    all_gather x1, waiting for transfers between devices: 15 us -> 18.3 us  [attend(): lax.all_gather(sent.reshape(kept * ROWS, LANES), ('zh', 'zl', 'core'), ax...]
    all_to_all x2, waiting for transfers between devices: 10.4 us -> 7.97 us  [over_y(): return lax.all_to_all(spread, 'y', 0, 0, tiled=True)]
    all_to_all x1, starting transfers between devices: 7.28 us -> 5.03 us  [per_device(): lax.all_to_all(head_values, 'x', 0, 0, tiled=True)]
    all_to_all x2, starting transfers between devices: 9.65 us -> 8.12 us  [over_y(): return lax.all_to_all(spread, 'y', 0, 0, tiled=True)]
    all_to_all x1 -> x2, starting transfers between devices: 10.5 us -> 11.4 us  [the longest x1 7.65 us: per_device(): lax.all_to_all(jnp.broadcast_to(part[None], (ny,) + part.shape), 'y', 0,...]
    all_to_all x1 -> x2, waiting for transfers between devices: 5.25 us -> 5.95 us  [the longest x1 3.09 us: per_device(): lax.all_to_all(jnp.broadcast_to(part[None], (ny,) + part.shape), 'y', 0,...]
  transfers between devices with their start and end apart: 7 -> 8, of which waited for: 5 -> 6; matrix products, arithmetic and copies ran while one was open for 12% -> 12% of each run, Pallas kernels for 3% -> 3%
where the time goes in v9:
time: 152 us; the launch traced here: 150 us
  waiting for transfers between devices  45.2 us (30%)
  starting transfers between devices  39.1 us (26%)
  blocking collectives  19.1 us (13%)
  local copies, waits for them, and re-layouts  15.4 us (10%)
  between operations  14.2 us (9%)
  other arithmetic  7.5 us (5%)
  Pallas kernels  5.17 us (3%)
  matrix products  2.57 us (2%)
    all_to_all x1, blocking collectives, per_device(): terms = lax.all_to_all(chip, ('x', 'zl'), 0, 0, tiled=True)  19.1 us
    all_gather x1, waiting for transfers between devices, attend(): lax.all_gather(sent.reshape(kept * ROWS, LANES), ('zh', 'zl', 'core'), ax...  18.3 us
    all_to_all x1, waiting for transfers between devices, per_device(): lax.all_to_all(head_values, 'x', 0, 0, tiled=True)  12.4 us
    ppermute x1, starting transfers between devices, attend(): other = lax.ppermute(cols, 'zh', [(i, nzh - 1 - i) for i in range(nzh)])  11.3 us
    all_to_all x2, starting transfers between devices, over_y(): return lax.all_to_all(spread, 'y', 0, 0, tiled=True)  8.12 us
    all_to_all x2, waiting for transfers between devices, over_y(): return lax.all_to_all(spread, 'y', 0, 0, tiled=True)  7.97 us
    all_to_all x1, starting transfers between devices, per_device(): lax.all_to_all(jnp.broadcast_to(part[None], (ny,) + part.shape), 'y', 0,...  7.65 us
    pallas_call x1, Pallas kernels, attention(): pl.pallas_call(attention_kernel, out_shape=jax.ShapeDtypeStruct((copies,...  5.17 us
  transfers between devices with their start and end apart: 8, of which 6 were waited for; matrix products, arithmetic and copies ran while one was open for 12% of the time, Pallas kernels for 3%

profile of v9, /device:TPU:1, one launch (start us, length us, event | category | flops | bytes accessed | tf_op | source)
XLA Modules:
  0.0 149.6 jit_solution(3449424086376219002)
XLA Ops:
  6.5 0.9 copy-done
  8.1 7.7 %all-to-all-start.6 = ((bf16[8,2,32,128]{3,2,1,0:T(8,128)(2,1)}), bf16[8,2,32,128]{3,2,1,0:T(8,128)(2,1)S(1)}, u32[]{:S(2)}, u32[]{:S(2)}) async-start(bf16[8,2,32,128]{3,2,1,0:T(8,128)(2,1)} %broadcast_in_dim.152), calls=%async_computation.6 | async-start | bytes 262144 | tf_op jit(solution)/shard_map/all_to_all | solution.py:180
  16.7 1.3 convert_reduce_fusion.3
  20.7 3.1 %all-to-all-done.6 = bf16[8,2,32,128]{3,2,1,0:T(8,128)(2,1)S(1)} async-done(((bf16[8,2,32,128]{3,2,1,0:T(8,128)(2,1)}), bf16[8,2,32,128]{3,2,1,0:T(8,128)(2,1)S(1)}, u32[]{:S(2)}, u32[]{:S(2)}) %all-to-all-start.6) | async-done | bytes 131104 | tf_op jit(solution)/shard_map/all_to_all | solution.py:180
  23.8 0.9 broadcast_in_dim.153
  24.7 3.8 %all-to-all-start.7 = ((bf16[4,8,2,32,128]{4,3,2,1,0:T(8,128)(2,1)}), bf16[4,8,2,32,128]{4,3,2,1,0:T(8,128)(2,1)S(1)}, u32[]{:S(2)}, u32[]{:S(2)}) async-start(bf16[4,8,2,32,128]{4,3,2,1,0:T(8,128)(2,1)} %broadcast_in_dim.153), calls=%async_computation.7 | async-start | bytes 1048576 | tf_op jit(solution)/shard_map/all_to_all | solution.py:182
  29.3 2.0 %broadcast_in_dim.154 = bf16[8,56,1024]{2,1,0:T(8,128)(2,1)} broadcast(bf16[56,1024]{1,0:T(8,128)(2,1)} %bitcast.84), dimensions={1,2} | broadcast | bytes 1032192 | tf_op jit(solution)/shard_map/broadcast_in_dim | solution.py:195
  32.5 2.9 %all-to-all-done.7 = bf16[4,8,2,32,128]{4,3,2,1,0:T(8,128)(2,1)S(1)} async-done(((bf16[4,8,2,32,128]{4,3,2,1,0:T(8,128)(2,1)}), bf16[4,8,2,32,128]{4,3,2,1,0:T(8,128)(2,1)S(1)}, u32[]{:S(2)}, u32[]{:S(2)}) %all-to-all-start.7) | async-done | bytes 524320 | tf_op jit(solution)/shard_map/all_to_all | solution.py:182
  35.4 62.2 %conditional.1 = (bf16[4,128,1024]{2,1,0:T(8,128)(2,1)}, bf16[8,1,56,1024]{3,2,0,1:T(8,128)(2,1)}, bf16[8,1,56,1024]{3,2,0,1:T(8,128)(2,1)}) conditional(s32[]{:T(128)} %clamp.3, (s32[]{:T(128)}, s32[128]{0:T(128)}, s32[8192]{0:T(1024)}, s32[128]{0:T(128)S(1)}, bf16[128,8,512]{2,1,0:T(8,128)(2,1)}, ...), branch_computations={%region_4.8_spmd, %region_8.12_spmd, %region_12.15_spmd} | conditional | flops 6471061504 | bytes 89880696 | solution.py:230
  35.7 0.9 reshape.240
  36.6 3.9 %all-to-all-start = ((bf16[8,56,1024]{2,1,0:T(8,128)(2,1)}), bf16[8,56,1024]{2,1,0:T(8,128)(2,1)S(1)}, u32[]{:S(2)}, u32[]{:S(2)}) async-start(bf16[8,56,1024]{2,1,0:T(8,128)(2,1)} %get-tuple-element.74), calls=%async_computation | async-start | bytes 1835008 | tf_op jit(solution)/shard_map/cond/branch_0_fun/all_to_all | solution.py:198
  40.5 11.3 %collective-permute-start = (bf16[56,1024]{1,0:T(8,128)(2,1)}, bf16[56,1024]{1,0:T(8,128)(2,1)S(1)}, u32[]{:S(2)}, u32[]{:S(2)}) collective-permute-start(bf16[56,1024]{1,0:T(8,128)(2,1)} %get-tuple-element.75), channel_id=1, source_target_pairs={{0,8},{8,0},{1,9},{9,1},{2,10},{10,2},{3,11},{11,3},{4,12},{12,4},... | collective-permute-start | bytes 344072 | tf_op jit(solution)/shard_map/cond/branch_0_fun/ppermute | solution.py:213
  55.2 8.0 %all-to-all-done = bf16[8,56,1024]{2,1,0:T(8,128)(2,1)S(1)} async-done(((bf16[8,56,1024]{2,1,0:T(8,128)(2,1)}), bf16[8,56,1024]{2,1,0:T(8,128)(2,1)S(1)}, u32[]{:S(2)}, u32[]{:S(2)}) %all-to-all-start) | async-done | bytes 917536 | tf_op jit(solution)/shard_map/cond/branch_0_fun/all_to_all | solution.py:198
  63.2 1.2 broadcast_in_dim.76
  64.4 4.2 %all-to-all-start.1 = ((bf16[8,56,1024]{2,1,0:T(8,128)(2,1)}), bf16[8,56,1024]{2,1,0:T(8,128)(2,1)}, u32[]{:S(2)}, u32[]{:S(2)}) async-start(bf16[8,56,1024]{2,1,0:T(8,128)(2,1)} %broadcast_in_dim.76), calls=%async_computation.1 | async-start | bytes 1835008 | tf_op jit(solution)/shard_map/cond/branch_0_fun/all_to_all | solution.py:198
  69.7 1.3 pad.7.vup_ref
  71.5 18.3 %all-gather.4.cloned.1.call-done = bf16[20480,128]{1,0:T(8,128)(2,1)} async-done(((bf16[1280,128]{1,0:T(8,128)(2,1)}), bf16[20480,128]{1,0:T(8,128)(2,1)}) %all-gather.4.cloned.1.call-update) | async-done | bytes 5242896 | tf_op jit(solution)/shard_map/cond/branch_0_fun/all_gather | solution.py:208
  89.9 2.5 %copy-done.3 = bf16[20480,128]{1,0:T(8,128)(2,1)S(1)} copy-done((bf16[20480,128]{1,0:T(8,128)(2,1)S(1)}, bf16[20480,128]{1,0:T(8,128)(2,1)}, u32[]{:S(2)}) %copy-start.3) | copy-done | bytes 5242904 | tf_op jit(solution)/shard_map/cond
  92.4 5.2 %latent_attention.3 = bf16[4,128,1024]{2,1,0:T(8,128)(2,1)} custom-call(s32[134]{0:T(256)S(1)} %pad_add_fusion.scal, s32[8,128,1]{2,1,0:T(8,128)S(1)} %broadcast_in_dim.75.lo_ref, bf16[8,128,512]{2,1,0:T(8,128)(2,1)S(1)} %bitcast.64, bf16[8,512,128]{2,1,0:T(8,128)(2,1)S(1)} %pad.7.vup_ref, bf16[640,32,128]{2,1,0:T(8,128)(2,1)S(1)} %bitcast.69), custom_call_target="tpu_custom_call" | custom-call | flops 6442450944 | bytes 5242880 | tf_op jit(solution)/shard_map/cond/branch_0_fun/latent_attention/pallas_call | solution.py:103
  97.6 5.0 %all-to-all-start.8 = ((bf16[4,128,1024]{2,1,0:T(8,128)(2,1)}), bf16[4,128,1024]{2,1,0:T(8,128)(2,1)S(1)}, u32[]{:S(2)}, u32[]{:S(2)}) async-start(bf16[4,128,1024]{2,1,0:T(8,128)(2,1)} %get-tuple-element.109), calls=%async_computation.8 | async-start | bytes 2097152 | tf_op jit(solution)/shard_map/all_to_all | solution.py:237
  102.6 2.3 %maximum_select_fusion = bf16[8,2,56,1024]{3,2,1,0:T(8,128)(2,1)S(1)} fusion(bf16[8,1,56,1024]{3,2,1,0:T(8,128)(2,1)} %bitcast.25, bf16[8,1,56,1024]{3,2,1,0:T(8,128)(2,1)} %bitcast.79, pred[]{:T(512)S(6)} %eq.129), kind=kLoop, calls=%fused_computation.93 | loop fusion | flops 2752512 | bytes 3670017 | tf_op jit(solution)/shard_map/jit(_where)/select_n | solution.py:238
  105.0 12.4 %all-to-all-done.8 = bf16[4,128,1024]{2,1,0:T(8,128)(2,1)S(1)} async-done(((bf16[4,128,1024]{2,1,0:T(8,128)(2,1)}), bf16[4,128,1024]{2,1,0:T(8,128)(2,1)S(1)}, u32[]{:S(2)}, u32[]{:S(2)}) %all-to-all-start.8) | async-done | bytes 1048608 | tf_op jit(solution)/shard_map/all_to_all | solution.py:237
  118.2 3.2 %collective-permute-start.3 = (bf16[256,896]{1,0:T(8,128)(2,1)S(1)}, bf16[256,896]{1,0:T(8,128)(2,1)S(1)}, u32[]{:S(2)}, u32[]{:S(2)}) collective-permute-start(bf16[256,896]{1,0:T(8,128)(2,1)S(1)} %convolution_convert_fusion.2), channel_id=1, source_target_pairs={{0,1},{1,0},{2,3},{3,2},{4,5},{5,4},{6,7},{7,6},{8,9},{9,8},{10,11... | collective-permute-start | bytes 1376264 | tf_op jit(solution)/shard_map/ppermute | solution.py:250
  123.0 19.1 %all_to_all.44 = bf16[16,16,896]{2,1,0:T(8,128)(2,1)S(1)} all-to-all(bf16[16,16,896]{2,1,0:T(8,128)(2,1)S(1)} %bitcast.81), channel_id=1, replica_groups=mesh['x'=4,'y'=8,'zh'=2,'zl'=4,'core'=2] {'x','zl'}, dimensions={0} | all-to-all | bytes 917504 | tf_op jit(solution)/shard_map/all_to_all | solution.py:254
  (56 shorter events, 12.9 us)
Async XLA Ops:
  6.5 0.9 copy-start
  8.1 15.7 %all-to-all-start.6 = ((bf16[8,2,32,128]{3,2,1,0:T(8,128)(2,1)}), bf16[8,2,32,128]{3,2,1,0:T(8,128)(2,1)S(1)}, u32[]{:S(2)}, u32[]{:S(2)}) async-start(bf16[8,2,32,128]{3,2,1,0:T(8,128)(2,1)} %broadcast_in_dim.152), calls=%async_computation.6 | async-start | bytes 262144 | tf_op jit(solution)/shard_map/all_to_all | solution.py:180
  24.7 10.7 %all-to-all-start.7 = ((bf16[4,8,2,32,128]{4,3,2,1,0:T(8,128)(2,1)}), bf16[4,8,2,32,128]{4,3,2,1,0:T(8,128)(2,1)S(1)}, u32[]{:S(2)}, u32[]{:S(2)}) async-start(bf16[4,8,2,32,128]{4,3,2,1,0:T(8,128)(2,1)} %broadcast_in_dim.153), calls=%async_computation.7 | async-start | bytes 1048576 | tf_op jit(solution)/shard_map/all_to_all | solution.py:182
  35.4 33.2 %copy-start.11 = (s32[8192]{0:T(1024)S(1)}, s32[8192]{0:T(1024)}, u32[]{:S(2)}) copy-start(s32[8192]{0:T(1024)} %get-tuple-element.66) | copy-start | bytes 98308 | tf_op jit(solution)/shard_map/cond
  35.4 33.9 %copy-start.4 = (bf16[128,8,512]{2,1,0:T(8,128)(2,1)S(1)}, bf16[128,8,512]{2,1,0:T(8,128)(2,1)}, u32[]{:S(2)}) copy-start(bf16[128,8,512]{2,1,0:T(8,128)(2,1)} %get-tuple-element.202) | copy-start | bytes 3145732 | tf_op jit(solution)/shard_map/cond
  35.4 54.4 %all-gather.4.cloned.1.call-start = ((), (), s32[]{:S(2)}) async-start(), calls=%async_computation.10 | async-start | bytes 5570560 | tf_op jit(solution)/shard_map/cond/branch_0_fun/all_gather | solution.py:208
  36.6 34.5 %copy-start.14 = (s32[128]{0:T(128)S(1)}, s32[128]{0:T(128)}, u32[]{:S(2)}) copy-start(s32[128]{0:T(128)} %get-tuple-element.64) | copy-start | bytes 1540 | tf_op jit(solution)/shard_map/cond
  36.6 26.6 %all-to-all-start = ((bf16[8,56,1024]{2,1,0:T(8,128)(2,1)}), bf16[8,56,1024]{2,1,0:T(8,128)(2,1)S(1)}, u32[]{:S(2)}, u32[]{:S(2)}) async-start(bf16[8,56,1024]{2,1,0:T(8,128)(2,1)} %get-tuple-element.74), calls=%async_computation | async-start | bytes 1835008 | tf_op jit(solution)/shard_map/cond/branch_0_fun/all_to_all | solution.py:198
  40.5 14.7 %collective-permute-start = (bf16[56,1024]{1,0:T(8,128)(2,1)}, bf16[56,1024]{1,0:T(8,128)(2,1)S(1)}, u32[]{:S(2)}, u32[]{:S(2)}) collective-permute-start(bf16[56,1024]{1,0:T(8,128)(2,1)} %get-tuple-element.75), channel_id=1, source_target_pairs={{0,8},{8,0},{1,9},{9,1},{2,10},{10,2},{3,11},{11,3},{4,12},{12,4},... | collective-permute-start | bytes 344072 | tf_op jit(solution)/shard_map/cond/branch_0_fun/ppermute | solution.py:213
  63.2 6.1 %copy-start.8 = (bf16[8,56,1024]{2,1,0:T(8,128)(2,1)}, bf16[8,56,1024]{2,1,0:T(8,128)(2,1)S(1)}, u32[]{:S(2)}) copy-start(bf16[8,56,1024]{2,1,0:T(8,128)(2,1)S(1)} %all-to-all-done) | copy-start | bytes 2752516 | tf_op jit(solution)/shard_map/cond
  64.4 33.2 %all-to-all-start.1 = ((bf16[8,56,1024]{2,1,0:T(8,128)(2,1)}), bf16[8,56,1024]{2,1,0:T(8,128)(2,1)}, u32[]{:S(2)}, u32[]{:S(2)}) async-start(bf16[8,56,1024]{2,1,0:T(8,128)(2,1)} %broadcast_in_dim.76), calls=%async_computation.1 | async-start | bytes 1835008 | tf_op jit(solution)/shard_map/cond/branch_0_fun/all_to_all | solution.py:198
  89.9 2.5 %copy-start.3 = (bf16[20480,128]{1,0:T(8,128)(2,1)S(1)}, bf16[20480,128]{1,0:T(8,128)(2,1)}, u32[]{:S(2)}) copy-start(bf16[20480,128]{1,0:T(8,128)(2,1)} %all-gather.4.cloned.1.call-done) | copy-start | bytes 15728644 | tf_op jit(solution)/shard_map/cond
  97.6 19.7 %all-to-all-start.8 = ((bf16[4,128,1024]{2,1,0:T(8,128)(2,1)}), bf16[4,128,1024]{2,1,0:T(8,128)(2,1)S(1)}, u32[]{:S(2)}, u32[]{:S(2)}) async-start(bf16[4,128,1024]{2,1,0:T(8,128)(2,1)} %get-tuple-element.109), calls=%async_computation.8 | async-start | bytes 2097152 | tf_op jit(solution)/shard_map/all_to_all | solution.py:237
  118.2 4.7 %collective-permute-start.3 = (bf16[256,896]{1,0:T(8,128)(2,1)S(1)}, bf16[256,896]{1,0:T(8,128)(2,1)S(1)}, u32[]{:S(2)}, u32[]{:S(2)}) collective-permute-start(bf16[256,896]{1,0:T(8,128)(2,1)S(1)} %convolution_convert_fusion.2), channel_id=1, source_target_pairs={{0,1},{1,0},{2,3},{3,2},{4,5},{5,4},{6,7},{7,6},{8,9},{9,8},{10,11... | collective-permute-start | bytes 1376264 | tf_op jit(solution)/shard_map/ppermute | solution.py:250
Sparse Core Ops, SparseCore 0:
  38.3 51.4 all-gather.3

commit v10 on v8

--- a/solution.py
+++ b/solution.py
@@ -178,15 +178,15 @@
     corner = (0, number // across * ROWS, number % across * LANES)
     part = lax.dynamic_slice(latent.reshape(halves, BLK, width), corner, (halves, ROWS, LANES))
     spread = jnp.broadcast_to(part[None], (plane,) + part.shape)
-    plane_rows = lax.all_to_all(spread, ("x", "y"), 0, 0, tiled=True)
+    plane_rows = lax.all_to_all(spread, ("y", "x"), 0, 0, tiled=True)
     plane_rows = plane_rows.reshape(slices, ROWS * LANES)
 
     need, rank, level = need_tables(segment_ids, block_of_slot, plane, nzh, halves)
     my_need = lax.dynamic_index_in_dim(need, x * ny + y, 0, keepdims=False)
     my_rank = lax.dynamic_index_in_dim(rank, x * ny + y, 0, keepdims=False).astype(jnp.int32)
-    row_need = lax.dynamic_index_in_dim(my_need.reshape(plane, nzh, halves), zh, 1, keepdims=False)
-    row_rank = lax.dynamic_index_in_dim(my_rank.reshape(plane, nzh, halves), zh, 1, keepdims=False)
-    row_rank = jnp.where(row_need, row_rank, -1).reshape(1, slices)
+    row_rank = jnp.where(my_need, my_rank, -1).reshape(plane, nzh, halves)
+    row_rank = lax.dynamic_index_in_dim(row_rank, zh, 1, keepdims=False)
+    row_rank = row_rank.reshape(nx, ny, halves).transpose(1, 0, 2).reshape(1, slices)
     pick = (row_rank == jnp.arange(LEVELS[-1], dtype=jnp.int32)[:, None]).astype(jnp.bfloat16)
     pick, my_rank = lax.optimization_barrier((pick, my_rank))
 
@@ -221,7 +221,8 @@
             place = jnp.sum(jnp.where(slot_of_block[:, None] == slots[None, :], my_rank[None, :], 0), axis=1)
             place = jnp.minimum(place, kept - 1)
         else:
-            place = slot_seq // nzh * halves + slot_half
+            column = slot_seq // nzh
+            place = (column % ny * nx + column // ny) * halves + slot_half
         start = (slot_seq % nzh) * PARTS * kept + place
         scal = jnp.concatenate([my_blocks, first, start]).astype(jnp.int32)
         return attention(scal, lo_rows, q, vup, gathered, nx), mine, theirs

time: 151 us -> 152 us (level)
  the two profiles are of different devices: /device:TPU:1 before, /device:TPU:8 now
where the time goes in v10:
time: 152 us; the launch traced here: 151 us
  waiting for transfers between devices  44.3 us (29%)
  starting transfers between devices  41.2 us (27%)
  blocking collectives  20.7 us (14%)
  local copies, waits for them, and re-layouts  14.7 us (10%)
  between operations  14.2 us (9%)
  other arithmetic  7.4 us (5%)
  Pallas kernels  4.54 us (3%)
  matrix products  2.57 us (2%)
    all_to_all x1, blocking collectives, per_device(): terms = lax.all_to_all(chip, ('x', 'zl'), 0, 0, tiled=True)  20.7 us
    all_to_all x1, waiting for transfers between devices, per_device(): lax.all_to_all(head_values, 'x', 0, 0, tiled=True)  13.2 us
    all_gather x1, waiting for transfers between devices, attend(): lax.all_gather(sent.reshape(kept * ROWS, LANES), ('zh', 'zl', 'core'), ax...  12.6 us
    ppermute x1, starting transfers between devices, attend(): other = lax.ppermute(cols, 'zh', [(i, nzh - 1 - i) for i in range(nzh)])  10.9 us
    all_to_all x1, starting transfers between devices, per_device(): plane_rows = lax.all_to_all(spread, ('y', 'x'), 0, 0, tiled=True)  10.2 us
    all_to_all x2, starting transfers between devices, over_y(): return lax.all_to_all(spread, 'y', 0, 0, tiled=True)  9.76 us
    all_to_all x1, starting transfers between devices, per_device(): lax.all_to_all(head_values, 'x', 0, 0, tiled=True)  8.48 us
    all_to_all x1, waiting for transfers between devices, per_device(): plane_rows = lax.all_to_all(spread, ('y', 'x'), 0, 0, tiled=True)  8.37 us
  transfers between devices with their start and end apart: 7, of which 7 were waited for; matrix products, arithmetic and copies ran while one was open for 12% of the time, Pallas kernels for 3%

profile of v10, /device:TPU:8, one launch (start us, length us, event | category | flops | bytes accessed | tf_op | source)
XLA Modules:
  0.0 151.2 jit_solution(15541147795950178279)
XLA Ops:
  6.5 0.9 copy-done
  7.4 0.9 broadcast_in_dim.146
  8.4 10.2 %all-to-all-start.6 = ((bf16[32,2,32,128]{3,2,1,0:T(8,128)(2,1)}), bf16[32,2,32,128]{3,2,1,0:T(8,128)(2,1)S(1)}, u32[]{:S(2)}, u32[]{:S(2)}) async-start(bf16[32,2,32,128]{3,2,1,0:T(8,128)(2,1)} %broadcast_in_dim.146), calls=%async_computation.6 | async-start | bytes 1048576 | tf_op jit(solution)/shard_map/all_to_all | solution.py:181
  19.5 1.3 convert_reduce_fusion.3
  20.8 2.0 %broadcast_in_dim.147 = bf16[8,56,1024]{2,1,0:T(8,128)(2,1)} broadcast(bf16[56,1024]{1,0:T(8,128)(2,1)} %bitcast.89), dimensions={1,2} | broadcast | bytes 1032192 | tf_op jit(solution)/shard_map/broadcast_in_dim | solution.py:194
  27.4 8.4 %all-to-all-done.6 = bf16[32,2,32,128]{3,2,1,0:T(8,128)(2,1)S(1)} async-done(((bf16[32,2,32,128]{3,2,1,0:T(8,128)(2,1)}), bf16[32,2,32,128]{3,2,1,0:T(8,128)(2,1)S(1)}, u32[]{:S(2)}, u32[]{:S(2)}) %all-to-all-start.6) | async-done | bytes 524320 | tf_op jit(solution)/shard_map/all_to_all | solution.py:181
  35.7 58.5 %conditional.1 = (bf16[4,128,1024]{2,1,0:T(8,128)(2,1)}, bf16[8,1,56,1024]{3,2,0,1:T(8,128)(2,1)}, bf16[8,1,56,1024]{3,2,0,1:T(8,128)(2,1)}) conditional(s32[]{:T(128)} %clamp.3, (s32[]{:T(128)}, s32[128]{0:T(128)}, s32[8192]{0:T(1024)}, s32[128]{0:T(128)S(1)}, bf16[128,8,512]{2,1,0:T(8,128)(2,1)}, ...), branch_computations={%region_4.8_spmd, %region_8.12_spmd, %region_12.15_spmd} | conditional | flops 6471061504 | bytes 89880696 | solution.py:230
  36.0 0.9 reshape.232
  37.0 4.2 %all-to-all-start = ((bf16[8,56,1024]{2,1,0:T(8,128)(2,1)}), bf16[8,56,1024]{2,1,0:T(8,128)(2,1)S(1)}, u32[]{:S(2)}, u32[]{:S(2)}) async-start(bf16[8,56,1024]{2,1,0:T(8,128)(2,1)} %get-tuple-element.74), calls=%async_computation | async-start | bytes 1835008 | tf_op jit(solution)/shard_map/cond/branch_0_fun/all_to_all | solution.py:197
  41.2 10.9 %collective-permute-start = (bf16[56,1024]{1,0:T(8,128)(2,1)}, bf16[56,1024]{1,0:T(8,128)(2,1)S(1)}, u32[]{:S(2)}, u32[]{:S(2)}) collective-permute-start(bf16[56,1024]{1,0:T(8,128)(2,1)} %get-tuple-element.75), channel_id=1, source_target_pairs={{0,8},{8,0},{1,9},{9,1},{2,10},{10,2},{3,11},{11,3},{4,12},{12,4},... | collective-permute-start | bytes 344072 | tf_op jit(solution)/shard_map/cond/branch_0_fun/ppermute | solution.py:212
  55.7 2.3 %collective-permute-done = bf16[56,1024]{1,0:T(8,128)(2,1)S(1)} collective-permute-done((bf16[56,1024]{1,0:T(8,128)(2,1)}, bf16[56,1024]{1,0:T(8,128)(2,1)S(1)}, u32[]{:S(2)}, u32[]{:S(2)}) %collective-permute-start) | collective-permute-done | bytes 114720 | tf_op jit(solution)/shard_map/cond/branch_0_fun/ppermute | solution.py:212
  58.0 6.2 %all-to-all-done = bf16[8,56,1024]{2,1,0:T(8,128)(2,1)S(1)} async-done(((bf16[8,56,1024]{2,1,0:T(8,128)(2,1)}), bf16[8,56,1024]{2,1,0:T(8,128)(2,1)S(1)}, u32[]{:S(2)}, u32[]{:S(2)}) %all-to-all-start) | async-done | bytes 917536 | tf_op jit(solution)/shard_map/cond/branch_0_fun/all_to_all | solution.py:197
  64.2 1.2 broadcast_in_dim.75
  65.4 5.5 %all-to-all-start.1 = ((bf16[8,56,1024]{2,1,0:T(8,128)(2,1)}), bf16[8,56,1024]{2,1,0:T(8,128)(2,1)}, u32[]{:S(2)}, u32[]{:S(2)}) async-start(bf16[8,56,1024]{2,1,0:T(8,128)(2,1)} %broadcast_in_dim.75), calls=%async_computation.1 | async-start | bytes 1835008 | tf_op jit(solution)/shard_map/cond/branch_0_fun/all_to_all | solution.py:197
  72.0 1.3 pad.7.vup_ref
  73.9 12.6 %all-gather.4.cloned.1.call-done = bf16[20480,128]{1,0:T(8,128)(2,1)} async-done(((bf16[1280,128]{1,0:T(8,128)(2,1)}), bf16[20480,128]{1,0:T(8,128)(2,1)}) %all-gather.4.cloned.1.call-update) | async-done | bytes 5242896 | tf_op jit(solution)/shard_map/cond/branch_0_fun/all_gather | solution.py:207
  86.6 2.5 %copy-done.3 = bf16[20480,128]{1,0:T(8,128)(2,1)S(1)} copy-done((bf16[20480,128]{1,0:T(8,128)(2,1)S(1)}, bf16[20480,128]{1,0:T(8,128)(2,1)}, u32[]{:S(2)}) %copy-start.3) | copy-done | bytes 5242904 | tf_op jit(solution)/shard_map/cond
  89.1 4.5 %latent_attention.3 = bf16[4,128,1024]{2,1,0:T(8,128)(2,1)} custom-call(s32[134]{0:T(256)S(1)} %pad_add_fusion.scal, s32[8,128,1]{2,1,0:T(8,128)S(1)} %broadcast_in_dim.74.lo_ref, bf16[8,128,512]{2,1,0:T(8,128)(2,1)S(1)} %bitcast.69, bf16[8,512,128]{2,1,0:T(8,128)(2,1)S(1)} %pad.7.vup_ref, bf16[640,32,128]{2,1,0:T(8,128)(2,1)S(1)} %bitcast.74), custom_call_target="tpu_custom_call" | custom-call | flops 6442450944 | bytes 5242880 | tf_op jit(solution)/shard_map/cond/branch_0_fun/latent_attention/pallas_call | solution.py:103
  94.2 8.5 %all-to-all-start.7 = ((bf16[4,128,1024]{2,1,0:T(8,128)(2,1)}), bf16[4,128,1024]{2,1,0:T(8,128)(2,1)S(1)}, u32[]{:S(2)}, u32[]{:S(2)}) async-start(bf16[4,128,1024]{2,1,0:T(8,128)(2,1)} %get-tuple-element.109), calls=%async_computation.7 | async-start | bytes 2097152 | tf_op jit(solution)/shard_map/all_to_all | solution.py:237
  102.7 2.3 %maximum_select_fusion = bf16[8,2,56,1024]{3,2,1,0:T(8,128)(2,1)S(1)} fusion(bf16[8,1,56,1024]{3,2,1,0:T(8,128)(2,1)} %bitcast.28, bf16[8,1,56,1024]{3,2,1,0:T(8,128)(2,1)} %bitcast.84, pred[]{:T(512)S(6)} %eq.133), kind=kLoop, calls=%fused_computation.100 | loop fusion | flops 2752512 | bytes 3670017 | tf_op jit(solution)/shard_map/jit(_where)/select_n | solution.py:238
  105.0 13.2 %all-to-all-done.7 = bf16[4,128,1024]{2,1,0:T(8,128)(2,1)S(1)} async-done(((bf16[4,128,1024]{2,1,0:T(8,128)(2,1)}), bf16[4,128,1024]{2,1,0:T(8,128)(2,1)S(1)}, u32[]{:S(2)}, u32[]{:S(2)}) %all-to-all-start.7) | async-done | bytes 1048608 | tf_op jit(solution)/shard_map/all_to_all | solution.py:237
  119.1 1.9 %collective-permute-start.3 = (bf16[256,896]{1,0:T(8,128)(2,1)S(1)}, bf16[256,896]{1,0:T(8,128)(2,1)S(1)}, u32[]{:S(2)}, u32[]{:S(2)}) collective-permute-start(bf16[256,896]{1,0:T(8,128)(2,1)S(1)} %convolution_convert_fusion.2), channel_id=1, source_target_pairs={{0,1},{1,0},{2,3},{3,2},{4,5},{5,4},{6,7},{7,6},{8,9},{9,8},{10,11... | collective-permute-start | bytes 1376264 | tf_op jit(solution)/shard_map/ppermute | solution.py:250
  121.7 1.0 collective-permute-done.3
  122.9 20.7 %all_to_all.39 = bf16[16,16,896]{2,1,0:T(8,128)(2,1)S(1)} all-to-all(bf16[16,16,896]{2,1,0:T(8,128)(2,1)S(1)} %bitcast.86), channel_id=1, replica_groups=mesh['x'=4,'y'=8,'zh'=2,'zl'=4,'core'=2] {'x','zl'}, dimensions={0} | all-to-all | bytes 917504 | tf_op jit(solution)/shard_map/all_to_all | solution.py:254
  (52 shorter events, 12.0 us)
Async XLA Ops:
  6.5 0.9 copy-start
  8.4 27.4 %all-to-all-start.6 = ((bf16[32,2,32,128]{3,2,1,0:T(8,128)(2,1)}), bf16[32,2,32,128]{3,2,1,0:T(8,128)(2,1)S(1)}, u32[]{:S(2)}, u32[]{:S(2)}) async-start(bf16[32,2,32,128]{3,2,1,0:T(8,128)(2,1)} %broadcast_in_dim.146), calls=%async_computation.6 | async-start | bytes 1048576 | tf_op jit(solution)/shard_map/all_to_all | solution.py:181
  35.7 35.2 %copy-start.11 = (s32[8192]{0:T(1024)S(1)}, s32[8192]{0:T(1024)}, u32[]{:S(2)}) copy-start(s32[8192]{0:T(1024)} %get-tuple-element.66) | copy-start | bytes 98308 | tf_op jit(solution)/shard_map/cond
  35.7 36.0 %copy-start.4 = (bf16[128,8,512]{2,1,0:T(8,128)(2,1)S(1)}, bf16[128,8,512]{2,1,0:T(8,128)(2,1)}, u32[]{:S(2)}) copy-start(bf16[128,8,512]{2,1,0:T(8,128)(2,1)} %get-tuple-element.202) | copy-start | bytes 3145732 | tf_op jit(solution)/shard_map/cond
  35.7 50.7 %all-gather.4.cloned.1.call-start = ((), (), s32[]{:S(2)}) async-start(), calls=%async_computation.9 | async-start | bytes 5570560 | tf_op jit(solution)/shard_map/cond/branch_0_fun/all_gather | solution.py:207
  36.9 36.5 %copy-start.14 = (s32[128]{0:T(128)S(1)}, s32[128]{0:T(128)}, u32[]{:S(2)}) copy-start(s32[128]{0:T(128)} %get-tuple-element.64) | copy-start | bytes 1540 | tf_op jit(solution)/shard_map/cond
  37.0 27.3 %all-to-all-start = ((bf16[8,56,1024]{2,1,0:T(8,128)(2,1)}), bf16[8,56,1024]{2,1,0:T(8,128)(2,1)S(1)}, u32[]{:S(2)}, u32[]{:S(2)}) async-start(bf16[8,56,1024]{2,1,0:T(8,128)(2,1)} %get-tuple-element.74), calls=%async_computation | async-start | bytes 1835008 | tf_op jit(solution)/shard_map/cond/branch_0_fun/all_to_all | solution.py:197
  41.2 16.9 %collective-permute-start = (bf16[56,1024]{1,0:T(8,128)(2,1)}, bf16[56,1024]{1,0:T(8,128)(2,1)S(1)}, u32[]{:S(2)}, u32[]{:S(2)}) collective-permute-start(bf16[56,1024]{1,0:T(8,128)(2,1)} %get-tuple-element.75), channel_id=1, source_target_pairs={{0,8},{8,0},{1,9},{9,1},{2,10},{10,2},{3,11},{11,3},{4,12},{12,4},... | collective-permute-start | bytes 344072 | tf_op jit(solution)/shard_map/cond/branch_0_fun/ppermute | solution.py:212
  64.2 7.5 %copy-start.8 = (bf16[8,56,1024]{2,1,0:T(8,128)(2,1)}, bf16[8,56,1024]{2,1,0:T(8,128)(2,1)S(1)}, u32[]{:S(2)}) copy-start(bf16[8,56,1024]{2,1,0:T(8,128)(2,1)S(1)} %all-to-all-done) | copy-start | bytes 2752516 | tf_op jit(solution)/shard_map/cond
  65.4 28.8 %all-to-all-start.1 = ((bf16[8,56,1024]{2,1,0:T(8,128)(2,1)}), bf16[8,56,1024]{2,1,0:T(8,128)(2,1)}, u32[]{:S(2)}, u32[]{:S(2)}) async-start(bf16[8,56,1024]{2,1,0:T(8,128)(2,1)} %broadcast_in_dim.75), calls=%async_computation.1 | async-start | bytes 1835008 | tf_op jit(solution)/shard_map/cond/branch_0_fun/all_to_all | solution.py:197
  86.6 2.5 %copy-start.3 = (bf16[20480,128]{1,0:T(8,128)(2,1)S(1)}, bf16[20480,128]{1,0:T(8,128)(2,1)}, u32[]{:S(2)}) copy-start(bf16[20480,128]{1,0:T(8,128)(2,1)} %all-gather.4.cloned.1.call-done) | copy-start | bytes 15728644 | tf_op jit(solution)/shard_map/cond
  94.2 24.0 %all-to-all-start.7 = ((bf16[4,128,1024]{2,1,0:T(8,128)(2,1)}), bf16[4,128,1024]{2,1,0:T(8,128)(2,1)S(1)}, u32[]{:S(2)}, u32[]{:S(2)}) async-start(bf16[4,128,1024]{2,1,0:T(8,128)(2,1)} %get-tuple-element.109), calls=%async_computation.7 | async-start | bytes 2097152 | tf_op jit(solution)/shard_map/all_to_all | solution.py:237
  119.1 3.7 %collective-permute-start.3 = (bf16[256,896]{1,0:T(8,128)(2,1)S(1)}, bf16[256,896]{1,0:T(8,128)(2,1)S(1)}, u32[]{:S(2)}, u32[]{:S(2)}) collective-permute-start(bf16[256,896]{1,0:T(8,128)(2,1)S(1)} %convolution_convert_fusion.2), channel_id=1, source_target_pairs={{0,1},{1,0},{2,3},{3,2},{4,5},{5,4},{6,7},{7,6},{8,9},{9,8},{10,11... | collective-permute-start | bytes 1376264 | tf_op jit(solution)/shard_map/ppermute | solution.py:250
Sparse Core Ops, SparseCore 0:
  38.7 47.7 all-gather.3
